TPU v7x, 32 devices: a whole 2x2x4 slice. The times are simulated.
32 devices in a mesh: slab: 8 (over z, x), tile: 4 (over y, core).
Axes of the slice: x: 2, y: 2, z: 4, core: 2. Of those that a mesh axis runs over, the one named last changes fastest.
Arguments:
- encoded: bfloat16 [8, 16, 2048, 128], P('slab', None, 'tile'), may hold values from -6 to 6
- spacing: float32 [8, 16, 2048], P('slab', None, 'tile'), may hold values from 0.002 to 0.05
- counts: int32 [8, 2048], P('slab', 'tile'), may hold values from 1 to 16
- seg_first: int32 [2048], P('tile'), may hold values from 0 to 1
- seg_last: int32 [2048], P('tile'), may hold values from 7 to 8
- direction: int32 [2048], P('tile'), may hold values from 0 to 1
- field_in: bfloat16 [8, 128, 256], P('slab'), may hold values from -0.5 to 0.5
- field_mid: bfloat16 [8, 256, 256], P('slab'), may hold values from -0.375 to 0.375
- field_out: bfloat16 [8, 256, 64], P('slab'), may hold values from -0.375 to 0.375
- color_head: float32 [64, 3], replicated, may hold values from -0.75 to 0.75
- target: float32 [2048, 3], P('tile'), may hold values from 0 to 1
Outputs:
- front_trans: float32 [8, 2048], P('slab', 'tile')
- grad_in: float32 [8, 128, 256], P('slab')
- grad_mid: float32 [8, 256, 256], P('slab')
- grad_out: float32 [8, 256, 64], P('slab')
All inputs are finite; a program needn't handle non-finite values.
Results may differ from a plain program's by a relative error of at most 0.014.
The roundings to bfloat16 on the way count: a program that leaves them out, or rounds other values in their place, can miss the bound.
Values sent between devices are 32-bit elements; how exact they have to be, the bound alone decides.
No kernel may reach another device: no remote copies, remote signals or barrier semaphores. Data moves between devices by JAX's collectives and lax.ppermute only.
A program may use at most 64 MiB of HBM per device.

v0:
```python
import jax
import jax.numpy as jnp
from jax import lax
from jax.sharding import PartitionSpec as P


def field(field_in, field_mid, field_out, inputs):
    hidden_one = jax.nn.relu(jnp.dot(inputs, field_in, preferred_element_type=jnp.float32)).astype(
        jnp.bfloat16
    )
    hidden_two = jax.nn.relu(
        jnp.dot(hidden_one, field_mid, preferred_element_type=jnp.float32)
    ).astype(jnp.bfloat16)
    outputs = jnp.dot(hidden_two, field_out, preferred_element_type=jnp.float32)
    return (hidden_one, hidden_two, outputs)


def composite(outputs, spacing, live_mask, direction):
    optical = jax.nn.softplus(outputs[:, :, 0]) * spacing * live_mask
    running = jnp.cumsum(optical, axis=0)
    column_sum = running[-1]
    before = jnp.where(direction[None, :] > 0, column_sum[None, :] - running, running - optical)
    weights = jnp.exp(-before) * (1.0 - jnp.exp(-optical))
    colors = jnp.sum(weights[:, :, None] * outputs, axis=0)
    return (jnp.exp(-column_sum), colors)


def make_combine(front_first):

    def combine(earlier, later):
        trans_early, color_early = earlier
        trans_late, color_late = later
        joined = jnp.where(
            front_first[:, None],
            color_early + trans_early[:, None] * color_late,
            color_late + trans_late[:, None] * color_early,
        )
        return (trans_early * trans_late, joined)

    return combine


def field_grads(field_mid, field_out, inputs, hidden_one, hidden_two, grad_outputs):
    grad_low = grad_outputs.astype(jnp.bfloat16)
    grad_three = jnp.dot(hidden_two.T, grad_low, preferred_element_type=jnp.float32)
    back_two = (
        jnp.dot(grad_low, field_out.T, preferred_element_type=jnp.float32) * (hidden_two > 0)
    ).astype(jnp.bfloat16)
    grad_two = jnp.dot(hidden_one.T, back_two, preferred_element_type=jnp.float32)
    back_one = (
        jnp.dot(back_two, field_mid.T, preferred_element_type=jnp.float32) * (hidden_one > 0)
    ).astype(jnp.bfloat16)
    grad_one = jnp.dot(inputs.T, back_one, preferred_element_type=jnp.float32)
    return (grad_one, grad_two, grad_three)


def pixel_grad(color_total, color_head, target, ray_count):
    logits = jnp.dot(color_total, color_head, precision=lax.Precision.HIGHEST)
    shade = jax.nn.sigmoid(logits)
    error = (shade - target) / ray_count
    return jnp.dot(error * shade * (1.0 - shade), color_head.T, precision=lax.Precision.HIGHEST)


def body(
    encoded,
    spacing,
    counts,
    seg_first,
    seg_last,
    direction,
    field_in,
    field_mid,
    field_out,
    color_head,
    target,
):
    samples = encoded.shape[1]
    ray_count = encoded.shape[2]
    width_in = encoded.shape[3]
    width_out = field_out.shape[2]
    my_slab = lax.axis_index("slab")
    reverse_rays = direction > 0
    active = (seg_first <= my_slab) & (my_slab < seg_last)
    sample_ids = jnp.arange(samples, dtype=jnp.int32)
    live_mask = ((sample_ids[:, None] < counts[0][None, :]) & active[None, :]).astype(jnp.float32)
    inputs = encoded[0].reshape(-1, width_in)
    hidden_one, hidden_two, outputs = field(field_in[0], field_mid[0], field_out[0], inputs)
    outputs_three = outputs.reshape(samples, ray_count, width_out)
    own_trans, own_color = composite(outputs_three, spacing[0], live_mask, direction)
    combine_low = make_combine(jnp.logical_not(reverse_rays))
    identity = (jnp.ones((ray_count,), jnp.float32), jnp.zeros((ray_count, width_out), jnp.float32))
    every_trans, every_color = (
        lax.all_gather(own_trans[None], "slab", axis=0, tiled=True),
        lax.all_gather(own_color[None], "slab", axis=0, tiled=True),
    )
    slab_ids = jnp.arange(every_trans.shape[0], dtype=jnp.int32)

    def step_low(running_pair, item):
        item_trans, item_color, item_slab = item
        keep = item_slab < my_slab
        masked = (jnp.where(keep, item_trans, 1.0), jnp.where(keep, item_color, 0.0))
        return (combine_low(running_pair, masked), None)

    def step_high(running_pair, item):
        item_trans, item_color, item_slab = item
        keep = item_slab > my_slab
        masked = (jnp.where(keep, item_trans, 1.0), jnp.where(keep, item_color, 0.0))
        return (make_combine(reverse_rays)(running_pair, masked), None)

    low_pair, _ = lax.scan(step_low, identity, (every_trans, every_color, slab_ids))
    high_pair, _ = lax.scan(step_high, identity, (every_trans, every_color, slab_ids), reverse=True)
    front_trans = jnp.where(reverse_rays, high_pair[0], low_pair[0])
    front_color = jnp.where(reverse_rays[:, None], high_pair[1], low_pair[1])
    back_color = jnp.where(reverse_rays[:, None], low_pair[1], high_pair[1])
    color_total = (
        front_color
        + front_trans[:, None] * own_color
        + (front_trans * own_trans)[:, None] * back_color
    )
    grad_color = pixel_grad(color_total, color_head, target, ray_count)
    grad_seg_color = front_trans[:, None] * grad_color
    grad_seg_trans = front_trans * jnp.sum(grad_color * back_color, axis=1)
    space_here = spacing[0]
    _, pull_back = jax.vjp(
        lambda values: composite(values, space_here, live_mask, direction), outputs_three
    )
    grad_outputs = pull_back((grad_seg_trans, grad_seg_color))[0].reshape(-1, width_out)
    grad_one, grad_two, grad_three = field_grads(
        field_mid[0], field_out[0], inputs, hidden_one, hidden_two, grad_outputs
    )
    grad_one, grad_two, grad_three = lax.psum((grad_one, grad_two, grad_three), "tile")
    return (front_trans[None], grad_one[None], grad_two[None], grad_three[None])


def solution(mesh):
    return jax.shard_map(
        body,
        mesh=mesh,
        in_specs=(
            P("slab", None, "tile", None),
            P("slab", None, "tile"),
            P("slab", "tile"),
            P("tile"),
            P("tile"),
            P("tile"),
            P("slab", None, None),
            P("slab", None, None),
            P("slab", None, None),
            P(),
            P("tile", None),
        ),
        out_specs=(
            P("slab", "tile"),
            P("slab", None, None),
            P("slab", None, None),
            P("slab", None, None),
        ),
        check_vma=False,
    )
```

profile of v0, /device:TPU:0, one launch (start us, length us, event | category | flops | bytes accessed | tf_op | source)
XLA Modules:
  0.0 170.8 jit_solution(10603551223175499338)
XLA Ops:
  7.2 1.5 copy-done
  8.8 2.1 %fusion.4 = bf16[8192,256]{1,0:T(8,128)(2,1)S(1)} fusion(bf16[8192,128]{1,0:T(8,128)(2,1)S(1)} %bitcast.107, bf16[1,128,256]{2,1,0:T(8,128)(2,1)} %param.21), kind=kOutput, calls=%fused_computation.16 | convolution fusion | flops 541065216 | bytes 6356992 | tf_op jit(solution)/shard_map/dot_general | solution.py:8
  10.9 1.3 fusion.7
  12.2 0.7 copy-done.1
  12.9 1.9 %copy-done.3 = bf16[8192,256]{1,0:T(8,128)(2,1)} copy-done((bf16[8192,256]{1,0:T(8,128)(2,1)}, bf16[8192,256]{1,0:T(8,128)(2,1)S(1)}, u32[]{:S(2)}) %copy-start.3) | copy-done | bytes 4194328
  14.8 1.4 fusion.40
  16.2 1.4 copy-done.5
  17.8 1.2 subtract_multiply_fusion
  19.0 2.5 %multiply_reduce_fusion.1 = f32[512,64]{0,1:T(8,128)} fusion(f32[16,512,64]{1,2,0:T(8,128)} %copy-done.5, f32[16,512]{1,0:T(8,128)S(1)} %bitcast.117), kind=kLoop, calls=%fused_computation.22 | loop fusion | flops 1015808 | bytes 2260992 | tf_op jit(solution)/shard_map/reduce_sum | solution.py:24
  21.6 0.0 all-reduce.5.cloned.1.call-start
  21.7 28.1 %all-gather.1 = f32[8,1,512]{2,1,0:T(1,128)S(1)} all-gather(f32[1,1,512]{2,1,0:T(1,128)S(1)} %get-tuple-element.373), channel_id=1, replica_groups=mesh['slab'=8,'tile'=4] {'slab'}, dimensions={0}, use_global_device_ids=true | all-gather | bytes 18432 | tf_op jit(solution)/shard_map/all_gather | solution.py:93
  49.7 14.8 %all-gather.4.cloned.1.call-done = f32[4096,64]{0,1:T(8,128)} async-done(((f32[512,64]{0,1:T(8,128)}), f32[4096,64]{0,1:T(8,128)}) %all-gather.4.cloned.1.call-update) | async-done | bytes 1048592 | tf_op jit(solution)/shard_map/all_gather | solution.py:94
  64.5 3.2 %copy.41 = f32[4096,64]{1,0:T(8,128)} copy(f32[4096,64]{0,1:T(8,128)} %all-gather.4.cloned.1.call-done) | data formatting | bytes 2097152
  67.7 20.4 %while.31 = (s32[]{:T(128)}, f32[512]{0:T(512)S(1)}, f32[512,64]{1,0:T(8,128)S(1)}, s32[8]{0:T(128)S(1)}, s32[]{:T(128)}, /*index=5*/f32[8,512]{1,0:T(8,128)S(1)...) while((s32[]{:T(128)}, f32[512]{0:T(512)S(1)}, ...), condition=%wide.region_5.6_spmd.clone, body=%wide.region_4.5_spmd.clone.sunk | while | flops 230916 | bytes 410255 | solution.py:110
  67.7 0.6 dynamic_slice.60
  69.0 1.3 fusion.80
  70.3 0.6 dynamic_slice.60
  71.5 1.3 fusion.80
  72.8 0.6 dynamic_slice.60
  74.1 1.3 fusion.80
  75.4 0.6 dynamic_slice.60
  76.6 1.3 fusion.80
  77.9 0.6 dynamic_slice.60
  79.2 1.3 fusion.80
  80.5 0.6 dynamic_slice.60
  81.7 1.3 fusion.80
  83.0 0.6 dynamic_slice.60
  84.3 1.3 fusion.80
  85.6 0.6 dynamic_slice.60
  86.8 1.3 fusion.80
  88.1 0.1 copy.35
  88.2 20.5 %while.30 = (s32[]{:T(128)}, f32[512]{0:T(512)S(1)}, f32[512,64]{1,0:T(8,128)S(1)}, s32[8]{0:T(128)S(1)}, s32[]{:T(128)}, /*index=5*/f32[8,512]{1,0:T(8,128)S(1)...) while((s32[]{:T(128)}, f32[512]{0:T(512)S(1)}, ...), condition=%wide.region_3.4_spmd.clone, body=%wide.region_2.3_spmd.clone.sunk | while | flops 230917 | bytes 410275 | solution.py:111
  88.3 0.6 dynamic_slice.57
  89.5 1.3 fusion.78
  90.8 0.6 dynamic_slice.57
  92.1 1.3 fusion.78
  93.4 0.6 dynamic_slice.57
  94.7 1.3 fusion.78
  95.9 0.6 dynamic_slice.57
  97.2 1.3 fusion.78
  98.5 0.6 dynamic_slice.57
  99.8 1.3 fusion.78
  101.1 0.6 dynamic_slice.57
  102.3 1.3 fusion.78
  103.6 0.6 dynamic_slice.57
  104.9 1.3 fusion.78
  106.2 0.6 dynamic_slice.57
  107.5 1.3 fusion.78
  108.7 0.1 copy.34
  108.9 0.2 fusion.13
  109.2 0.3 multiply_reduce_fusion.2
  109.5 2.2 %multiply_reduce_fusion = f32[16,512]{1,0:T(8,128)S(1)} fusion(f32[16,512,64]{1,2,0:T(8,128)} %copy-done.5, f32[512,64]{0,1:T(8,128)S(1)} %get-tuple-element.372), kind=kLoop, calls=%fused_computation.21 | loop fusion | flops 1040384 | bytes 2260992 | tf_op jit(solution)/shard_map/transpose(jvp())/reduce_sum | solution.py:24
  111.8 1.5 fusion.15
  113.3 0.2 fusion.16
  113.6 0.1 copy.45
  113.7 1.4 convolution_bitcast_fusion.1
  115.1 1.3 fusion.6
  116.4 2.0 %copy-done.6 = bf16[8192,256]{1,0:T(8,128)(2,1)} copy-done((bf16[8192,256]{1,0:T(8,128)(2,1)}, bf16[8192,256]{1,0:T(8,128)(2,1)S(1)}, u32[]{:S(2)}) %copy-start.6) | copy-done | bytes 4194328
  118.4 2.0 %convolution_bitcast_fusion = f32[1,256,256]{2,1,0:T(8,128)} fusion(bf16[8192,256]{1,0:T(8,128)(2,1)S(1)} %copy-done.2, bf16[8192,256]{1,0:T(8,128)(2,1)S(1)} %fusion.6), kind=kOutput, calls=%fused_computation.24 | convolution fusion | flops 1073741824 | bytes 8650752 | tf_op jit(solution)/shard_map/dot_general | solution.py:49
  120.3 6.7 %fusion.9 = f32[1,128,256]{1,2,0:T(8,128)} fusion(bf16[8192,128]{1,0:T(8,128)(2,1)S(1)} %bitcast.108, bf16[8192,256]{1,0:T(8,128)(2,1)} %copy-done.6, bf16[8192,256]{1,0:T(8,128)(2,1)} %copy-done.1, bf16[1,256,256]{2,1,0:T(8,128)(2,1)S(1)} %copy-done.9), kind=kOutput, calls=%fused_computation.25 | convolution fusion | flops 1616904192 | bytes 10747904 | tf_op jit(solution)/shard_map/dot_general | solution.py:53
  127.1 32.1 %all-reduce.5.cloned.1.call-done = (f32[1,128,256]{1,2,0:T(8,128)}, f32[1,256,256]{2,1,0:T(8,128)}, f32[1,256,64]{1,2,0:T(8,128)}) async-done(((f32[1,128,256]{1,2,0:T(8,128)}, f32[1,256,256]{2,1,0:T(8,128)}, f32[1,256,64]{1,2,0:T(8,128)}), (f32[1,128,256]{1,2,0:T(8,128)}, f32[1,256,256]{2,1,0:T(8,128)}, f32[1,256,64]{1,2,0:T(8,128)})) %all-reduce.5.cloned.1.call-update) | async-done | bytes 458768 | tf_op jit(solution)/shard_map/psum | solution.py:131
  159.2 1.7 copy.40
  160.9 1.7 copy.74
  162.5 1.5 copy.75
  (86 shorter events, 0.8 us)
Async XLA Ops:
  7.2 1.6 copy-start
  7.2 57.4 %all-gather.4.cloned.1.call-start = ((), (), s32[]{:S(2)}) async-start(), calls=%async_computation | async-start | bytes 1179648 | tf_op jit(solution)/shard_map/all_gather | solution.py:94
  8.8 2.1 %copy-start.9 = (bf16[1,256,256]{2,1,0:T(8,128)(2,1)S(1)}, bf16[1,256,256]{2,1,0:T(8,128)(2,1)}, u32[]{:S(2)}) copy-start(bf16[1,256,256]{2,1,0:T(8,128)(2,1)} %param.22) | copy-start | bytes 393220
  10.9 1.9 %copy-start.1 = (bf16[8192,256]{1,0:T(8,128)(2,1)}, bf16[8192,256]{1,0:T(8,128)(2,1)S(1)}, u32[]{:S(2)}) copy-start(bf16[8192,256]{1,0:T(8,128)(2,1)S(1)} %fusion.4) | copy-start | bytes 12582916
  10.9 3.9 %copy-start.10 = (bf16[1,256,64]{1,2,0:T(8,128)(2,1)S(1)}, bf16[1,256,64]{1,2,0:T(8,128)(2,1)}, u32[]{:S(2)}) copy-start(bf16[1,256,64]{1,2,0:T(8,128)(2,1)} %param.23) | copy-start | bytes 98308
  12.8 2.0 %copy-start.3 = (bf16[8192,256]{1,0:T(8,128)(2,1)}, bf16[8192,256]{1,0:T(8,128)(2,1)S(1)}, u32[]{:S(2)}) copy-start(bf16[8192,256]{1,0:T(8,128)(2,1)S(1)} %fusion.7) | copy-start | bytes 12582916
  12.8 4.8 %copy-start.16 = (s32[512]{0:T(512)S(1)}, s32[512]{0:T(512)}, u32[]{:S(2)}) copy-start(s32[512]{0:T(512)} %param.19) | copy-start | bytes 6148
  12.8 4.8 %copy-start.17 = (s32[512]{0:T(512)S(1)}, s32[512]{0:T(512)}, u32[]{:S(2)}) copy-start(s32[512]{0:T(512)} %param.18) | copy-start | bytes 6148
  12.8 4.8 %copy-start.8 = (f32[1,16,512]{2,1,0:T(8,128)S(1)}, f32[1,16,512]{2,1,0:T(8,128)}, u32[]{:S(2)}) copy-start(f32[1,16,512]{2,1,0:T(8,128)} %param.16) | copy-start | bytes 98308
  12.8 4.8 %copy-start.12 = (s32[1,512]{1,0:T(1,128)S(1)}, s32[1,512]{1,0:T(1,128)}, u32[]{:S(2)}) copy-start(s32[1,512]{1,0:T(1,128)} %param.17) | copy-start | bytes 6148
  12.9 4.9 %copy-start.15 = (s32[512]{0:T(512)S(1)}, s32[512]{0:T(512)}, u32[]{:S(2)}) copy-start(s32[512]{0:T(512)} %param.20) | copy-start | bytes 6148
  16.2 1.4 copy-start.5
  21.6 137.6 %all-reduce.5.cloned.1.call-start = ((), (), s32[]{:S(2)}) async-start(), calls=%async_computation.1 | async-start | bytes 917504 | tf_op jit(solution)/shard_map/psum | solution.py:131
  67.7 41.2 %copy-start.7 = (f32[512,64]{0,1:T(8,128)S(1)}, f32[512,64]{0,1:T(8,128)}, u32[]{:S(2)}) copy-start(f32[512,64]{0,1:T(8,128)} %multiply_reduce_fusion.1) | copy-start | bytes 393220
  67.7 41.2 %copy-start.13 = (f32[64,3]{0,1:T(4,128)S(1)}, f32[64,3]{0,1:T(4,128)}, u32[]{:S(2)}) copy-start(f32[64,3]{0,1:T(4,128)} %param.24) | copy-start | bytes 2308
  67.7 41.4 %copy-start.14 = (f32[512,3]{0,1:T(4,128)S(1)}, f32[512,3]{0,1:T(4,128)}, u32[]{:S(2)}) copy-start(f32[512,3]{0,1:T(4,128)} %param.25) | copy-start | bytes 18436
  108.9 4.8 %copy-start.4 = (bf16[8192,256]{1,0:T(8,128)(2,1)S(1)}, bf16[8192,256]{1,0:T(8,128)(2,1)}, u32[]{:S(2)}) copy-start(bf16[8192,256]{1,0:T(8,128)(2,1)} %copy-done.3) | copy-start | bytes 12582916
  108.9 6.2 %copy-start.11 = (f32[512]{0:T(512)}, f32[512]{0:T(512)S(1)}, u32[]{:S(2)}) copy-start(f32[512]{0:T(512)S(1)} %get-tuple-element.368) | copy-start | bytes 6148
  115.1 3.3 %copy-start.2 = (bf16[8192,256]{1,0:T(8,128)(2,1)S(1)}, bf16[8192,256]{1,0:T(8,128)(2,1)}, u32[]{:S(2)}) copy-start(bf16[8192,256]{1,0:T(8,128)(2,1)} %copy-done.1) | copy-start | bytes 12582916
  116.4 2.0 %copy-start.6 = (bf16[8192,256]{1,0:T(8,128)(2,1)}, bf16[8192,256]{1,0:T(8,128)(2,1)S(1)}, u32[]{:S(2)}) copy-start(bf16[8192,256]{1,0:T(8,128)(2,1)S(1)} %fusion.6) | copy-start | bytes 12582916
Sparse Core Ops, SparseCore 0:
  21.7 42.8 all-gather.3
  127.2 31.9 all-reduce.4
where the time goes:
time: 172 us; the launch traced here: 171 us
  waiting for transfers between devices  46.9 us (27%)
  other arithmetic  28.4 us (17%)
  blocking collectives  28.1 us (16%)
  local copies, waits for them, and re-layouts  25.5 us (15%)
  matrix products  16.7 us (10%)
  between operations  14.4 us (8%)
  loops' own time  10.7 us (6%)
    psum x1, waiting for transfers between devices, body(): lax.psum((grad_one, grad_two, grad_three), 'tile')  32.1 us
    all_gather x1, blocking collectives, body(): lax.all_gather(own_trans[None], 'slab', axis=0, tiled=True)  28.1 us
    select_n x16, other arithmetic, combine(): jnp.where(front_first[:, None], color_early + trans_early[:, None] * colo...  20.2 us
    unnamed x42, local copies, waits for them, and re-layouts  15.5 us
    all_gather x1, waiting for transfers between devices, body(): lax.all_gather(own_color[None], 'slab', axis=0, tiled=True)  14.8 us
    dynamic_slice x16, local copies, waits for them, and re-layouts, body(): lax.scan(step_low, identity, (every_trans, every_color, slab_ids))  9.6 us
    dot_general x1, matrix products, field_grads(): grad_one = jnp.dot(inputs.T, back_one, preferred_element_type=jnp.float32)  6.71 us
    another operation x1, loops' own time, body(): lax.scan(step_high, identity, (every_trans, every_color, slab_ids), rever...  5.54 us
  transfers between devices with their start and end apart: 2, of which 2 were waited for; matrix products, arithmetic and copies ran while one was open for 0% of the time, Pallas kernels for 0%

commit v1 on v0

v1 whole, which is shorter than its diff:
```python
import functools

import jax
import jax.numpy as jnp
from jax import lax
from jax.experimental import pallas as pl
from jax.experimental.pallas import tpu as pltpu
from jax.sharding import PartitionSpec as P

F32 = jnp.float32
BF16 = jnp.bfloat16
VMEM = pl.BlockSpec(memory_space=pltpu.VMEM)
SMEM = pl.BlockSpec(memory_space=pltpu.SMEM)
ANY = pl.BlockSpec(memory_space=pl.ANY)
LIMIT = pltpu.CompilerParams(vmem_limit_bytes=48 * 1024 * 1024)


def dot_nn(a, b):
    return lax.dot_general(a, b, (((1,), (0,)), ((), ())), preferred_element_type=F32)


def dot_nt(a, b):
    return lax.dot_general(a, b, (((1,), (1,)), ((), ())), preferred_element_type=F32)


def dot_tn(a, b):
    return lax.dot_general(a, b, (((0,), (0,)), ((), ())), preferred_element_type=F32)


def running_sum(values):
    rows = values.shape[0]
    ids = lax.broadcasted_iota(jnp.int32, values.shape, 0)
    shift = 1
    while shift < rows:
        moved = pltpu.roll(values, shift, 0)
        values = values + jnp.where(ids >= shift, moved, 0.0)
        shift *= 2
    return values


def split_three(values):
    high = values.astype(BF16)
    rest = values - high.astype(F32)
    mid = rest.astype(BF16)
    low = (rest - mid.astype(F32)).astype(BF16)
    return high, mid, low


def projection(head, field_out):
    first = jnp.where(lax.broadcasted_iota(jnp.int32, (1, head.shape[0]), 1) == 0, 1.0, 0.0).astype(BF16)
    density = dot_nt(first, field_out)
    high, mid, low = split_three(head.T)
    proj = dot_nt(high, field_out) + (dot_nt(mid, field_out) + dot_nt(low, field_out))
    proj_high = proj.astype(BF16).astype(F32)
    rest = proj - proj_high
    return jnp.concatenate([density, proj_high, rest, jnp.zeros_like(density)], axis=0)


def forward_kernel(
    slab_ref, x_ref, spacing_ref, counts_ref, first_ref, last_ref, direction_ref,
    w1_ref, w2_ref, w3_ref, head_ref,
    seg_ref, h1_ref, h2_ref, save_ref, w8_ref, out8,
):
    samples, rays, _ = x_ref.shape
    w8 = projection(head_ref[...], w3_ref[...])
    w8_ref[...] = w8
    w16 = jnp.concatenate([w8, jnp.zeros_like(w8)], axis=0).astype(BF16)
    w1 = w1_ref[...]
    w2 = w2_ref[...]

    def step(j, carry):
        x = x_ref[j]
        h1 = jnp.maximum(dot_nn(x, w1), 0.0).astype(BF16)
        h1_ref[j] = h1
        h2 = jnp.maximum(dot_nn(h1, w2), 0.0).astype(BF16)
        h2_ref[j] = h2
        out8[j] = dot_nt(w16, h2)[:8]
        return carry

    lax.fori_loop(0, samples, step, 0, unroll=2)

    slab = slab_ref[0]
    density = out8[:, 0, :]
    proj = [out8[:, 1 + k, :] + out8[:, 4 + k, :] for k in range(3)]
    ids = lax.broadcasted_iota(jnp.int32, density.shape, 0)
    active = (first_ref[...] <= slab) & (slab < last_ref[...])
    live = jnp.where((ids < counts_ref[...]) & active, 1.0, 0.0)
    span = spacing_ref[...] * live
    optical = (jnp.maximum(density, 0.0) + jnp.log1p(jnp.exp(-jnp.abs(density)))) * span
    running = running_sum(optical)
    column = running[samples - 1 : samples]
    before = jnp.where(direction_ref[...] > 0, column - running, running - optical)
    reach = jnp.exp(-before)
    passed = jnp.exp(-optical)
    weights = reach * (1.0 - passed)
    seg_ref[...] = jnp.concatenate(
        [jnp.exp(-column)] + [jnp.sum(weights * p, axis=0, keepdims=True) for p in proj], axis=0
    )
    save_ref[0] = weights
    save_ref[1] = reach * passed
    save_ref[2] = span * jax.nn.sigmoid(density)
    for k in range(3):
        save_ref[3 + k] = proj[k]


def backward_kernel(
    ids_ref, x_ref, h1_ref, h2_ref, save_ref, w8_ref, w2_ref, head_ref, target_ref, direction_ref, *refs,
    n_pieces, n_slab,
):
    pieces = refs[:n_pieces]
    front_ref, keep_ref, send_ref, every, q8, acc = refs[n_pieces:]
    samples, rays, _ = x_ref.shape
    slab = ids_ref[0]
    core = ids_ref[1]
    at = 0
    for piece in pieces:
        if len(piece.shape) == 2:
            every[at] = piece[...]
            at += 1
        else:
            for i in range(piece.shape[0]):
                every[at + i] = piece[i]
            at += piece.shape[0]
    forward_ray = direction_ref[...] <= 0

    one = jnp.ones((1, rays), F32)
    zero = jnp.zeros((3, rays), F32)

    def compose(ascending):
        trans, color = one, zero
        order = range(n_slab) if ascending else range(n_slab - 1, -1, -1)
        early = forward_ray if ascending else jnp.logical_not(forward_ray)
        for s in order:
            item = every[jnp.bitwise_xor(slab, s)]
            keep = (s < slab) if ascending else (s > slab)
            item_trans = jnp.where(keep, item[0:1], 1.0)
            item_color = jnp.where(keep, item[1:4], 0.0)
            color = jnp.where(early, color + trans * item_color, item_color + item_trans * color)
            trans = trans * item_trans
        return trans, color

    low_trans, low_color = compose(True)
    high_trans, high_color = compose(False)
    front_trans = jnp.where(forward_ray, low_trans, high_trans)
    front_color = jnp.where(forward_ray, low_color, high_color)
    back_color = jnp.where(forward_ray, high_color, low_color)
    front_ref[...] = front_trans
    own = every[0]
    own_trans = own[0:1]
    logits = front_color + front_trans * own[1:4] + (front_trans * own_trans) * back_color
    shade = jax.nn.sigmoid(logits)
    error = (shade - target_ref[...].T) / rays
    grad_logit = error * shade * (1.0 - shade)
    grad_trans = front_trans * jnp.sum(grad_logit * back_color, axis=0, keepdims=True)
    pull = front_trans * grad_logit

    weights = save_ref[0]
    grad_weight = pull[0:1] * save_ref[3] + pull[1:2] * save_ref[4] + pull[2:3] * save_ref[5]
    product = weights * grad_weight
    running = running_sum(product)
    total = running[samples - 1 : samples]
    after = jnp.where(forward_ray, total - running, running - product)
    grad_optical = grad_weight * save_ref[1] - after - grad_trans * own_trans
    q8[:, 0, :] = grad_optical * save_ref[2]
    for k in range(3):
        q = weights * pull[k : k + 1]
        q8[:, 1 + k, :] = q
        q8[:, 4 + k, :] = q
    q8[:, 7, :] = jnp.zeros_like(weights)

    w8 = w8_ref[...]
    w16 = jnp.concatenate([w8, w8], axis=0).astype(BF16)
    w2 = w2_ref[...]
    acc[...] = jnp.zeros_like(acc)
    half_mid = w2.shape[0] // 2
    half_in = x_ref.shape[2] // 2
    rows_in = half_mid + half_in

    def step(j, carry):
        rows = q8[j]
        high = rows.astype(BF16).astype(F32)
        q16 = jnp.concatenate([high, rows - high], axis=0).astype(BF16)
        h1 = h1_ref[j]
        h2 = h2_ref[j]
        x = x_ref[j]
        grad_out = dot_nn(q16, h2)
        back_two = jnp.where(h2 > 0, dot_tn(q16, w16), 0.0).astype(BF16)
        grad_mid = dot_tn(h1, back_two)
        back_one = jnp.where(h1 > 0, dot_nt(back_two, w2), 0.0).astype(BF16)
        grad_in = dot_tn(x, back_one)
        for h in range(2):
            acc[h, :half_mid] += grad_mid[h * half_mid : (h + 1) * half_mid]
            acc[h, half_mid:rows_in] += grad_in[h * half_in : (h + 1) * half_in]
        acc[0, rows_in:] += grad_out[:8] + grad_out[8:]
        return carry

    lax.fori_loop(0, samples, step, 0, unroll=2)
    keep_ref[...] = acc[core]
    send_ref[...] = acc[1 - core]


def final_kernel(core_ref, own_ref, other_ref, head_ref, in_ref, mid_ref, out_ref):
    core = core_ref[0]
    half_mid = mid_ref.shape[0] // 2
    half_in = in_ref.shape[0] // 2
    rows_in = half_mid + half_in
    for h in range(2):

        def place(source):
            mid_ref[h * half_mid : (h + 1) * half_mid] = source[:half_mid]
            in_ref[h * half_in : (h + 1) * half_in] = source[half_mid:rows_in]
            if h == 0:
                factors = source[rows_in:]
                head = head_ref[...].T
                first = jnp.where(lax.broadcasted_iota(jnp.int32, (1, head.shape[1]), 1) == 0, 1.0, 0.0)
                rows = jnp.concatenate([first, head, jnp.zeros((4, head.shape[1]), F32)], axis=0)
                out_ref[...] = lax.dot_general(
                    factors, rows, (((0,), (0,)), ((), ())),
                    preferred_element_type=F32, precision=lax.Precision.HIGHEST,
                )

        pl.when(core == h)(functools.partial(place, own_ref))
        pl.when(core != h)(functools.partial(place, other_ref))


def pairs(size, bit):
    return [(i, i ^ bit) for i in range(size)]


def make_body(n_slab, n_tile):

    def body(
        encoded, spacing, counts, seg_first, seg_last, direction,
        field_in, field_mid, field_out, color_head, target,
    ):
        _, samples, rays, width = encoded.shape
        hidden = field_mid.shape[1]
        slab = lax.axis_index("slab")
        tile = lax.axis_index("tile")
        core = tile % 2
        x = encoded[0]
        row = lambda a: a.reshape(1, rays)
        w1, w2, w3 = field_in[0], field_mid[0], field_out[0]
        ids = jnp.stack([slab, core]).astype(jnp.int32)
        seg, h1, h2, save, w8 = pl.pallas_call(
            forward_kernel,
            name="forward",
            out_shape=(
                jax.ShapeDtypeStruct((4, rays), F32),
                jax.ShapeDtypeStruct((samples, rays, hidden), BF16),
                jax.ShapeDtypeStruct((samples, rays, hidden), BF16),
                jax.ShapeDtypeStruct((6, samples, rays), F32),
                jax.ShapeDtypeStruct((8, hidden), F32),
            ),
            in_specs=[SMEM] + [VMEM] * 10,
            out_specs=(VMEM,) * 5,
            scratch_shapes=[pltpu.VMEM((samples, 8, rays), F32)],
            compiler_params=LIMIT,
        )(ids, x, spacing[0], counts, row(seg_first), row(seg_last), row(direction), w1, w2, w3, color_head)

        pieces = [seg]
        known = seg[None]
        bit = 1
        while bit < n_slab:
            got = lax.ppermute(known, "slab", pairs(n_slab, bit))
            pieces.append(got)
            bit *= 2
            if bit < n_slab:
                known = jnp.concatenate([known, got], axis=0)

        half = (hidden + width) // 2 + 8
        front, keep, send = pl.pallas_call(
            functools.partial(backward_kernel, n_pieces=len(pieces), n_slab=n_slab),
            name="backward",
            out_shape=(
                jax.ShapeDtypeStruct((1, rays), F32),
                jax.ShapeDtypeStruct((half, hidden), F32),
                jax.ShapeDtypeStruct((half, hidden), F32),
            ),
            in_specs=[SMEM] + [VMEM] * (9 + len(pieces)),
            out_specs=(VMEM,) * 3,
            scratch_shapes=[
                pltpu.VMEM((n_slab, 4, rays), F32),
                pltpu.VMEM((samples, 8, rays), F32),
                pltpu.VMEM((2, half, hidden), F32),
            ],
            compiler_params=LIMIT,
        )(ids, x, h1, h2, save, w8, w2, color_head, target, row(direction), *pieces)

        part = keep + lax.ppermute(send, "tile", pairs(n_tile, 1))
        bit = 2
        while bit < n_tile:
            part = part + lax.ppermute(part, "tile", pairs(n_tile, bit))
            bit *= 2
        other = lax.ppermute(part, "tile", pairs(n_tile, 1))
        grad_in, grad_mid, grad_out = pl.pallas_call(
            final_kernel,
            name="final",
            out_shape=(
                jax.ShapeDtypeStruct(w1.shape, F32),
                jax.ShapeDtypeStruct(w2.shape, F32),
                jax.ShapeDtypeStruct(w3.shape, F32),
            ),
            in_specs=[SMEM] + [VMEM] * 3,
            out_specs=(VMEM,) * 3,
            compiler_params=LIMIT,
        )(core.reshape(1).astype(jnp.int32), part, other, color_head)
        return front, grad_in[None], grad_mid[None], grad_out[None]

    return body


def solution(mesh):
    return jax.shard_map(
        make_body(mesh.shape["slab"], mesh.shape["tile"]),
        mesh=mesh,
        in_specs=(
            P("slab", None, "tile", None),
            P("slab", None, "tile"),
            P("slab", "tile"),
            P("tile"),
            P("tile"),
            P("tile"),
            P("slab", None, None),
            P("slab", None, None),
            P("slab", None, None),
            P(),
            P("tile", None),
        ),
        out_specs=(
            P("slab", "tile"),
            P("slab", None, None),
            P("slab", None, None),
            P("slab", None, None),
        ),
        check_vma=False,
    )
```

time: 172 us -> 59.5 us (0.35)
  waiting for transfers between devices: 46.9 us -> 12.7 us
  other arithmetic: 28.4 us -> 0.16 us
  blocking collectives: 28.1 us -> 0 us
  Pallas kernels: 0 us -> 23.6 us
  matrix products: 16.7 us -> 0 us
  local copies, waits for them, and re-layouts: 25.5 us -> 11.6 us
  between operations: 14.4 us -> 0.71 us
  loops' own time: 10.7 us -> 0 us
  starting transfers between devices: 0.08 us -> 10.2 us
    psum x1 -> x0, waiting for transfers between devices: 32.1 us -> none  [body(): lax.psum((grad_one, grad_two, grad_three), 'tile')]
    all_gather x1 -> x0, blocking collectives: 28.1 us -> none  [body(): lax.all_gather(own_trans[None], 'slab', axis=0, tiled=True)]
    pallas_call x0 -> x3, Pallas kernels: none -> 23.6 us  [the longest x1 12 us: body(): pl.pallas_call(functools.partial(backward_kernel, n_pieces=len(pieces), n...]
    select_n x32 -> x0, other arithmetic: 20.3 us -> none  [the longest x16 20.2 us: combine(): jnp.where(front_first[:, None], color_early + trans_early[:, None] * colo...]
    dot_general x9 -> x0, matrix products: 16.7 us -> none  [the longest x1 6.71 us: field_grads(): grad_one = jnp.dot(inputs.T, back_one, preferred_element_type=jnp.float32)]
    all_gather x1 -> x0, waiting for transfers between devices: 14.8 us -> none  [body(): lax.all_gather(own_color[None], 'slab', axis=0, tiled=True)]
    ppermute x0 -> x6, waiting for transfers between devices: none -> 12.7 us  [the longest x1 5.38 us: body(): part = part + lax.ppermute(part, 'tile', pairs(n_tile, bit))]
    another operation x2 -> x0, loops' own time: 10.7 us -> none  [the longest x1 5.54 us: body(): lax.scan(step_high, identity, (every_trans, every_color, slab_ids), rever...]
  transfers between devices with their start and end apart: 2 -> 6, of which waited for: 2 -> 6; matrix products, arithmetic and copies ran while one was open for 0% -> 1% of each run, Pallas kernels for 0% -> 0%
where the time goes in v1:
time: 59.5 us; the launch traced here: 58.9 us
  Pallas kernels  23.6 us (40%)
  waiting for transfers between devices  12.7 us (21%)
  local copies, waits for them, and re-layouts  11.6 us (19%)
  starting transfers between devices  10.2 us (17%)
  between operations  0.71 us (1%)
    pallas_call x1, Pallas kernels, body(): pl.pallas_call(functools.partial(backward_kernel, n_pieces=len(pieces), n...  12 us
    unnamed x26, local copies, waits for them, and re-layouts  11.6 us
    pallas_call x1, Pallas kernels, body(): pl.pallas_call(forward_kernel, name='forward', out_shape=(jax.ShapeDtypeS...  10.5 us
    ppermute x3, starting transfers between devices, body(): got = lax.ppermute(known, 'slab', pairs(n_slab, bit))  8.15 us
    ppermute x1, waiting for transfers between devices, body(): part = part + lax.ppermute(part, 'tile', pairs(n_tile, bit))  5.38 us
    ppermute x3, waiting for transfers between devices, body(): got = lax.ppermute(known, 'slab', pairs(n_slab, bit))  4.4 us
    ppermute x1, starting transfers between devices, body(): part = part + lax.ppermute(part, 'tile', pairs(n_tile, bit))  1.91 us
    ppermute x1, waiting for transfers between devices, body(): part = keep + lax.ppermute(send, 'tile', pairs(n_tile, 1))  1.44 us
  transfers between devices with their start and end apart: 6, of which 6 were waited for; matrix products, arithmetic and copies ran while one was open for 1% of the time, Pallas kernels for 0%

profile of v1, /device:TPU:0, one launch (start us, length us, event | category | flops | bytes accessed | tf_op | source)
XLA Modules:
  0.0 58.9 jit_solution(14888219975160571644)
XLA Ops:
  0.6 0.8 %copy.16.head_ref = f32[64,3]{1,0:T(8,128)S(1)} copy(f32[64,3]{0,1:T(4,128)} %param.20) | data formatting | bytes 1536 | tf_op args[9]
  1.4 0.9 %copy.15 = bf16[1,256,64]{2,1,0:T(8,128)(2,1)S(1)} copy(bf16[1,256,64]{1,2,0:T(8,128)(2,1)} %param.19) | data formatting | bytes 65536 | tf_op args[8]
  2.3 0.1 pad_add_fusion.slab_ref.ids_ref
  2.4 0.0 copy-start
  2.4 1.6 %copy-done = bf16[1,16,512,128]{3,2,1,0:T(8,128)(2,1)S(1)} copy-done((bf16[1,16,512,128]{3,2,1,0:T(8,128)(2,1)S(1)}, bf16[1,16,512,128]{3,2,1,0:T(8,128)(2,1)}, u32[]{:S(2)}) %copy-start) | copy-done | bytes 2097176
  4.0 0.0 copy-start.2
  4.0 0.9 %copy-done.2 = bf16[1,256,256]{2,1,0:T(8,128)(2,1)S(1)} copy-done((bf16[1,256,256]{2,1,0:T(8,128)(2,1)S(1)}, bf16[1,256,256]{2,1,0:T(8,128)(2,1)}, u32[]{:S(2)}) %copy-start.2) | copy-done | bytes 131096
  4.9 0.0 copy-start.4
  4.9 0.8 %copy-done.4 = bf16[1,128,256]{2,1,0:T(8,128)(2,1)S(1)} copy-done((bf16[1,128,256]{2,1,0:T(8,128)(2,1)S(1)}, bf16[1,128,256]{2,1,0:T(8,128)(2,1)}, u32[]{:S(2)}) %copy-start.4) | copy-done | bytes 65560
  5.7 0.0 copy-start.5
  5.7 0.8 %copy-done.5 = f32[1,16,512]{2,1,0:T(8,128)S(1)} copy-done((f32[1,16,512]{2,1,0:T(8,128)S(1)}, f32[1,16,512]{2,1,0:T(8,128)}, u32[]{:S(2)}) %copy-start.5) | copy-done | bytes 32792
  6.5 0.0 copy-start.6
  6.5 0.7 %copy-done.6 = s32[512]{0:T(512)S(1)} copy-done((s32[512]{0:T(512)S(1)}, s32[512]{0:T(512)}, u32[]{:S(2)}) %copy-start.6) | copy-done | bytes 2072
  7.1 0.0 copy-start.8
  7.1 0.7 %copy-done.8 = s32[1,512]{1,0:T(1,128)S(1)} copy-done((s32[1,512]{1,0:T(1,128)S(1)}, s32[1,512]{1,0:T(1,128)}, u32[]{:S(2)}) %copy-start.8) | copy-done | bytes 2072
  7.8 0.0 copy-start.9
  7.8 0.7 %copy-done.9 = s32[512]{0:T(512)S(1)} copy-done((s32[512]{0:T(512)S(1)}, s32[512]{0:T(512)}, u32[]{:S(2)}) %copy-start.9) | copy-done | bytes 2072
  8.5 0.0 copy-start.10
  8.5 0.7 %copy-done.10 = s32[512]{0:T(512)S(1)} copy-done((s32[512]{0:T(512)S(1)}, s32[512]{0:T(512)}, u32[]{:S(2)}) %copy-start.10) | copy-done | bytes 2072
  9.2 0.0 copy-start.1
  9.2 10.5 %forward.1 = (f32[4,512]{1,0:T(4,128)S(1)}, bf16[16,512,256]{2,1,0:T(8,128)(2,1)}, bf16[16,512,256]{2,1,0:T(8,128)(2,1)}, f32[6,16,512]{2,1,0:T(8,128)S(1)}, f32[8,256]{1,0:T(8,128)S(1)}) custom-call(s32[2]{0:T(128)S(1)} %pad_add_fusion.slab_ref.ids_ref, bf16[16,512,128]{2,1,0:T(8,128)(2,1)S(1)} %bitcast.14, f32[16,512]{1,0:T(8,128)S(1)} %bitcast.24, ...), custom_call_target="tpu_custom_call" | custom-call | tf_op jit(solution)/shard_map/forward/pallas_call | solution.py:245
  19.7 2.9 %collective-permute-start = (f32[1,4,512]{2,1,0:T(4,128)S(1)}, f32[1,4,512]{2,1,0:T(4,128)S(1)}, u32[]{:S(2)}, u32[]{:S(2)}) collective-permute-start(f32[1,4,512]{2,1,0:T(4,128)S(1)} %bitcast.20), channel_id=1, source_target_pairs={{0,4},{4,0},{8,12},{12,8},{16,20},{20,16},{24,28},{28,24},{1,5},{5... | collective-permute-start | bytes 24584 | tf_op jit(solution)/shard_map/ppermute | solution.py:265
  22.6 1.6 %collective-permute-done.refs_1_ = f32[1,4,512]{2,1,0:T(4,128)S(1)} collective-permute-done((f32[1,4,512]{2,1,0:T(4,128)S(1)}, f32[1,4,512]{2,1,0:T(4,128)S(1)}, u32[]{:S(2)}, u32[]{:S(2)}) %collective-permute-start) | collective-permute-done | bytes 8224 | tf_op jit(solution)/shard_map/ppermute | solution.py:265
  24.3 2.1 %collective-permute-start.1 = (f32[2,4,512]{2,1,0:T(4,128)S(1)}, f32[2,4,512]{2,1,0:T(4,128)S(1)}, u32[]{:S(2)}, u32[]{:S(2)}) collective-permute-start(f32[2,4,512]{2,1,0:T(4,128)S(1)} %pad_maximum_fusion.1), channel_id=1, source_target_pairs={{0,8},{4,12},{8,0},{12,4},{16,24},{20,28},{24,16},{28,20},{1,9},{5... | collective-permute-start | bytes 49160 | tf_op jit(solution)/shard_map/ppermute | solution.py:265
  26.4 1.7 %collective-permute-done.1.refs_2_ = f32[2,4,512]{2,1,0:T(4,128)S(1)} collective-permute-done((f32[2,4,512]{2,1,0:T(4,128)S(1)}, f32[2,4,512]{2,1,0:T(4,128)S(1)}, u32[]{:S(2)}, u32[]{:S(2)}) %collective-permute-start.1) | collective-permute-done | bytes 16416 | tf_op jit(solution)/shard_map/ppermute | solution.py:265
  28.1 3.1 %collective-permute-start.2 = (f32[4,4,512]{2,1,0:T(4,128)S(1)}, f32[4,4,512]{2,1,0:T(4,128)S(1)}, u32[]{:S(2)}, u32[]{:S(2)}) collective-permute-start(f32[4,4,512]{2,1,0:T(4,128)S(1)} %pad_maximum_fusion), channel_id=1, source_target_pairs={{0,16},{4,20},{8,24},{12,28},{16,0},{20,4},{24,8},{28,12},{1,17},{... | collective-permute-start | bytes 98312 | tf_op jit(solution)/shard_map/ppermute | solution.py:265
  31.2 0.8 %copy.18.target_ref = f32[512,3]{1,0:T(8,128)S(1)} copy(f32[512,3]{0,1:T(4,128)} %param.21) | data formatting | bytes 12288 | tf_op args[10]
  32.0 1.1 %collective-permute-done.2.refs_3_ = f32[4,4,512]{2,1,0:T(4,128)S(1)} collective-permute-done((f32[4,4,512]{2,1,0:T(4,128)S(1)}, f32[4,4,512]{2,1,0:T(4,128)S(1)}, u32[]{:S(2)}, u32[]{:S(2)}) %collective-permute-start.2) | collective-permute-done | bytes 32800 | tf_op jit(solution)/shard_map/ppermute | solution.py:265
  33.1 0.0 copy-done.1
  33.1 0.0 copy-start.3
  33.1 0.9 %copy-done.3 = bf16[1,256,256]{2,1,0:T(8,128)(2,1)S(1)} copy-done((bf16[1,256,256]{2,1,0:T(8,128)(2,1)S(1)}, bf16[1,256,256]{2,1,0:T(8,128)(2,1)}, u32[]{:S(2)}) %copy-start.3) | copy-done | bytes 131096
  34.0 0.0 copy-start.7
  34.0 0.7 %copy-done.7 = s32[512]{0:T(512)S(1)} copy-done((s32[512]{0:T(512)S(1)}, s32[512]{0:T(512)}, u32[]{:S(2)}) %copy-start.7) | copy-done | bytes 2072
  34.7 12.0 %backward.1 = (f32[1,512]{1,0:T(1,128)}, f32[200,256]{1,0:T(8,128)S(1)}, f32[200,256]{1,0:T(8,128)S(1)}) custom-call(s32[2]{0:T(128)S(1)} %pad_add_fusion.slab_ref.ids_ref, bf16[16,512,128]{2,1,0:T(8,128)(2,1)S(1)} %bitcast.15, bf16[16,512,256]{2,1,0:T(8,128)(2,1)} %get-tuple-element.15.h1_ref, bf16[16,512,256]{2,1,0:T(8,128)(2,1)} %get-tuple-element.16.h2_ref, ...), custom_call_target="tpu_custom_call" | custom-call | tf_op jit(solution)/shard_map/backward/pallas_call | solution.py:272
  46.7 0.1 collective-permute-start.3
  46.8 1.4 %collective-permute-done.3 = f32[200,256]{1,0:T(8,128)S(1)} collective-permute-done((f32[200,256]{1,0:T(8,128)S(1)}, f32[200,256]{1,0:T(8,128)S(1)}, u32[]{:S(2)}, u32[]{:S(2)}) %collective-permute-start.3) | collective-permute-done | bytes 204832 | tf_op jit(solution)/shard_map/ppermute | solution.py:290
  48.2 1.9 %collective-permute-start.4 = (f32[200,256]{1,0:T(8,128)S(1)}, f32[200,256]{1,0:T(8,128)S(1)}, u32[]{:S(2)}, u32[]{:S(2)}) collective-permute-start(f32[200,256]{1,0:T(8,128)S(1)} %add.11), channel_id=1, source_target_pairs={{0,2},{1,3},{2,0},{3,1},{4,6},{5,7},{6,4},{7,5},{8,10},{9,11},{10,... | collective-permute-start | bytes 614408 | tf_op jit(solution)/shard_map/ppermute | solution.py:293
  50.2 5.4 %collective-permute-done.4 = f32[200,256]{1,0:T(8,128)S(1)} collective-permute-done((f32[200,256]{1,0:T(8,128)S(1)}, f32[200,256]{1,0:T(8,128)S(1)}, u32[]{:S(2)}, u32[]{:S(2)}) %collective-permute-start.4) | collective-permute-done | bytes 204832 | tf_op jit(solution)/shard_map/ppermute | solution.py:293
  55.6 0.1 collective-permute-start.5
  55.7 1.4 %collective-permute-done.5.other_ref = f32[200,256]{1,0:T(8,128)S(1)} collective-permute-done((f32[200,256]{1,0:T(8,128)S(1)}, f32[200,256]{1,0:T(8,128)S(1)}, u32[]{:S(2)}, u32[]{:S(2)}) %collective-permute-start.5) | collective-permute-done | bytes 204832 | tf_op jit(solution)/shard_map/ppermute | solution.py:295
  57.1 1.1 %final.1 = (f32[128,256]{1,0:T(8,128)}, f32[256,256]{1,0:T(8,128)}, f32[256,64]{1,0:T(8,128)S(1)}) custom-call(s32[1]{0:T(128)} %bitcast.1.core_ref, f32[200,256]{1,0:T(8,128)S(1)} %add.12.own_ref, f32[200,256]{1,0:T(8,128)S(1)} %collective-permute-done.5.other_ref, f32[64,3]{1,0:T(8,128)S(1)} %copy.16.head_ref), custom_call_target="tpu_custom_call" | custom-call | tf_op jit(solution)/shard_map/final/pallas_call | solution.py:296
  58.2 0.7 %copy.20 = f32[1,256,64]{1,2,0:T(8,128)} copy(f32[1,256,64]{2,1,0:T(8,128)S(1)} %bitcast.19) | data formatting | bytes 131072
  (4 shorter events, 0.1 us)
Async XLA Ops:
  2.4 1.6 %copy-start = (bf16[1,16,512,128]{3,2,1,0:T(8,128)(2,1)S(1)}, bf16[1,16,512,128]{3,2,1,0:T(8,128)(2,1)}, u32[]{:S(2)}) copy-start(bf16[1,16,512,128]{3,2,1,0:T(8,128)(2,1)} %param.11) | copy-start | bytes 6291460
  4.0 0.9 %copy-start.2 = (bf16[1,256,256]{2,1,0:T(8,128)(2,1)S(1)}, bf16[1,256,256]{2,1,0:T(8,128)(2,1)}, u32[]{:S(2)}) copy-start(bf16[1,256,256]{2,1,0:T(8,128)(2,1)} %param.18) | copy-start | bytes 393220
  4.9 0.8 %copy-start.4 = (bf16[1,128,256]{2,1,0:T(8,128)(2,1)S(1)}, bf16[1,128,256]{2,1,0:T(8,128)(2,1)}, u32[]{:S(2)}) copy-start(bf16[1,128,256]{2,1,0:T(8,128)(2,1)} %param.17) | copy-start | bytes 196612
  5.7 0.8 %copy-start.5 = (f32[1,16,512]{2,1,0:T(8,128)S(1)}, f32[1,16,512]{2,1,0:T(8,128)}, u32[]{:S(2)}) copy-start(f32[1,16,512]{2,1,0:T(8,128)} %param.12) | copy-start | bytes 98308
  6.5 0.7 %copy-start.6 = (s32[512]{0:T(512)S(1)}, s32[512]{0:T(512)}, u32[]{:S(2)}) copy-start(s32[512]{0:T(512)} %param.16) | copy-start | bytes 6148
  7.1 0.7 %copy-start.8 = (s32[1,512]{1,0:T(1,128)S(1)}, s32[1,512]{1,0:T(1,128)}, u32[]{:S(2)}) copy-start(s32[1,512]{1,0:T(1,128)} %counts_ref.1) | copy-start | bytes 6148
  7.8 0.7 %copy-start.9 = (s32[512]{0:T(512)S(1)}, s32[512]{0:T(512)}, u32[]{:S(2)}) copy-start(s32[512]{0:T(512)} %param.14) | copy-start | bytes 6148
  8.5 0.7 %copy-start.10 = (s32[512]{0:T(512)S(1)}, s32[512]{0:T(512)}, u32[]{:S(2)}) copy-start(s32[512]{0:T(512)} %param.15) | copy-start | bytes 6148
  9.2 23.9 %copy-start.1 = (bf16[1,16,512,128]{3,2,1,0:T(8,128)(2,1)S(1)}, bf16[1,16,512,128]{3,2,1,0:T(8,128)(2,1)}, u32[]{:S(2)}) copy-start(bf16[1,16,512,128]{3,2,1,0:T(8,128)(2,1)} %param.11) | copy-start | bytes 6291460
  19.7 4.6 %collective-permute-start = (f32[1,4,512]{2,1,0:T(4,128)S(1)}, f32[1,4,512]{2,1,0:T(4,128)S(1)}, u32[]{:S(2)}, u32[]{:S(2)}) collective-permute-start(f32[1,4,512]{2,1,0:T(4,128)S(1)} %bitcast.20), channel_id=1, source_target_pairs={{0,4},{4,0},{8,12},{12,8},{16,20},{20,16},{24,28},{28,24},{1,5},{5... | collective-permute-start | bytes 24584 | tf_op jit(solution)/shard_map/ppermute | solution.py:265
  24.3 3.8 %collective-permute-start.1 = (f32[2,4,512]{2,1,0:T(4,128)S(1)}, f32[2,4,512]{2,1,0:T(4,128)S(1)}, u32[]{:S(2)}, u32[]{:S(2)}) collective-permute-start(f32[2,4,512]{2,1,0:T(4,128)S(1)} %pad_maximum_fusion.1), channel_id=1, source_target_pairs={{0,8},{4,12},{8,0},{12,4},{16,24},{20,28},{24,16},{28,20},{1,9},{5... | collective-permute-start | bytes 49160 | tf_op jit(solution)/shard_map/ppermute | solution.py:265
  28.1 5.0 %collective-permute-start.2 = (f32[4,4,512]{2,1,0:T(4,128)S(1)}, f32[4,4,512]{2,1,0:T(4,128)S(1)}, u32[]{:S(2)}, u32[]{:S(2)}) collective-permute-start(f32[4,4,512]{2,1,0:T(4,128)S(1)} %pad_maximum_fusion), channel_id=1, source_target_pairs={{0,16},{4,20},{8,24},{12,28},{16,0},{20,4},{24,8},{28,12},{1,17},{... | collective-permute-start | bytes 98312 | tf_op jit(solution)/shard_map/ppermute | solution.py:265
  33.1 0.9 %copy-start.3 = (bf16[1,256,256]{2,1,0:T(8,128)(2,1)S(1)}, bf16[1,256,256]{2,1,0:T(8,128)(2,1)}, u32[]{:S(2)}) copy-start(bf16[1,256,256]{2,1,0:T(8,128)(2,1)} %param.18) | copy-start | bytes 393220
  34.0 0.7 %copy-start.7 = (s32[512]{0:T(512)S(1)}, s32[512]{0:T(512)}, u32[]{:S(2)}) copy-start(s32[512]{0:T(512)} %param.16) | copy-start | bytes 6148
  46.7 1.5 %collective-permute-start.3 = (f32[200,256]{1,0:T(8,128)S(1)}, f32[200,256]{1,0:T(8,128)S(1)}, u32[]{:S(2)}, u32[]{:S(2)}) collective-permute-start(f32[200,256]{1,0:T(8,128)S(1)} %get-tuple-element.22), channel_id=1, source_target_pairs={{0,1},{1,0},{2,3},{3,2},{4,5},{5,4},{6,7},{7,6},{8,9},{9,8},{10,11... | collective-permute-start | bytes 614408 | tf_op jit(solution)/shard_map/ppermute | solution.py:290
  48.2 7.3 %collective-permute-start.4 = (f32[200,256]{1,0:T(8,128)S(1)}, f32[200,256]{1,0:T(8,128)S(1)}, u32[]{:S(2)}, u32[]{:S(2)}) collective-permute-start(f32[200,256]{1,0:T(8,128)S(1)} %add.11), channel_id=1, source_target_pairs={{0,2},{1,3},{2,0},{3,1},{4,6},{5,7},{6,4},{7,5},{8,10},{9,11},{10,... | collective-permute-start | bytes 614408 | tf_op jit(solution)/shard_map/ppermute | solution.py:293
  55.6 1.5 %collective-permute-start.5 = (f32[200,256]{1,0:T(8,128)S(1)}, f32[200,256]{1,0:T(8,128)S(1)}, u32[]{:S(2)}, u32[]{:S(2)}) collective-permute-start(f32[200,256]{1,0:T(8,128)S(1)} %add.12.own_ref), channel_id=1, source_target_pairs={{0,1},{1,0},{2,3},{3,2},{4,5},{5,4},{6,7},{7,6},{8,9},{9,8},{10,11... | collective-permute-start | bytes 614408 | tf_op jit(solution)/shard_map/ppermute | solution.py:295

commit v2 on v1

v2 whole, which is shorter than its diff:
```python
import functools

import jax
import jax.numpy as jnp
from jax import lax
from jax.experimental import pallas as pl
from jax.experimental.pallas import tpu as pltpu
from jax.sharding import PartitionSpec as P

F32 = jnp.float32
BF16 = jnp.bfloat16
VMEM = pl.BlockSpec(memory_space=pltpu.VMEM)
SMEM = pl.BlockSpec(memory_space=pltpu.SMEM)
HBM = pl.BlockSpec(memory_space=pltpu.HBM)
LIMIT = pltpu.CompilerParams(vmem_limit_bytes=32 * 1024 * 1024)
CHUNKS = 4


def dot_nn(a, b):
    return lax.dot_general(a, b, (((1,), (0,)), ((), ())), preferred_element_type=F32)


def dot_nt(a, b):
    return lax.dot_general(a, b, (((1,), (1,)), ((), ())), preferred_element_type=F32)


def dot_tn(a, b):
    return lax.dot_general(a, b, (((0,), (0,)), ((), ())), preferred_element_type=F32)


def running_sum(values):
    rows = values.shape[0]
    ids = lax.broadcasted_iota(jnp.int32, values.shape, 0)
    shift = 1
    while shift < rows:
        moved = pltpu.roll(values, shift, 0)
        values = values + jnp.where(ids >= shift, moved, 0.0)
        shift *= 2
    return values


def split_three(values):
    high = values.astype(BF16)
    rest = values - high.astype(F32)
    mid = rest.astype(BF16)
    low = (rest - mid.astype(F32)).astype(BF16)
    return high, mid, low


def projection(head, field_out):
    first = jnp.where(lax.broadcasted_iota(jnp.int32, (1, head.shape[1]), 1) == 0, 1.0, 0.0).astype(BF16)
    density = dot_nn(first, field_out)
    high, mid, low = split_three(head)
    proj = dot_nn(high, field_out) + (dot_nn(mid, field_out) + dot_nn(low, field_out))
    proj_high = proj.astype(BF16).astype(F32)
    rest = proj - proj_high
    eight = jnp.concatenate([density, proj_high, rest, jnp.zeros_like(density)], axis=0)
    return jnp.concatenate([eight, eight], axis=0).astype(BF16)


def positive(values):
    rounded = values.astype(BF16)
    return jnp.maximum(rounded, jnp.zeros_like(rounded))


def where_positive(mask, values):
    rounded = values.astype(BF16)
    return jnp.where(mask > 0, rounded, jnp.zeros_like(rounded))


def forward_kernel(
    slab_ref, x_hbm, spacing_hbm, counts_hbm, first_hbm, last_hbm, direction_hbm, target_hbm,
    w1_hbm, w2_hbm, w3_hbm, head_hbm,
    seg_ref, x_ref, h1_ref, h2_ref, save_ref, w16_ref, w2_ref, direction_ref, target_ref,
    w1_ref, w3_ref, head_ref, spacing_ref, counts_ref, first_ref, last_ref, out8, sems,
):
    samples, _, rays = out8.shape
    count = x_ref.shape[0]
    chunk = count // CHUNKS
    moves = [
        pltpu.make_async_copy(source, place, sems.at[i])
        for i, (source, place) in enumerate(
            (
                (head_hbm, head_ref), (w3_hbm, w3_ref), (w1_hbm, w1_ref), (w2_hbm, w2_ref),
                (spacing_hbm, spacing_ref), (counts_hbm, counts_ref), (first_hbm, first_ref),
                (last_hbm, last_ref), (direction_hbm, direction_ref), (target_hbm, target_ref),
            )
        )
    ]
    loads = [
        pltpu.make_async_copy(
            x_hbm.at[pl.ds(c * chunk, chunk)], x_ref.at[pl.ds(c * chunk, chunk)], sems.at[len(moves) + c]
        )
        for c in range(CHUNKS)
    ]
    for move in moves[:3] + loads[:1] + moves[3:4] + loads[1:] + moves[4:]:
        move.start()
    moves[0].wait()
    moves[1].wait()
    w16_ref[...] = projection(head_ref[...], w3_ref[...])
    moves[2].wait()
    moves[3].wait()

    for c in range(CHUNKS):
        loads[c].wait()
        rows = pl.ds(c * chunk, chunk)
        h1 = positive(dot_nn(x_ref[rows], w1_ref[...]))
        h1_ref[rows] = h1
        h2 = positive(dot_nn(h1, w2_ref[...]))
        h2_ref[rows] = h2
        eight = dot_nt(w16_ref[...], h2)[:8]
        each = chunk // rays
        for j in range(each):
            out8[c * each + j] = eight[:, j * rays : (j + 1) * rays]

    for move in moves[4:]:
        move.wait()
    slab = slab_ref[0]
    density = out8[:, 0, :]
    proj = [out8[:, 1 + k, :] + out8[:, 4 + k, :] for k in range(3)]
    ids = lax.broadcasted_iota(jnp.int32, density.shape, 0)
    active = (first_ref[...] <= slab) & (slab < last_ref[...])
    live = jnp.where((ids < counts_ref[...]) & active, 1.0, 0.0)
    span = spacing_ref[...] * live
    optical = (jnp.maximum(density, 0.0) + jnp.log1p(jnp.exp(-jnp.abs(density)))) * span
    running = running_sum(optical)
    column = running[samples - 1 : samples]
    before = jnp.where(direction_ref[...] > 0, column - running, running - optical)
    reach = jnp.exp(-before)
    passed = jnp.exp(-optical)
    weights = reach * (1.0 - passed)
    seg_ref[...] = jnp.concatenate(
        [jnp.exp(-column)] + [jnp.sum(weights * p, axis=0, keepdims=True) for p in proj], axis=0
    )
    save_ref[0] = weights
    save_ref[1] = reach * passed
    save_ref[2] = span * jax.nn.sigmoid(density)
    for k in range(3):
        save_ref[3 + k] = proj[k]


def backward_kernel(
    ids_ref, x_ref, h1_ref, h2_ref, save_ref, w16_ref, w2_ref, direction_ref, target_ref, *refs,
    n_pieces, n_slab,
):
    pieces = refs[:n_pieces]
    front_hbm, keep_ref, send_ref, front_ref, every, q8, q16, mid_ref, in_ref, out_ref, sem = refs[n_pieces:]
    samples, _, rays = q8.shape
    count = x_ref.shape[0]
    slab = ids_ref[0]
    core = ids_ref[1]
    at = 0
    for piece in pieces:
        for i in range(piece.shape[0]):
            every[at + i] = piece[i]
        at += piece.shape[0]
    forward_ray = direction_ref[...] <= 0

    one = jnp.ones((1, rays), F32)
    zero = jnp.zeros((3, rays), F32)

    def compose(ascending):
        trans, color = one, zero
        order = range(n_slab) if ascending else range(n_slab - 1, -1, -1)
        early = forward_ray if ascending else jnp.logical_not(forward_ray)
        for s in order:
            item = every[jnp.bitwise_xor(slab, s)]
            keep = (s < slab) if ascending else (s > slab)
            item_trans = jnp.where(keep, item[0:1], 1.0)
            item_color = jnp.where(keep, item[1:4], 0.0)
            color = jnp.where(early, color + trans * item_color, item_color + item_trans * color)
            trans = trans * item_trans
        return trans, color

    low_trans, low_color = compose(True)
    high_trans, high_color = compose(False)
    front_trans = jnp.where(forward_ray, low_trans, high_trans)
    front_color = jnp.where(forward_ray, low_color, high_color)
    back_color = jnp.where(forward_ray, high_color, low_color)
    front_ref[...] = front_trans
    store = pltpu.make_async_copy(front_ref, front_hbm, sem)
    store.start()
    own = every[0]
    own_trans = own[0:1]
    logits = front_color + front_trans * own[1:4] + (front_trans * own_trans) * back_color
    shade = jax.nn.sigmoid(logits)
    error = (shade - target_ref[...]) / rays
    grad_logit = error * shade * (1.0 - shade)
    grad_trans = front_trans * jnp.sum(grad_logit * back_color, axis=0, keepdims=True)
    pull = front_trans * grad_logit

    weights = save_ref[0]
    grad_weight = pull[0:1] * save_ref[3] + pull[1:2] * save_ref[4] + pull[2:3] * save_ref[5]
    product = weights * grad_weight
    running = running_sum(product)
    total = running[samples - 1 : samples]
    after = jnp.where(forward_ray, total - running, running - product)
    grad_optical = grad_weight * save_ref[1] - after - grad_trans * own_trans
    q8[:, 0, :] = grad_optical * save_ref[2]
    for k in range(3):
        q = weights * pull[k : k + 1]
        q8[:, 1 + k, :] = q
        q8[:, 4 + k, :] = q
    q8[:, 7, :] = jnp.zeros_like(weights)
    for j in range(samples):
        rows = q8[j]
        high = rows.astype(BF16).astype(F32)
        q16[:, j * rays : (j + 1) * rays] = jnp.concatenate([high, rows - high], axis=0).astype(BF16)

    chunk = count // CHUNKS
    for c in range(CHUNKS):
        rows = pl.ds(c * chunk, chunk)
        q = q16[:, rows]
        h1 = h1_ref[rows]
        h2 = h2_ref[rows]
        back_two = where_positive(h2, dot_tn(q, w16_ref[...]))
        grad_out = dot_nn(q, h2)
        grad_mid = dot_tn(h1, back_two)
        back_one = where_positive(h1, dot_nt(back_two, w2_ref[...]))
        grad_in = dot_tn(x_ref[rows], back_one)
        for ref, part in ((out_ref, grad_out), (mid_ref, grad_mid), (in_ref, grad_in)):
            ref[...] = part if c == 0 else ref[...] + part

    half_mid = mid_ref.shape[0] // 2
    half_in = in_ref.shape[0] // 2
    rows_in = half_mid + half_in
    for place, half in ((send_ref, 1 - core), (keep_ref, core)):
        place[:half_mid] = mid_ref[pl.ds(pl.multiple_of(half * half_mid, half_mid), half_mid)]
        place[half_mid:rows_in] = in_ref[pl.ds(pl.multiple_of(half * half_in, half_in), half_in)]
        place[rows_in:] = out_ref[:8] + out_ref[8:]
    store.wait()


def final_kernel(core_ref, own_ref, other_ref, head_ref, in_hbm, mid_hbm, out_hbm, out_ref, sems):
    core = core_ref[0]
    half_mid = mid_hbm.shape[0] // 2
    half_in = in_hbm.shape[0] // 2
    rows_in = half_mid + half_in
    moves = []
    for source, half in ((own_ref, core), (other_ref, 1 - core)):
        for start, size, place in ((0, half_mid, mid_hbm), (half_mid, half_in, in_hbm)):
            moves.append(
                pltpu.make_async_copy(
                    source.at[pl.ds(start, size)],
                    place.at[pl.ds(pl.multiple_of(half * size, size), size)],
                    sems.at[len(moves)],
                )
            )
    for move in moves:
        move.start()
    factors = own_ref[rows_in:]
    head = head_ref[...]
    width = head.shape[1]
    first = jnp.where(lax.broadcasted_iota(jnp.int32, (1, width), 1) == 0, 1.0, 0.0)
    rows = jnp.concatenate([first, head, jnp.zeros((4, width), F32)], axis=0)
    out_ref[...] = lax.dot_general(
        rows, factors, (((0,), (0,)), ((), ())), preferred_element_type=F32, precision=lax.Precision.HIGHEST
    )
    moves.append(pltpu.make_async_copy(out_ref, out_hbm, sems.at[len(moves)]))
    moves[-1].start()
    for move in moves:
        move.wait()


def pairs(size, bit):
    return [(i, i ^ bit) for i in range(size)]


def make_body(n_slab, n_tile):

    def body(
        encoded, spacing, counts, seg_first, seg_last, direction,
        field_in, field_mid, field_out, color_head, target,
    ):
        _, samples, rays, width = encoded.shape
        hidden = field_mid.shape[1]
        features = field_out.shape[2]
        count = samples * rays
        slab = lax.axis_index("slab")
        core = lax.axis_index("tile") % 2
        row = lambda a: a.reshape(1, rays)
        ids = jnp.stack([slab, core]).astype(jnp.int32)
        seg, *kept = pl.pallas_call(
            forward_kernel,
            name="forward",
            out_shape=(
                pltpu.VMEM((4, rays), F32),
                pltpu.VMEM((count, width), BF16),
                pltpu.VMEM((count, hidden), BF16),
                pltpu.VMEM((count, hidden), BF16),
                pltpu.VMEM((6, samples, rays), F32),
                pltpu.VMEM((16, hidden), BF16),
                pltpu.VMEM((hidden, hidden), BF16),
                pltpu.VMEM((1, rays), jnp.int32),
                pltpu.VMEM((3, rays), F32),
            ),
            in_specs=[SMEM] + [HBM] * 11,
            out_specs=(VMEM,) * 9,
            scratch_shapes=[
                pltpu.VMEM((width, hidden), BF16),
                pltpu.VMEM((features, hidden), BF16),
                pltpu.VMEM((3, features), F32),
                pltpu.VMEM((samples, rays), F32),
                pltpu.VMEM((1, rays), jnp.int32),
                pltpu.VMEM((1, rays), jnp.int32),
                pltpu.VMEM((1, rays), jnp.int32),
                pltpu.VMEM((samples, 8, rays), F32),
                pltpu.SemaphoreType.DMA((10 + CHUNKS,)),
            ],
            compiler_params=LIMIT,
        )(
            ids,
            *(
                pltpu.with_memory_space_constraint(a, pltpu.HBM)
                for a in (
                    encoded[0].reshape(count, width), spacing[0], counts, row(seg_first), row(seg_last),
                    row(direction), target.T, field_in[0], field_mid[0], field_out[0].T, color_head.T,
                )
            ),
        )

        known = seg[None]
        pieces = [known]
        bit = 1
        while bit < n_slab:
            got = lax.ppermute(known, "slab", pairs(n_slab, bit))
            pieces.append(got)
            bit *= 2
            if bit < n_slab:
                known = jnp.concatenate([known, got], axis=0)

        half = (hidden + width) // 2 + 8
        front, keep, send = pl.pallas_call(
            functools.partial(backward_kernel, n_pieces=len(pieces), n_slab=n_slab),
            name="backward",
            out_shape=(
                pltpu.HBM((1, rays), F32),
                pltpu.VMEM((half, hidden), F32),
                pltpu.VMEM((half, hidden), F32),
            ),
            in_specs=[SMEM] + [VMEM] * (8 + len(pieces)),
            out_specs=(HBM, VMEM, VMEM),
            scratch_shapes=[
                pltpu.VMEM((1, rays), F32),
                pltpu.VMEM((n_slab, 4, rays), F32),
                pltpu.VMEM((samples, 8, rays), F32),
                pltpu.VMEM((16, count), BF16),
                pltpu.VMEM((hidden, hidden), F32),
                pltpu.VMEM((width, hidden), F32),
                pltpu.VMEM((16, hidden), F32),
                pltpu.SemaphoreType.DMA,
            ],
            compiler_params=LIMIT,
        )(ids, *kept, *pieces)

        part = keep + lax.ppermute(send, "tile", pairs(n_tile, 1))
        bit = 2
        while bit < n_tile:
            part = part + lax.ppermute(part, "tile", pairs(n_tile, bit))
            bit *= 2
        other = lax.ppermute(part, "tile", pairs(n_tile, 1))
        grad_in, grad_mid, grad_out = pl.pallas_call(
            final_kernel,
            name="final",
            out_shape=(
                pltpu.HBM((width, hidden), F32),
                pltpu.HBM((hidden, hidden), F32),
                pltpu.HBM((features, hidden), F32),
            ),
            in_specs=[SMEM] + [VMEM] * 3,
            out_specs=(HBM,) * 3,
            scratch_shapes=[pltpu.VMEM((features, hidden), F32), pltpu.SemaphoreType.DMA((5,))],
            compiler_params=LIMIT,
        )(core.reshape(1).astype(jnp.int32), part, other, color_head.T)
        return front, grad_in[None], grad_mid[None], grad_out.T[None]

    return body


def solution(mesh):
    return jax.shard_map(
        make_body(mesh.shape["slab"], mesh.shape["tile"]),
        mesh=mesh,
        in_specs=(
            P("slab", None, "tile", None),
            P("slab", None, "tile"),
            P("slab", "tile"),
            P("tile"),
            P("tile"),
            P("tile"),
            P("slab", None, None),
            P("slab", None, None),
            P("slab", None, None),
            P(),
            P("tile", None),
        ),
        out_specs=(
            P("slab", "tile"),
            P("slab", None, None),
            P("slab", None, None),
            P("slab", None, None),
        ),
        check_vma=False,
    )
```

time: 59.5 us -> 37.7 us (0.63)
  local copies, waits for them, and re-layouts: 11.6 us -> 0.01 us
  Pallas kernels: 23.6 us -> 12.9 us
  waiting for transfers between devices: 12.7 us -> 13.5 us
    unnamed x26 -> x2, local copies, waits for them, and re-layouts: 11.6 us -> 0.01 us
    pallas_call x1, Pallas kernels: 12 us -> 6.1 us  [body(): pl.pallas_call(functools.partial(backward_kernel, n_pieces=len(pieces), n...]
    pallas_call x2, Pallas kernels: 11.6 us -> 6.85 us  [the longest x1 5.91 us: body(): pl.pallas_call(forward_kernel, name='forward', out_shape=(pltpu.VMEM((4,...]
    ppermute x3, waiting for transfers between devices: 4.4 us -> 5.24 us  [body(): got = lax.ppermute(known, 'slab', pairs(n_slab, bit))]
  transfers between devices with their start and end apart: 6 -> 6, of which waited for: 6 -> 6; matrix products, arithmetic and copies ran while one was open for 1% -> 0% of each run, Pallas kernels for 0% -> 0%
where the time goes in v2:
time: 37.7 us; the launch traced here: 37.5 us
  waiting for transfers between devices  13.5 us (36%)
  Pallas kernels  12.9 us (34%)
  starting transfers between devices  10.3 us (27%)
  between operations  0.69 us (2%)
    ppermute x3, starting transfers between devices, body(): got = lax.ppermute(known, 'slab', pairs(n_slab, bit))  8.21 us
    pallas_call x1, Pallas kernels, body(): pl.pallas_call(functools.partial(backward_kernel, n_pieces=len(pieces), n...  6.1 us
    pallas_call x1, Pallas kernels, body(): pl.pallas_call(forward_kernel, name='forward', out_shape=(pltpu.VMEM((4,...  5.91 us
    ppermute x1, waiting for transfers between devices, body(): part = part + lax.ppermute(part, 'tile', pairs(n_tile, bit))  5.38 us
    ppermute x3, waiting for transfers between devices, body(): got = lax.ppermute(known, 'slab', pairs(n_slab, bit))  5.24 us
    ppermute x1, starting transfers between devices, body(): part = part + lax.ppermute(part, 'tile', pairs(n_tile, bit))  1.9 us
    ppermute x1, waiting for transfers between devices, body(): part = keep + lax.ppermute(send, 'tile', pairs(n_tile, 1))  1.44 us
    ppermute x1, waiting for transfers between devices, body(): other = lax.ppermute(part, 'tile', pairs(n_tile, 1))  1.44 us
  transfers between devices with their start and end apart: 6, of which 6 were waited for; matrix products, arithmetic and copies ran while one was open for 0% of the time, Pallas kernels for 0%

profile of v2, /device:TPU:0, one launch (start us, length us, event | category | flops | bytes accessed | tf_op | source)
XLA Modules:
  0.0 37.5 jit_solution(10143960767151532212)
XLA Ops:
  0.6 0.1 pad_add_fusion.slab_ref.ids_ref
  0.7 5.9 %forward.1 = (f32[4,512]{1,0:T(4,128)S(1)}, bf16[8192,128]{1,0:T(8,128)(2,1)S(1)}, bf16[8192,256]{1,0:T(8,128)(2,1)S(1)}, bf16[8192,256]{1,0:T(8,128)(2,1)S(1)},...) custom-call(s32[2]{0:T(128)S(1)} %pad_add_fusion.slab_ref.ids_ref, ...), custom_call_target="tpu_custom_call" | custom-call | tf_op jit(solution)/shard_map/forward/pallas_call | solution.py:283
  6.6 3.0 %collective-permute-start = (f32[1,4,512]{2,1,0:T(4,128)S(1)}, f32[1,4,512]{2,1,0:T(4,128)S(1)}, u32[]{:S(2)}, u32[]{:S(2)}) collective-permute-start(f32[1,4,512]{2,1,0:T(4,128)S(1)} %bitcast.20), channel_id=1, source_target_pairs={{0,4},{4,0},{8,12},{12,8},{16,20},{20,16},{24,28},{28,24},{1,5},{5... | collective-permute-start | bytes 24584 | tf_op jit(solution)/shard_map/ppermute | solution.py:326
  9.6 1.6 %collective-permute-done.refs_1_ = f32[1,4,512]{2,1,0:T(4,128)S(1)} collective-permute-done((f32[1,4,512]{2,1,0:T(4,128)S(1)}, f32[1,4,512]{2,1,0:T(4,128)S(1)}, u32[]{:S(2)}, u32[]{:S(2)}) %collective-permute-start) | collective-permute-done | bytes 8224 | tf_op jit(solution)/shard_map/ppermute | solution.py:326
  11.3 2.1 %collective-permute-start.1 = (f32[2,4,512]{2,1,0:T(4,128)S(1)}, f32[2,4,512]{2,1,0:T(4,128)S(1)}, u32[]{:S(2)}, u32[]{:S(2)}) collective-permute-start(f32[2,4,512]{2,1,0:T(4,128)S(1)} %pad_maximum_fusion.1), channel_id=1, source_target_pairs={{0,8},{4,12},{8,0},{12,4},{16,24},{20,28},{24,16},{28,20},{1,9},{5... | collective-permute-start | bytes 49160 | tf_op jit(solution)/shard_map/ppermute | solution.py:326
  13.4 1.7 %collective-permute-done.1.refs_2_ = f32[2,4,512]{2,1,0:T(4,128)S(1)} collective-permute-done((f32[2,4,512]{2,1,0:T(4,128)S(1)}, f32[2,4,512]{2,1,0:T(4,128)S(1)}, u32[]{:S(2)}, u32[]{:S(2)}) %collective-permute-start.1) | collective-permute-done | bytes 16416 | tf_op jit(solution)/shard_map/ppermute | solution.py:326
  15.1 3.1 %collective-permute-start.2 = (f32[4,4,512]{2,1,0:T(4,128)S(1)}, f32[4,4,512]{2,1,0:T(4,128)S(1)}, u32[]{:S(2)}, u32[]{:S(2)}) collective-permute-start(f32[4,4,512]{2,1,0:T(4,128)S(1)} %pad_maximum_fusion), channel_id=1, source_target_pairs={{0,16},{4,20},{8,24},{12,28},{16,0},{20,4},{24,8},{28,12},{1,17},{... | collective-permute-start | bytes 98312 | tf_op jit(solution)/shard_map/ppermute | solution.py:326
  18.2 1.9 %collective-permute-done.2.refs_3_ = f32[4,4,512]{2,1,0:T(4,128)S(1)} collective-permute-done((f32[4,4,512]{2,1,0:T(4,128)S(1)}, f32[4,4,512]{2,1,0:T(4,128)S(1)}, u32[]{:S(2)}, u32[]{:S(2)}) %collective-permute-start.2) | collective-permute-done | bytes 32800 | tf_op jit(solution)/shard_map/ppermute | solution.py:326
  20.1 0.0 copy-start
  20.1 6.1 %backward.1 = (f32[1,512]{1,0:T(1,128)}, f32[200,256]{1,0:T(8,128)S(1)}, f32[200,256]{1,0:T(8,128)S(1)}) custom-call(s32[2]{0:T(128)S(1)} %pad_add_fusion.slab_ref.ids_ref, bf16[8192,128]{1,0:T(8,128)(2,1)S(1)} %get-tuple-element.19.x_ref, bf16[8192,256]{1,0:T(8,128)(2,1)S(1)} %get-tuple-element.20.h1_ref, bf16[8192,256]{1,0:T(8,128)(2,1)S(1)} %get-tuple-element.21.h2_ref, ...), custom_call_target="tpu_custom_call" | custom-call | tf_op jit(solution)/shard_map/backward/pallas_call | solution.py:333
  26.2 0.1 collective-permute-start.3
  26.3 1.4 %collective-permute-done.3 = f32[200,256]{1,0:T(8,128)S(1)} collective-permute-done((f32[200,256]{1,0:T(8,128)S(1)}, f32[200,256]{1,0:T(8,128)S(1)}, u32[]{:S(2)}, u32[]{:S(2)}) %collective-permute-start.3) | collective-permute-done | bytes 204832 | tf_op jit(solution)/shard_map/ppermute | solution.py:356
  27.8 1.9 %collective-permute-start.4 = (f32[200,256]{1,0:T(8,128)S(1)}, f32[200,256]{1,0:T(8,128)S(1)}, u32[]{:S(2)}, u32[]{:S(2)}) collective-permute-start(f32[200,256]{1,0:T(8,128)S(1)} %add.11), channel_id=1, source_target_pairs={{0,2},{1,3},{2,0},{3,1},{4,6},{5,7},{6,4},{7,5},{8,10},{9,11},{10,... | collective-permute-start | bytes 614408 | tf_op jit(solution)/shard_map/ppermute | solution.py:359
  29.7 5.4 %collective-permute-done.4 = f32[200,256]{1,0:T(8,128)S(1)} collective-permute-done((f32[200,256]{1,0:T(8,128)S(1)}, f32[200,256]{1,0:T(8,128)S(1)}, u32[]{:S(2)}, u32[]{:S(2)}) %collective-permute-start.4) | collective-permute-done | bytes 204832 | tf_op jit(solution)/shard_map/ppermute | solution.py:359
  35.1 0.1 collective-permute-start.5
  35.2 1.4 %collective-permute-done.5.other_ref = f32[200,256]{1,0:T(8,128)S(1)} collective-permute-done((f32[200,256]{1,0:T(8,128)S(1)}, f32[200,256]{1,0:T(8,128)S(1)}, u32[]{:S(2)}, u32[]{:S(2)}) %collective-permute-start.5) | collective-permute-done | bytes 204832 | tf_op jit(solution)/shard_map/ppermute | solution.py:361
  36.6 0.0 copy-done
  36.6 0.9 %final.1 = (f32[128,256]{1,0:T(8,128)}, f32[256,256]{1,0:T(8,128)}, f32[64,256]{1,0:T(8,128)}) custom-call(s32[1]{0:T(128)} %bitcast.1.core_ref, f32[200,256]{1,0:T(8,128)S(1)} %add.12.own_ref, f32[200,256]{1,0:T(8,128)S(1)} %collective-permute-done.5.other_ref, f32[3,64]{1,0:T(4,128)S(1)} %bitcast.25), custom_call_target="tpu_custom_call" | custom-call | tf_op jit(solution)/shard_map/final/pallas_call | solution.py:362
  (4 shorter events, 0.1 us)
Async XLA Ops:
  6.6 4.6 %collective-permute-start = (f32[1,4,512]{2,1,0:T(4,128)S(1)}, f32[1,4,512]{2,1,0:T(4,128)S(1)}, u32[]{:S(2)}, u32[]{:S(2)}) collective-permute-start(f32[1,4,512]{2,1,0:T(4,128)S(1)} %bitcast.20), channel_id=1, source_target_pairs={{0,4},{4,0},{8,12},{12,8},{16,20},{20,16},{24,28},{28,24},{1,5},{5... | collective-permute-start | bytes 24584 | tf_op jit(solution)/shard_map/ppermute | solution.py:326
  11.3 3.8 %collective-permute-start.1 = (f32[2,4,512]{2,1,0:T(4,128)S(1)}, f32[2,4,512]{2,1,0:T(4,128)S(1)}, u32[]{:S(2)}, u32[]{:S(2)}) collective-permute-start(f32[2,4,512]{2,1,0:T(4,128)S(1)} %pad_maximum_fusion.1), channel_id=1, source_target_pairs={{0,8},{4,12},{8,0},{12,4},{16,24},{20,28},{24,16},{28,20},{1,9},{5... | collective-permute-start | bytes 49160 | tf_op jit(solution)/shard_map/ppermute | solution.py:326
  15.1 5.0 %collective-permute-start.2 = (f32[4,4,512]{2,1,0:T(4,128)S(1)}, f32[4,4,512]{2,1,0:T(4,128)S(1)}, u32[]{:S(2)}, u32[]{:S(2)}) collective-permute-start(f32[4,4,512]{2,1,0:T(4,128)S(1)} %pad_maximum_fusion), channel_id=1, source_target_pairs={{0,16},{4,20},{8,24},{12,28},{16,0},{20,4},{24,8},{28,12},{1,17},{... | collective-permute-start | bytes 98312 | tf_op jit(solution)/shard_map/ppermute | solution.py:326
  20.1 16.5 %copy-start = (f32[64,3]{0,1:T(4,128)S(1)}, f32[64,3]{0,1:T(4,128)}, u32[]{:S(2)}) copy-start(f32[64,3]{0,1:T(4,128)} %param.20) | copy-start | bytes 2308
  26.2 1.5 %collective-permute-start.3 = (f32[200,256]{1,0:T(8,128)S(1)}, f32[200,256]{1,0:T(8,128)S(1)}, u32[]{:S(2)}, u32[]{:S(2)}) collective-permute-start(f32[200,256]{1,0:T(8,128)S(1)} %get-tuple-element.30), channel_id=1, source_target_pairs={{0,1},{1,0},{2,3},{3,2},{4,5},{5,4},{6,7},{7,6},{8,9},{9,8},{10,11... | collective-permute-start | bytes 614408 | tf_op jit(solution)/shard_map/ppermute | solution.py:356
  27.8 7.3 %collective-permute-start.4 = (f32[200,256]{1,0:T(8,128)S(1)}, f32[200,256]{1,0:T(8,128)S(1)}, u32[]{:S(2)}, u32[]{:S(2)}) collective-permute-start(f32[200,256]{1,0:T(8,128)S(1)} %add.11), channel_id=1, source_target_pairs={{0,2},{1,3},{2,0},{3,1},{4,6},{5,7},{6,4},{7,5},{8,10},{9,11},{10,... | collective-permute-start | bytes 614408 | tf_op jit(solution)/shard_map/ppermute | solution.py:359
  35.1 1.5 %collective-permute-start.5 = (f32[200,256]{1,0:T(8,128)S(1)}, f32[200,256]{1,0:T(8,128)S(1)}, u32[]{:S(2)}, u32[]{:S(2)}) collective-permute-start(f32[200,256]{1,0:T(8,128)S(1)} %add.12.own_ref), channel_id=1, source_target_pairs={{0,1},{1,0},{2,3},{3,2},{4,5},{5,4},{6,7},{7,6},{8,9},{9,8},{10,11... | collective-permute-start | bytes 614408 | tf_op jit(solution)/shard_map/ppermute | solution.py:361

commit v3 on v2

--- a/solution.py
+++ b/solution.py
@@ -10,10 +10,10 @@
 F32 = jnp.float32
 BF16 = jnp.bfloat16
 VMEM = pl.BlockSpec(memory_space=pltpu.VMEM)
-SMEM = pl.BlockSpec(memory_space=pltpu.SMEM)
 HBM = pl.BlockSpec(memory_space=pltpu.HBM)
 LIMIT = pltpu.CompilerParams(vmem_limit_bytes=32 * 1024 * 1024)
-CHUNKS = 4
+FORWARD_CHUNKS = 4
+BACKWARD_CHUNKS = 8
 
 
 def dot_nn(a, b):
@@ -69,14 +69,14 @@
 
 
 def forward_kernel(
-    slab_ref, x_hbm, spacing_hbm, counts_hbm, first_hbm, last_hbm, direction_hbm, target_hbm,
+    x_hbm, spacing_hbm, counts_hbm, first_hbm, last_hbm, direction_hbm, target_hbm,
     w1_hbm, w2_hbm, w3_hbm, head_hbm,
-    seg_ref, x_ref, h1_ref, h2_ref, save_ref, w16_ref, w2_ref, direction_ref, target_ref,
-    w1_ref, w3_ref, head_ref, spacing_ref, counts_ref, first_ref, last_ref, out8, sems,
+    seg_ref, order_ref, x_ref, h1_ref, h2_ref, save_ref, w16_ref, w2_ref, target_ref,
+    w1_ref, w3_ref, head_ref, spacing_ref, counts_ref, first_ref, last_ref, direction_ref, out8, sems,
 ):
     samples, _, rays = out8.shape
     count = x_ref.shape[0]
-    chunk = count // CHUNKS
+    chunk = count // FORWARD_CHUNKS
     moves = [
         pltpu.make_async_copy(source, place, sems.at[i])
         for i, (source, place) in enumerate(
@@ -88,10 +88,8 @@
         )
     ]
     loads = [
-        pltpu.make_async_copy(
-            x_hbm.at[pl.ds(c * chunk, chunk)], x_ref.at[pl.ds(c * chunk, chunk)], sems.at[len(moves) + c]
-        )
-        for c in range(CHUNKS)
+        pltpu.make_async_copy(x_hbm.at[pl.ds(at, size)], x_ref.at[pl.ds(at, size)], sems.at[len(moves) + i])
+        for i, (at, size) in enumerate(((0, chunk), (chunk, count - chunk)))
     ]
     for move in moves[:3] + loads[:1] + moves[3:4] + loads[1:] + moves[4:]:
         move.start()
@@ -101,8 +99,9 @@
     moves[2].wait()
     moves[3].wait()
 
-    for c in range(CHUNKS):
-        loads[c].wait()
+    for c in range(FORWARD_CHUNKS):
+        if c < 2:
+            loads[c].wait()
         rows = pl.ds(c * chunk, chunk)
         h1 = positive(dot_nn(x_ref[rows], w1_ref[...]))
         h1_ref[rows] = h1
@@ -115,7 +114,11 @@
 
     for move in moves[4:]:
         move.wait()
-    slab = slab_ref[0]
+    slab = lax.axis_index("slab")
+    reverse = jnp.minimum(jnp.maximum(direction_ref[...], 0), 1)
+    for bit in range(order_ref.shape[0]):
+        higher = (slab >> bit) & 1
+        order_ref[bit] = 1 - (reverse ^ higher)
     density = out8[:, 0, :]
     proj = [out8[:, 1 + k, :] + out8[:, 4 + k, :] for k in range(3)]
     ids = lax.broadcasted_iota(jnp.int32, density.shape, 0)
@@ -140,47 +143,30 @@
 
 
 def backward_kernel(
-    ids_ref, x_ref, h1_ref, h2_ref, save_ref, w16_ref, w2_ref, direction_ref, target_ref, *refs,
-    n_pieces, n_slab,
+    own_ref, order_ref, x_ref, h1_ref, h2_ref, save_ref, w16_ref, w2_ref, target_ref, *refs, n_tile,
 ):
-    pieces = refs[:n_pieces]
-    front_hbm, keep_ref, send_ref, front_ref, every, q8, q16, mid_ref, in_ref, out_ref, sem = refs[n_pieces:]
+    n_bits = order_ref.shape[0]
+    pieces = refs[:n_bits]
+    front_hbm, keep_ref, send_ref, front_ref, q8, q16, mid_ref, in_ref, out_ref, sem = refs[n_bits:]
     samples, _, rays = q8.shape
     count = x_ref.shape[0]
-    slab = ids_ref[0]
-    core = ids_ref[1]
-    at = 0
-    for piece in pieces:
-        for i in range(piece.shape[0]):
-            every[at + i] = piece[i]
-        at += piece.shape[0]
-    forward_ray = direction_ref[...] <= 0
-
-    one = jnp.ones((1, rays), F32)
-    zero = jnp.zeros((3, rays), F32)
-
-    def compose(ascending):
-        trans, color = one, zero
-        order = range(n_slab) if ascending else range(n_slab - 1, -1, -1)
-        early = forward_ray if ascending else jnp.logical_not(forward_ray)
-        for s in order:
-            item = every[jnp.bitwise_xor(slab, s)]
-            keep = (s < slab) if ascending else (s > slab)
-            item_trans = jnp.where(keep, item[0:1], 1.0)
-            item_color = jnp.where(keep, item[1:4], 0.0)
-            color = jnp.where(early, color + trans * item_color, item_color + item_trans * color)
-            trans = trans * item_trans
-        return trans, color
-
-    low_trans, low_color = compose(True)
-    high_trans, high_color = compose(False)
-    front_trans = jnp.where(forward_ray, low_trans, high_trans)
-    front_color = jnp.where(forward_ray, low_color, high_color)
-    back_color = jnp.where(forward_ray, high_color, low_color)
+    slab = lax.axis_index("slab")
+    kept = kept_half(lax.axis_index("tile"), n_tile)
+
+    front_trans = back_trans = jnp.ones((1, rays), F32)
+    front_color = back_color = jnp.zeros((3, rays), F32)
+    for bit in range(n_bits):
+        behind = order_ref[bit] > 0
+        trans, color = pieces[bit][0:1], pieces[bit][1:4]
+        front_color = jnp.where(behind, front_color, color + trans * front_color)
+        front_trans = jnp.where(behind, front_trans, trans * front_trans)
+        back_color = jnp.where(behind, back_color + back_trans * color, back_color)
+        back_trans = jnp.where(behind, back_trans * trans, back_trans)
+    forward_ray = (order_ref[0] ^ (slab & 1)) > 0
     front_ref[...] = front_trans
     store = pltpu.make_async_copy(front_ref, front_hbm, sem)
     store.start()
-    own = every[0]
+    own = own_ref[...]
     own_trans = own[0:1]
     logits = front_color + front_trans * own[1:4] + (front_trans * own_trans) * back_color
     shade = jax.nn.sigmoid(logits)
@@ -207,8 +193,8 @@
         high = rows.astype(BF16).astype(F32)
         q16[:, j * rays : (j + 1) * rays] = jnp.concatenate([high, rows - high], axis=0).astype(BF16)
 
-    chunk = count // CHUNKS
-    for c in range(CHUNKS):
+    chunk = count // BACKWARD_CHUNKS
+    for c in range(BACKWARD_CHUNKS):
         rows = pl.ds(c * chunk, chunk)
         q = q16[:, rows]
         h1 = h1_ref[rows]
@@ -224,20 +210,20 @@
     half_mid = mid_ref.shape[0] // 2
     half_in = in_ref.shape[0] // 2
     rows_in = half_mid + half_in
-    for place, half in ((send_ref, 1 - core), (keep_ref, core)):
+    for place, half in ((send_ref, 1 - kept), (keep_ref, kept)):
         place[:half_mid] = mid_ref[pl.ds(pl.multiple_of(half * half_mid, half_mid), half_mid)]
         place[half_mid:rows_in] = in_ref[pl.ds(pl.multiple_of(half * half_in, half_in), half_in)]
         place[rows_in:] = out_ref[:8] + out_ref[8:]
     store.wait()
 
 
-def final_kernel(core_ref, own_ref, other_ref, head_ref, in_hbm, mid_hbm, out_hbm, out_ref, sems):
-    core = core_ref[0]
+def final_kernel(own_ref, other_ref, head_ref, in_hbm, mid_hbm, out_hbm, out_ref, sems, *, n_tile):
+    kept = kept_half(lax.axis_index("tile"), n_tile)
     half_mid = mid_hbm.shape[0] // 2
     half_in = in_hbm.shape[0] // 2
     rows_in = half_mid + half_in
     moves = []
-    for source, half in ((own_ref, core), (other_ref, 1 - core)):
+    for source, half in ((own_ref, kept), (other_ref, 1 - kept)):
         for start, size, place in ((0, half_mid, mid_hbm), (half_mid, half_in, in_hbm)):
             moves.append(
                 pltpu.make_async_copy(
@@ -262,6 +248,22 @@
         move.wait()
 
 
+def kept_half(tile, n_tile):
+    half = tile & 1
+    shift = 1
+    while (1 << shift) < n_tile:
+        half = half ^ ((tile >> shift) & 1)
+        shift += 1
+    return half
+
+
+def joined(own, got, own_first):
+    first = jnp.where(own_first, own, got)
+    second = jnp.where(own_first, got, own)
+    row = lax.broadcasted_iota(jnp.int32, own.shape, 0)
+    return first[0:1] * second + jnp.where(row == 0, 0.0, first)
+
+
 def pairs(size, bit):
     return [(i, i ^ bit) for i in range(size)]
 
@@ -276,25 +278,23 @@
         hidden = field_mid.shape[1]
         features = field_out.shape[2]
         count = samples * rays
-        slab = lax.axis_index("slab")
-        core = lax.axis_index("tile") % 2
+        n_bits = (n_slab - 1).bit_length()
         row = lambda a: a.reshape(1, rays)
-        ids = jnp.stack([slab, core]).astype(jnp.int32)
-        seg, *kept = pl.pallas_call(
+        seg, order, *kept = pl.pallas_call(
             forward_kernel,
             name="forward",
             out_shape=(
                 pltpu.VMEM((4, rays), F32),
+                pltpu.VMEM((n_bits, 1, rays), jnp.int32),
                 pltpu.VMEM((count, width), BF16),
                 pltpu.VMEM((count, hidden), BF16),
                 pltpu.VMEM((count, hidden), BF16),
                 pltpu.VMEM((6, samples, rays), F32),
                 pltpu.VMEM((16, hidden), BF16),
                 pltpu.VMEM((hidden, hidden), BF16),
-                pltpu.VMEM((1, rays), jnp.int32),
                 pltpu.VMEM((3, rays), F32),
             ),
-            in_specs=[SMEM] + [HBM] * 11,
+            in_specs=[HBM] * 11,
             out_specs=(VMEM,) * 9,
             scratch_shapes=[
                 pltpu.VMEM((width, hidden), BF16),
@@ -304,12 +304,12 @@
                 pltpu.VMEM((1, rays), jnp.int32),
                 pltpu.VMEM((1, rays), jnp.int32),
                 pltpu.VMEM((1, rays), jnp.int32),
+                pltpu.VMEM((1, rays), jnp.int32),
                 pltpu.VMEM((samples, 8, rays), F32),
-                pltpu.SemaphoreType.DMA((10 + CHUNKS,)),
+                pltpu.SemaphoreType.DMA((12,)),
             ],
             compiler_params=LIMIT,
         )(
-            ids,
             *(
                 pltpu.with_memory_space_constraint(a, pltpu.HBM)
                 for a in (
@@ -319,30 +319,27 @@
             ),
         )
 
-        known = seg[None]
-        pieces = [known]
-        bit = 1
-        while bit < n_slab:
-            got = lax.ppermute(known, "slab", pairs(n_slab, bit))
+        block = seg
+        pieces = []
+        for bit in range(n_bits):
+            got = lax.ppermute(block, "slab", pairs(n_slab, 1 << bit))
             pieces.append(got)
-            bit *= 2
-            if bit < n_slab:
-                known = jnp.concatenate([known, got], axis=0)
+            if bit + 1 < n_bits:
+                block = joined(block, got, order[bit] > 0)
 
         half = (hidden + width) // 2 + 8
         front, keep, send = pl.pallas_call(
-            functools.partial(backward_kernel, n_pieces=len(pieces), n_slab=n_slab),
+            functools.partial(backward_kernel, n_tile=n_tile),
             name="backward",
             out_shape=(
                 pltpu.HBM((1, rays), F32),
                 pltpu.VMEM((half, hidden), F32),
                 pltpu.VMEM((half, hidden), F32),
             ),
-            in_specs=[SMEM] + [VMEM] * (8 + len(pieces)),
+            in_specs=[VMEM] * (9 + n_bits),
             out_specs=(HBM, VMEM, VMEM),
             scratch_shapes=[
                 pltpu.VMEM((1, rays), F32),
-                pltpu.VMEM((n_slab, 4, rays), F32),
                 pltpu.VMEM((samples, 8, rays), F32),
                 pltpu.VMEM((16, count), BF16),
                 pltpu.VMEM((hidden, hidden), F32),
@@ -351,27 +348,27 @@
                 pltpu.SemaphoreType.DMA,
             ],
             compiler_params=LIMIT,
-        )(ids, *kept, *pieces)
+        )(seg, order, *kept, *pieces)
 
         part = keep + lax.ppermute(send, "tile", pairs(n_tile, 1))
         bit = 2
         while bit < n_tile:
-            part = part + lax.ppermute(part, "tile", pairs(n_tile, bit))
+            part = part + lax.ppermute(part, "tile", pairs(n_tile, bit | 1))
             bit *= 2
         other = lax.ppermute(part, "tile", pairs(n_tile, 1))
         grad_in, grad_mid, grad_out = pl.pallas_call(
-            final_kernel,
+            functools.partial(final_kernel, n_tile=n_tile),
             name="final",
             out_shape=(
                 pltpu.HBM((width, hidden), F32),
                 pltpu.HBM((hidden, hidden), F32),
                 pltpu.HBM((features, hidden), F32),
             ),
-            in_specs=[SMEM] + [VMEM] * 3,
+            in_specs=[VMEM] * 3,
             out_specs=(HBM,) * 3,
             scratch_shapes=[pltpu.VMEM((features, hidden), F32), pltpu.SemaphoreType.DMA((5,))],
             compiler_params=LIMIT,
-        )(core.reshape(1).astype(jnp.int32), part, other, color_head.T)
+        )(part, other, color_head.T)
         return front, grad_in[None], grad_mid[None], grad_out.T[None]
 
     return body

time: 37.7 us -> 35.1 us (0.931)
  Pallas kernels: 12.9 us -> 10.8 us
  waiting for transfers between devices: 13.5 us -> 13.1 us
    pallas_call x2, Pallas kernels: 7.03 us -> 5.84 us  [the longest x1 4.91 us: body(): pl.pallas_call(functools.partial(backward_kernel, n_tile=n_tile), name='b...]
    pallas_call x1, Pallas kernels: 5.91 us -> 4.99 us  [body(): pl.pallas_call(forward_kernel, name='forward', out_shape=(pltpu.VMEM((4,...]
where the time goes in v3:
time: 35.1 us; the launch traced here: 34.9 us
  waiting for transfers between devices  13.1 us (37%)
  Pallas kernels  10.8 us (31%)
  starting transfers between devices  10.1 us (29%)
  between operations  0.68 us (2%)
    ppermute x3, starting transfers between devices, body(): got = lax.ppermute(block, 'slab', pairs(n_slab, 1 << bit))  8.16 us
    ppermute x1, waiting for transfers between devices, body(): part = part + lax.ppermute(part, 'tile', pairs(n_tile, bit | 1))  5.48 us
    pallas_call x1, Pallas kernels, body(): pl.pallas_call(forward_kernel, name='forward', out_shape=(pltpu.VMEM((4,...  4.99 us
    pallas_call x1, Pallas kernels, body(): pl.pallas_call(functools.partial(backward_kernel, n_tile=n_tile), name='b...  4.91 us
    ppermute x3, waiting for transfers between devices, body(): got = lax.ppermute(block, 'slab', pairs(n_slab, 1 << bit))  4.86 us
    ppermute x1, starting transfers between devices, body(): part = part + lax.ppermute(part, 'tile', pairs(n_tile, bit | 1))  1.65 us
    ppermute x1, waiting for transfers between devices, body(): part = keep + lax.ppermute(send, 'tile', pairs(n_tile, 1))  1.44 us
    ppermute x1, waiting for transfers between devices, body(): other = lax.ppermute(part, 'tile', pairs(n_tile, 1))  1.32 us
  transfers between devices with their start and end apart: 6, of which 6 were waited for; matrix products, arithmetic and copies ran while one was open for 0% of the time, Pallas kernels for 0%

profile of v3, /device:TPU:0, one launch (start us, length us, event | category | flops | bytes accessed | tf_op | source)
XLA Modules:
  0.0 34.9 jit_solution(7726873200411209065)
XLA Ops:
  0.6 5.0 %forward.1 = (f32[4,512]{1,0:T(4,128)S(1)}, s32[3,1,512]{2,1,0:T(1,128)S(1)}, bf16[8192,128]{1,0:T(8,128)(2,1)S(1)}, bf16[8192,256]{1,0:T(8,128)(2,1)S(1)}, bf16...) custom-call(bf16[8192,128]{1,0:T(8,128)(2,1)} %bitcast.21, ...), custom_call_target="tpu_custom_call" | custom-call | tf_op jit(solution)/shard_map/forward/pallas_call | solution.py:283
  5.6 3.0 %collective-permute-start = (f32[4,512]{1,0:T(4,128)S(1)}, f32[4,512]{1,0:T(4,128)S(1)}, u32[]{:S(2)}, u32[]{:S(2)}) collective-permute-start(f32[4,512]{1,0:T(4,128)S(1)} %get-tuple-element.19.own_ref), channel_id=1, source_target_pairs={{0,4},{4,0},{8,12},{12,8},{16,20},{20,16},{24,28},{28,24},{1,5},{5... | collective-permute-start | bytes 24584 | tf_op jit(solution)/shard_map/ppermute | solution.py:325
  8.7 1.6 %collective-permute-done.refs_0_ = f32[4,512]{1,0:T(4,128)S(1)} collective-permute-done((f32[4,512]{1,0:T(4,128)S(1)}, f32[4,512]{1,0:T(4,128)S(1)}, u32[]{:S(2)}, u32[]{:S(2)}) %collective-permute-start) | collective-permute-done | bytes 8224 | tf_op jit(solution)/shard_map/ppermute | solution.py:325
  10.3 0.1 select_add_fusion.1
  10.4 2.1 %collective-permute-start.1 = (f32[4,512]{1,0:T(4,128)S(1)}, f32[4,512]{1,0:T(4,128)S(1)}, u32[]{:S(2)}, u32[]{:S(2)}) collective-permute-start(f32[4,512]{1,0:T(4,128)S(1)} %select_add_fusion.1), channel_id=1, source_target_pairs={{0,8},{4,12},{8,0},{12,4},{16,24},{20,28},{24,16},{28,20},{1,9},{5... | collective-permute-start | bytes 24584 | tf_op jit(solution)/shard_map/ppermute | solution.py:325
  12.5 1.6 %collective-permute-done.1.refs_1_ = f32[4,512]{1,0:T(4,128)S(1)} collective-permute-done((f32[4,512]{1,0:T(4,128)S(1)}, f32[4,512]{1,0:T(4,128)S(1)}, u32[]{:S(2)}, u32[]{:S(2)}) %collective-permute-start.1) | collective-permute-done | bytes 8224 | tf_op jit(solution)/shard_map/ppermute | solution.py:325
  14.1 0.1 select_add_fusion
  14.2 3.0 %collective-permute-start.2 = (f32[4,512]{1,0:T(4,128)S(1)}, f32[4,512]{1,0:T(4,128)S(1)}, u32[]{:S(2)}, u32[]{:S(2)}) collective-permute-start(f32[4,512]{1,0:T(4,128)S(1)} %select_add_fusion), channel_id=1, source_target_pairs={{0,16},{4,20},{8,24},{12,28},{16,0},{20,4},{24,8},{28,12},{1,17},{... | collective-permute-start | bytes 24584 | tf_op jit(solution)/shard_map/ppermute | solution.py:325
  17.2 1.6 %collective-permute-done.2.refs_2_ = f32[4,512]{1,0:T(4,128)S(1)} collective-permute-done((f32[4,512]{1,0:T(4,128)S(1)}, f32[4,512]{1,0:T(4,128)S(1)}, u32[]{:S(2)}, u32[]{:S(2)}) %collective-permute-start.2) | collective-permute-done | bytes 8224 | tf_op jit(solution)/shard_map/ppermute | solution.py:325
  18.9 0.0 copy-start
  18.9 4.9 %backward.1 = (f32[1,512]{1,0:T(1,128)}, f32[200,256]{1,0:T(8,128)S(1)}, f32[200,256]{1,0:T(8,128)S(1)}) custom-call(f32[4,512]{1,0:T(4,128)S(1)} %get-tuple-element.19.own_ref, s32[3,1,512]{2,1,0:T(1,128)S(1)} %get-tuple-element.20.order_ref, bf16[8192,128]{1,0:T(8,128)(2,1)S(1)} %get-tuple-element.21.x_ref, ...), custom_call_target="tpu_custom_call" | custom-call | tf_op jit(solution)/shard_map/backward/pallas_call | solution.py:331
  23.8 0.1 collective-permute-start.3
  23.9 1.4 %collective-permute-done.3 = f32[200,256]{1,0:T(8,128)S(1)} collective-permute-done((f32[200,256]{1,0:T(8,128)S(1)}, f32[200,256]{1,0:T(8,128)S(1)}, u32[]{:S(2)}, u32[]{:S(2)}) %collective-permute-start.3) | collective-permute-done | bytes 204832 | tf_op jit(solution)/shard_map/ppermute | solution.py:353
  25.3 1.6 %collective-permute-start.4 = (f32[200,256]{1,0:T(8,128)S(1)}, f32[200,256]{1,0:T(8,128)S(1)}, u32[]{:S(2)}, u32[]{:S(2)}) collective-permute-start(f32[200,256]{1,0:T(8,128)S(1)} %add.14), channel_id=1, source_target_pairs={{0,3},{1,2},{2,1},{3,0},{4,7},{5,6},{6,5},{7,4},{8,11},{9,10},{10,... | collective-permute-start | bytes 614408 | tf_op jit(solution)/shard_map/ppermute | solution.py:356
  27.0 5.5 %collective-permute-done.4 = f32[200,256]{1,0:T(8,128)S(1)} collective-permute-done((f32[200,256]{1,0:T(8,128)S(1)}, f32[200,256]{1,0:T(8,128)S(1)}, u32[]{:S(2)}, u32[]{:S(2)}) %collective-permute-start.4) | collective-permute-done | bytes 204832 | tf_op jit(solution)/shard_map/ppermute | solution.py:356
  32.5 0.2 collective-permute-start.5
  32.7 1.3 %collective-permute-done.5.other_ref = f32[200,256]{1,0:T(8,128)S(1)} collective-permute-done((f32[200,256]{1,0:T(8,128)S(1)}, f32[200,256]{1,0:T(8,128)S(1)}, u32[]{:S(2)}, u32[]{:S(2)}) %collective-permute-start.5) | collective-permute-done | bytes 204832 | tf_op jit(solution)/shard_map/ppermute | solution.py:358
  34.0 0.0 copy-done
  34.0 0.9 %final.1 = (f32[128,256]{1,0:T(8,128)}, f32[256,256]{1,0:T(8,128)}, f32[64,256]{1,0:T(8,128)}) custom-call(f32[200,256]{1,0:T(8,128)S(1)} %add.15.own_ref, f32[200,256]{1,0:T(8,128)S(1)} %collective-permute-done.5.other_ref, f32[3,64]{1,0:T(4,128)S(1)} %bitcast.20), custom_call_target="tpu_custom_call" | custom-call | tf_op jit(solution)/shard_map/final/pallas_call | solution.py:359
  (8 shorter events, 0.1 us)
Async XLA Ops:
  5.6 4.6 %collective-permute-start = (f32[4,512]{1,0:T(4,128)S(1)}, f32[4,512]{1,0:T(4,128)S(1)}, u32[]{:S(2)}, u32[]{:S(2)}) collective-permute-start(f32[4,512]{1,0:T(4,128)S(1)} %get-tuple-element.19.own_ref), channel_id=1, source_target_pairs={{0,4},{4,0},{8,12},{12,8},{16,20},{20,16},{24,28},{28,24},{1,5},{5... | collective-permute-start | bytes 24584 | tf_op jit(solution)/shard_map/ppermute | solution.py:325
  10.4 3.7 %collective-permute-start.1 = (f32[4,512]{1,0:T(4,128)S(1)}, f32[4,512]{1,0:T(4,128)S(1)}, u32[]{:S(2)}, u32[]{:S(2)}) collective-permute-start(f32[4,512]{1,0:T(4,128)S(1)} %select_add_fusion.1), channel_id=1, source_target_pairs={{0,8},{4,12},{8,0},{12,4},{16,24},{20,28},{24,16},{28,20},{1,9},{5... | collective-permute-start | bytes 24584 | tf_op jit(solution)/shard_map/ppermute | solution.py:325
  14.2 4.7 %collective-permute-start.2 = (f32[4,512]{1,0:T(4,128)S(1)}, f32[4,512]{1,0:T(4,128)S(1)}, u32[]{:S(2)}, u32[]{:S(2)}) collective-permute-start(f32[4,512]{1,0:T(4,128)S(1)} %select_add_fusion), channel_id=1, source_target_pairs={{0,16},{4,20},{8,24},{12,28},{16,0},{20,4},{24,8},{28,12},{1,17},{... | collective-permute-start | bytes 24584 | tf_op jit(solution)/shard_map/ppermute | solution.py:325
  18.9 15.2 %copy-start = (f32[64,3]{0,1:T(4,128)S(1)}, f32[64,3]{0,1:T(4,128)}, u32[]{:S(2)}) copy-start(f32[64,3]{0,1:T(4,128)} %param.20) | copy-start | bytes 2308
  23.8 1.5 %collective-permute-start.3 = (f32[200,256]{1,0:T(8,128)S(1)}, f32[200,256]{1,0:T(8,128)S(1)}, u32[]{:S(2)}, u32[]{:S(2)}) collective-permute-start(f32[200,256]{1,0:T(8,128)S(1)} %get-tuple-element.30), channel_id=1, source_target_pairs={{0,1},{1,0},{2,3},{3,2},{4,5},{5,4},{6,7},{7,6},{8,9},{9,8},{10,11... | collective-permute-start | bytes 614408 | tf_op jit(solution)/shard_map/ppermute | solution.py:353
  25.3 7.1 %collective-permute-start.4 = (f32[200,256]{1,0:T(8,128)S(1)}, f32[200,256]{1,0:T(8,128)S(1)}, u32[]{:S(2)}, u32[]{:S(2)}) collective-permute-start(f32[200,256]{1,0:T(8,128)S(1)} %add.14), channel_id=1, source_target_pairs={{0,3},{1,2},{2,1},{3,0},{4,7},{5,6},{6,5},{7,4},{8,11},{9,10},{10,... | collective-permute-start | bytes 614408 | tf_op jit(solution)/shard_map/ppermute | solution.py:356
  32.5 1.5 %collective-permute-start.5 = (f32[200,256]{1,0:T(8,128)S(1)}, f32[200,256]{1,0:T(8,128)S(1)}, u32[]{:S(2)}, u32[]{:S(2)}) collective-permute-start(f32[200,256]{1,0:T(8,128)S(1)} %add.15.own_ref), channel_id=1, source_target_pairs={{0,1},{1,0},{2,3},{3,2},{4,5},{5,4},{6,7},{7,6},{8,9},{9,8},{10,11... | collective-permute-start | bytes 614408 | tf_op jit(solution)/shard_map/ppermute | solution.py:358

commit v4 on v3

--- a/solution.py
+++ b/solution.py
@@ -14,6 +14,8 @@
 LIMIT = pltpu.CompilerParams(vmem_limit_bytes=32 * 1024 * 1024)
 FORWARD_CHUNKS = 4
 BACKWARD_CHUNKS = 8
+INNER_CHUNKS = 8
+FIRST_CHUNKS = 8
 
 
 def dot_nn(a, b):
@@ -91,17 +93,16 @@
         pltpu.make_async_copy(x_hbm.at[pl.ds(at, size)], x_ref.at[pl.ds(at, size)], sems.at[len(moves) + i])
         for i, (at, size) in enumerate(((0, chunk), (chunk, count - chunk)))
     ]
-    for move in moves[:3] + loads[:1] + moves[3:4] + loads[1:] + moves[4:]:
+    for move in moves[2:3] + loads[:1] + moves[3:4] + moves[:2] + loads[1:] + moves[4:]:
         move.start()
-    moves[0].wait()
-    moves[1].wait()
+    for move in moves[:4] + loads[:1]:
+        move.wait()
     w16_ref[...] = projection(head_ref[...], w3_ref[...])
-    moves[2].wait()
-    moves[3].wait()
 
     for c in range(FORWARD_CHUNKS):
-        if c < 2:
-            loads[c].wait()
+        if c == 1:
+            for move in moves[4:] + loads[1:]:
+                move.wait()
         rows = pl.ds(c * chunk, chunk)
         h1 = positive(dot_nn(x_ref[rows], w1_ref[...]))
         h1_ref[rows] = h1
@@ -112,8 +113,6 @@
         for j in range(each):
             out8[c * each + j] = eight[:, j * rays : (j + 1) * rays]
 
-    for move in moves[4:]:
-        move.wait()
     slab = lax.axis_index("slab")
     reverse = jnp.minimum(jnp.maximum(direction_ref[...], 0), 1)
     for bit in range(order_ref.shape[0]):
@@ -143,13 +142,13 @@
 
 
 def backward_kernel(
-    own_ref, order_ref, x_ref, h1_ref, h2_ref, save_ref, w16_ref, w2_ref, target_ref, *refs, n_tile,
+    own_ref, order_ref, h1_ref, h2_ref, save_ref, w16_ref, target_ref, *refs, n_tile,
 ):
     n_bits = order_ref.shape[0]
     pieces = refs[:n_bits]
-    front_hbm, keep_ref, send_ref, front_ref, q8, q16, mid_ref, in_ref, out_ref, sem = refs[n_bits:]
+    front_hbm, keep_ref, send_ref, back_ref, q16, front_ref, q8, mid_ref, sem = refs[n_bits:]
     samples, _, rays = q8.shape
-    count = x_ref.shape[0]
+    count = h1_ref.shape[0]
     slab = lax.axis_index("slab")
     kept = kept_half(lax.axis_index("tile"), n_tile)
 
@@ -196,45 +195,44 @@
     chunk = count // BACKWARD_CHUNKS
     for c in range(BACKWARD_CHUNKS):
         rows = pl.ds(c * chunk, chunk)
-        q = q16[:, rows]
-        h1 = h1_ref[rows]
-        h2 = h2_ref[rows]
-        back_two = where_positive(h2, dot_tn(q, w16_ref[...]))
-        grad_out = dot_nn(q, h2)
-        grad_mid = dot_tn(h1, back_two)
-        back_one = where_positive(h1, dot_nt(back_two, w2_ref[...]))
-        grad_in = dot_tn(x_ref[rows], back_one)
-        for ref, part in ((out_ref, grad_out), (mid_ref, grad_mid), (in_ref, grad_in)):
+        back_two = where_positive(h2_ref[rows], dot_tn(q16[:, rows], w16_ref[...]))
+        back_ref[rows] = back_two
+        grad_mid = dot_tn(h1_ref[rows], back_two)
+        mid_ref[...] = grad_mid if c == 0 else mid_ref[...] + grad_mid
+
+    half = mid_ref.shape[0] // 2
+    for place, which in ((send_ref, 1 - kept), (keep_ref, kept)):
+        place[...] = mid_ref[pl.ds(pl.multiple_of(which * half, half), half)]
+    store.wait()
+
+
+def inner_kernel(h1_ref, w2_ref, back_ref, one_ref):
+    count = h1_ref.shape[0]
+    chunk = count // INNER_CHUNKS
+    for c in range(INNER_CHUNKS):
+        rows = pl.ds(c * chunk, chunk)
+        one_ref[rows] = where_positive(h1_ref[rows], dot_nt(back_ref[rows], w2_ref[...]))
+
+
+def first_kernel(x_ref, one_ref, h2_ref, q16, keep_ref, send_ref, in_ref, out_ref, *, n_tile):
+    kept = kept_half(lax.axis_index("tile"), n_tile)
+    count = x_ref.shape[0]
+    chunk = count // FIRST_CHUNKS
+    for c in range(FIRST_CHUNKS):
+        rows = pl.ds(c * chunk, chunk)
+        grad_in = dot_tn(x_ref[rows], one_ref[rows])
+        grad_out = dot_nn(q16[:, rows], h2_ref[rows])
+        for ref, part in ((out_ref, grad_out), (in_ref, grad_in)):
             ref[...] = part if c == 0 else ref[...] + part
 
-    half_mid = mid_ref.shape[0] // 2
-    half_in = in_ref.shape[0] // 2
-    rows_in = half_mid + half_in
-    for place, half in ((send_ref, 1 - kept), (keep_ref, kept)):
-        place[:half_mid] = mid_ref[pl.ds(pl.multiple_of(half * half_mid, half_mid), half_mid)]
-        place[half_mid:rows_in] = in_ref[pl.ds(pl.multiple_of(half * half_in, half_in), half_in)]
-        place[rows_in:] = out_ref[:8] + out_ref[8:]
-    store.wait()
-
-
-def final_kernel(own_ref, other_ref, head_ref, in_hbm, mid_hbm, out_hbm, out_ref, sems, *, n_tile):
-    kept = kept_half(lax.axis_index("tile"), n_tile)
-    half_mid = mid_hbm.shape[0] // 2
-    half_in = in_hbm.shape[0] // 2
-    rows_in = half_mid + half_in
-    moves = []
-    for source, half in ((own_ref, kept), (other_ref, 1 - kept)):
-        for start, size, place in ((0, half_mid, mid_hbm), (half_mid, half_in, in_hbm)):
-            moves.append(
-                pltpu.make_async_copy(
-                    source.at[pl.ds(start, size)],
-                    place.at[pl.ds(pl.multiple_of(half * size, size), size)],
-                    sems.at[len(moves)],
-                )
-            )
-    for move in moves:
-        move.start()
-    factors = own_ref[rows_in:]
+    half = in_ref.shape[0] // 2
+    for place, which in ((send_ref, 1 - kept), (keep_ref, kept)):
+        place[:half] = in_ref[pl.ds(pl.multiple_of(which * half, half), half)]
+        place[half:] = out_ref[:8] + out_ref[8:]
+
+
+def expand_kernel(factors_ref, head_ref, out_ref):
+    factors = factors_ref[factors_ref.shape[0] - 8 :]
     head = head_ref[...]
     width = head.shape[1]
     first = jnp.where(lax.broadcasted_iota(jnp.int32, (1, width), 1) == 0, 1.0, 0.0)
@@ -242,8 +240,29 @@
     out_ref[...] = lax.dot_general(
         rows, factors, (((0,), (0,)), ((), ())), preferred_element_type=F32, precision=lax.Precision.HIGHEST
     )
+
+
+def final_kernel(own_mid, other_mid, own_in, other_in, out_ref, in_hbm, mid_hbm, out_hbm, sems, *, n_tile):
+    kept = kept_half(lax.axis_index("tile"), n_tile)
+    half_mid = mid_hbm.shape[0] // 2
+    half_in = in_hbm.shape[0] // 2
+    moves = []
+    for source, place, size, half in (
+        (own_mid, mid_hbm, half_mid, kept),
+        (other_mid, mid_hbm, half_mid, 1 - kept),
+        (own_in, in_hbm, half_in, kept),
+        (other_in, in_hbm, half_in, 1 - kept),
+    ):
+        moves.append(
+            pltpu.make_async_copy(
+                source.at[pl.ds(0, size)],
+                place.at[pl.ds(pl.multiple_of(half * size, size), size)],
+                sems.at[len(moves)],
+            )
+        )
     moves.append(pltpu.make_async_copy(out_ref, out_hbm, sems.at[len(moves)]))
-    moves[-1].start()
+    for move in moves:
+        move.start()
     for move in moves:
         move.wait()
 
@@ -327,35 +346,73 @@
             if bit + 1 < n_bits:
                 block = joined(block, got, order[bit] > 0)
 
-        half = (hidden + width) // 2 + 8
-        front, keep, send = pl.pallas_call(
+        x, h1, h2, save, w16, w2, target_rows = kept
+        half_mid, half_in = hidden // 2, width // 2 + 8
+        front, keep_mid, send_mid, back, factors = pl.pallas_call(
             functools.partial(backward_kernel, n_tile=n_tile),
             name="backward",
             out_shape=(
                 pltpu.HBM((1, rays), F32),
-                pltpu.VMEM((half, hidden), F32),
-                pltpu.VMEM((half, hidden), F32),
+                pltpu.VMEM((half_mid, hidden), F32),
+                pltpu.VMEM((half_mid, hidden), F32),
+                pltpu.VMEM((count, hidden), BF16),
+                pltpu.VMEM((16, count), BF16),
             ),
-            in_specs=[VMEM] * (9 + n_bits),
-            out_specs=(HBM, VMEM, VMEM),
+            in_specs=[VMEM] * (7 + n_bits),
+            out_specs=(HBM, VMEM, VMEM, VMEM, VMEM),
             scratch_shapes=[
                 pltpu.VMEM((1, rays), F32),
                 pltpu.VMEM((samples, 8, rays), F32),
-                pltpu.VMEM((16, count), BF16),
                 pltpu.VMEM((hidden, hidden), F32),
-                pltpu.VMEM((width, hidden), F32),
-                pltpu.VMEM((16, hidden), F32),
                 pltpu.SemaphoreType.DMA,
             ],
             compiler_params=LIMIT,
-        )(seg, order, *kept, *pieces)
-
-        part = keep + lax.ppermute(send, "tile", pairs(n_tile, 1))
-        bit = 2
-        while bit < n_tile:
-            part = part + lax.ppermute(part, "tile", pairs(n_tile, bit | 1))
-            bit *= 2
-        other = lax.ppermute(part, "tile", pairs(n_tile, 1))
+            cost_estimate=pl.CostEstimate(flops=4 * count * hidden * hidden, bytes_accessed=0, transcendentals=0),
+        )(seg, order, h1, h2, save, w16, target_rows, *pieces)
+        back_one = pl.pallas_call(
+            inner_kernel,
+            name="inner",
+            out_shape=pltpu.VMEM((count, hidden), BF16),
+            in_specs=[VMEM] * 3,
+            out_specs=VMEM,
+            compiler_params=LIMIT,
+            cost_estimate=pl.CostEstimate(flops=2 * count * hidden * hidden, bytes_accessed=0, transcendentals=0),
+        )(h1, w2, back)
+
+        def chip_sum(keep, send):
+            return keep + lax.ppermute(send, "tile", pairs(n_tile, 1))
+
+        def tile_sum(part):
+            bit = 2
+            while bit < n_tile:
+                part = part + lax.ppermute(part, "tile", pairs(n_tile, bit | 1))
+                bit *= 2
+            return part, lax.ppermute(part, "tile", pairs(n_tile, 1))
+
+        part_mid = chip_sum(keep_mid, send_mid)
+        keep_in, send_in = pl.pallas_call(
+            functools.partial(first_kernel, n_tile=n_tile),
+            name="first",
+            out_shape=(pltpu.VMEM((half_in, hidden), F32), pltpu.VMEM((half_in, hidden), F32)),
+            in_specs=[VMEM] * 4,
+            out_specs=(VMEM, VMEM),
+            scratch_shapes=[pltpu.VMEM((width, hidden), F32), pltpu.VMEM((16, hidden), F32)],
+            compiler_params=LIMIT,
+            cost_estimate=pl.CostEstimate(flops=4 * count * hidden * hidden, bytes_accessed=0, transcendentals=0),
+        )(x, back_one, h2, factors)
+
+        part_mid, keep_in, send_in = lax.optimization_barrier((part_mid, keep_in, send_in))
+        own_mid, other_mid = tile_sum(part_mid)
+        own_in, other_in = tile_sum(chip_sum(keep_in, send_in))
+        expanded = pl.pallas_call(
+            expand_kernel,
+            name="expand",
+            out_shape=pltpu.VMEM((features, hidden), F32),
+            in_specs=[VMEM] * 2,
+            out_specs=VMEM,
+            compiler_params=LIMIT,
+            cost_estimate=pl.CostEstimate(flops=2 * 8 * features * hidden * 6, bytes_accessed=0, transcendentals=0),
+        )(own_in, color_head.T)
         grad_in, grad_mid, grad_out = pl.pallas_call(
             functools.partial(final_kernel, n_tile=n_tile),
             name="final",
@@ -364,11 +421,11 @@
                 pltpu.HBM((hidden, hidden), F32),
                 pltpu.HBM((features, hidden), F32),
             ),
-            in_specs=[VMEM] * 3,
+            in_specs=[VMEM] * 5,
             out_specs=(HBM,) * 3,
-            scratch_shapes=[pltpu.VMEM((features, hidden), F32), pltpu.SemaphoreType.DMA((5,))],
-            compiler_params=LIMIT,
-        )(part, other, color_head.T)
+            scratch_shapes=[pltpu.SemaphoreType.DMA((5,))],
+            compiler_params=LIMIT,
+        )(own_mid, other_mid, own_in, other_in, expanded)
         return front, grad_in[None], grad_mid[None], grad_out.T[None]
 
     return body

time: 35.1 us -> 34.6 us (0.986)
  waiting for transfers between devices: 13.1 us -> 11 us
  Pallas kernels: 10.8 us -> 11.7 us
  starting transfers between devices: 10.1 us -> 10.7 us
    pallas_call x0 -> x3, Pallas kernels: none -> 2.91 us  [the longest x1 1.36 us: body(): pl.pallas_call(functools.partial(first_kernel, n_tile=n_tile), name='firs...]
    ppermute x3 -> x6, waiting for transfers between devices: 8.24 us -> 6.11 us  [the longest x2 4.03 us: tile_sum(): part = part + lax.ppermute(part, 'tile', pairs(n_tile, bit | 1))]
    pallas_call x1, Pallas kernels: 4.91 us -> 3.12 us  [body(): pl.pallas_call(functools.partial(backward_kernel, n_tile=n_tile), name='b...]
    ppermute x3 -> x6, starting transfers between devices: 1.92 us -> 2.58 us  [the longest x2 2.16 us: tile_sum(): part = part + lax.ppermute(part, 'tile', pairs(n_tile, bit | 1))]
  transfers between devices with their start and end apart: 6 -> 9, of which waited for: 6 -> 7; matrix products, arithmetic and copies ran while one was open for 0% -> 0% of each run, Pallas kernels for 0% -> 8%
where the time goes in v4:
time: 34.6 us; the launch traced here: 34.4 us
  Pallas kernels  11.7 us (34%)
  waiting for transfers between devices  11 us (32%)
  starting transfers between devices  10.7 us (31%)
  between operations  0.73 us (2%)
    ppermute x3, starting transfers between devices, body(): got = lax.ppermute(block, 'slab', pairs(n_slab, 1 << bit))  8.16 us
    pallas_call x1, Pallas kernels, body(): pl.pallas_call(forward_kernel, name='forward', out_shape=(pltpu.VMEM((4,...  4.88 us
    ppermute x3, waiting for transfers between devices, body(): got = lax.ppermute(block, 'slab', pairs(n_slab, 1 << bit))  4.86 us
    ppermute x2, waiting for transfers between devices, tile_sum(): part = part + lax.ppermute(part, 'tile', pairs(n_tile, bit | 1))  4.03 us
    pallas_call x1, Pallas kernels, body(): pl.pallas_call(functools.partial(backward_kernel, n_tile=n_tile), name='b...  3.12 us
    ppermute x2, starting transfers between devices, tile_sum(): part = part + lax.ppermute(part, 'tile', pairs(n_tile, bit | 1))  2.16 us
    pallas_call x1, Pallas kernels, body(): pl.pallas_call(functools.partial(first_kernel, n_tile=n_tile), name='firs...  1.36 us
    pallas_call x1, Pallas kernels, body(): pl.pallas_call(inner_kernel, name='inner', out_shape=pltpu.VMEM((count, h...  1.29 us
  transfers between devices with their start and end apart: 9, of which 7 were waited for; matrix products, arithmetic and copies ran while one was open for 0% of the time, Pallas kernels for 8%

profile of v4, /device:TPU:0, one launch (start us, length us, event | category | flops | bytes accessed | tf_op | source)
XLA Modules:
  0.0 34.4 jit_solution(7899241146009609936)
XLA Ops:
  0.6 4.9 %forward.1 = (f32[4,512]{1,0:T(4,128)S(1)}, s32[3,1,512]{2,1,0:T(1,128)S(1)}, bf16[8192,128]{1,0:T(8,128)(2,1)S(1)}, bf16[8192,256]{1,0:T(8,128)(2,1)S(1)}, bf16...) custom-call(bf16[8192,128]{1,0:T(8,128)(2,1)} %bitcast.21, ...), custom_call_target="tpu_custom_call" | custom-call | tf_op jit(solution)/shard_map/forward/pallas_call | solution.py:302
  5.5 3.0 %collective-permute-start = (f32[4,512]{1,0:T(4,128)S(1)}, f32[4,512]{1,0:T(4,128)S(1)}, u32[]{:S(2)}, u32[]{:S(2)}) collective-permute-start(f32[4,512]{1,0:T(4,128)S(1)} %get-tuple-element.26.own_ref), channel_id=1, source_target_pairs={{0,4},{4,0},{8,12},{12,8},{16,20},{20,16},{24,28},{28,24},{1,5},{5... | collective-permute-start | bytes 24584 | tf_op jit(solution)/shard_map/ppermute | solution.py:344
  8.6 1.6 %collective-permute-done.refs_0_ = f32[4,512]{1,0:T(4,128)S(1)} collective-permute-done((f32[4,512]{1,0:T(4,128)S(1)}, f32[4,512]{1,0:T(4,128)S(1)}, u32[]{:S(2)}, u32[]{:S(2)}) %collective-permute-start) | collective-permute-done | bytes 8224 | tf_op jit(solution)/shard_map/ppermute | solution.py:344
  10.2 0.1 select_add_fusion.1
  10.2 2.1 %collective-permute-start.1 = (f32[4,512]{1,0:T(4,128)S(1)}, f32[4,512]{1,0:T(4,128)S(1)}, u32[]{:S(2)}, u32[]{:S(2)}) collective-permute-start(f32[4,512]{1,0:T(4,128)S(1)} %select_add_fusion.1), channel_id=1, source_target_pairs={{0,8},{4,12},{8,0},{12,4},{16,24},{20,28},{24,16},{28,20},{1,9},{5... | collective-permute-start | bytes 24584 | tf_op jit(solution)/shard_map/ppermute | solution.py:344
  12.4 1.6 %collective-permute-done.1.refs_1_ = f32[4,512]{1,0:T(4,128)S(1)} collective-permute-done((f32[4,512]{1,0:T(4,128)S(1)}, f32[4,512]{1,0:T(4,128)S(1)}, u32[]{:S(2)}, u32[]{:S(2)}) %collective-permute-start.1) | collective-permute-done | bytes 8224 | tf_op jit(solution)/shard_map/ppermute | solution.py:344
  14.0 0.1 select_add_fusion
  14.1 3.0 %collective-permute-start.2 = (f32[4,512]{1,0:T(4,128)S(1)}, f32[4,512]{1,0:T(4,128)S(1)}, u32[]{:S(2)}, u32[]{:S(2)}) collective-permute-start(f32[4,512]{1,0:T(4,128)S(1)} %select_add_fusion), channel_id=1, source_target_pairs={{0,16},{4,20},{8,24},{12,28},{16,0},{20,4},{24,8},{28,12},{1,17},{... | collective-permute-start | bytes 24584 | tf_op jit(solution)/shard_map/ppermute | solution.py:344
  17.1 1.6 %collective-permute-done.2.refs_2_ = f32[4,512]{1,0:T(4,128)S(1)} collective-permute-done((f32[4,512]{1,0:T(4,128)S(1)}, f32[4,512]{1,0:T(4,128)S(1)}, u32[]{:S(2)}, u32[]{:S(2)}) %collective-permute-start.2) | collective-permute-done | bytes 8224 | tf_op jit(solution)/shard_map/ppermute | solution.py:344
  18.7 3.1 %backward.1 = (f32[1,512]{1,0:T(1,128)}, f32[128,256]{1,0:T(8,128)S(1)}, f32[128,256]{1,0:T(8,128)S(1)}, bf16[8192,256]{1,0:T(8,128)(2,1)S(1)}, bf16[16,8192]{1,0:T(8,128)(2,1)S(1)}) custom-call(f32[4,512]{1,0:T(4,128)S(1)} %get-tuple-element.26.own_ref, s32[3,1,512]{2,1,0:T(1,128)S(1)} %get-tuple-element.27.order_ref, ...), custom_call_target="tpu_custom_call" | custom-call | flops 2147483648 | tf_op jit(solution)/shard_map/backward/pallas_call | solution.py:351
  21.9 0.1 collective-permute-start.3
  21.9 1.3 %inner.1.one_ref = bf16[8192,256]{1,0:T(8,128)(2,1)S(1)} custom-call(bf16[8192,256]{1,0:T(8,128)(2,1)S(1)} %get-tuple-element.28.h1_ref, bf16[256,256]{1,0:T(8,128)(2,1)S(1)} %get-tuple-element.37.w2_ref, bf16[8192,256]{1,0:T(8,128)(2,1)S(1)} %get-tuple-element.38.back_ref), custom_call_target="tpu_custom_call" | custom-call | flops 1073741824 | tf_op jit(solution)/shard_map/inner/pallas_call | solution.py:372
  23.3 0.0 copy-start
  23.3 1.4 %first.1 = (f32[72,256]{1,0:T(8,128)S(1)}, f32[72,256]{1,0:T(8,128)S(1)}) custom-call(bf16[8192,128]{1,0:T(8,128)(2,1)S(1)} %get-tuple-element.36.x_ref, bf16[8192,256]{1,0:T(8,128)(2,1)S(1)} %inner.1.one_ref, bf16[8192,256]{1,0:T(8,128)(2,1)S(1)} %get-tuple-element.29.h2_ref, bf16[16,8192]{1,0:T(8,128)(2,1)S(1)} %get-tuple-element.39.q16), custom_call_target="tpu_custom_call" | custom-call | flops 2147483648 | tf_op jit(solution)/shard_map/first/pallas_call | solution.py:393
  24.6 0.0 collective-permute-done.3
  24.7 2.0 %collective-permute-start.4 = (f32[128,256]{1,0:T(8,128)S(1)}, f32[128,256]{1,0:T(8,128)S(1)}, u32[]{:S(2)}, u32[]{:S(2)}) collective-permute-start(f32[128,256]{1,0:T(8,128)S(1)} %add.20), channel_id=1, source_target_pairs={{0,3},{1,2},{2,1},{3,0},{4,7},{5,6},{6,5},{7,4},{8,11},{9,10},{10,... | collective-permute-start | bytes 393224 | tf_op jit(solution)/shard_map/ppermute | solution.py:388
  26.7 0.0 collective-permute-start.6
  26.7 1.2 %collective-permute-done.6 = f32[72,256]{1,0:T(8,128)S(1)} collective-permute-done((f32[72,256]{1,0:T(8,128)S(1)}, f32[72,256]{1,0:T(8,128)S(1)}, u32[]{:S(2)}, u32[]{:S(2)}) %collective-permute-start.6) | collective-permute-done | bytes 73760 | tf_op jit(solution)/shard_map/ppermute | solution.py:383
  28.0 0.1 collective-permute-start.7
  28.1 2.4 %collective-permute-done.4 = f32[128,256]{1,0:T(8,128)S(1)} collective-permute-done((f32[128,256]{1,0:T(8,128)S(1)}, f32[128,256]{1,0:T(8,128)S(1)}, u32[]{:S(2)}, u32[]{:S(2)}) %collective-permute-start.4) | collective-permute-done | bytes 131104 | tf_op jit(solution)/shard_map/ppermute | solution.py:388
  30.5 0.1 collective-permute-start.5
  30.6 1.6 %collective-permute-done.7 = f32[72,256]{1,0:T(8,128)S(1)} collective-permute-done((f32[72,256]{1,0:T(8,128)S(1)}, f32[72,256]{1,0:T(8,128)S(1)}, u32[]{:S(2)}, u32[]{:S(2)}) %collective-permute-start.7) | collective-permute-done | bytes 73760 | tf_op jit(solution)/shard_map/ppermute | solution.py:388
  32.3 0.2 collective-permute-start.8
  32.5 0.0 copy-done
  32.5 0.3 expand.1.out_ref
  32.8 0.8 %collective-permute-done.8.other_in = f32[72,256]{1,0:T(8,128)S(1)} collective-permute-done((f32[72,256]{1,0:T(8,128)S(1)}, f32[72,256]{1,0:T(8,128)S(1)}, u32[]{:S(2)}, u32[]{:S(2)}) %collective-permute-start.8) | collective-permute-done | bytes 73760 | tf_op jit(solution)/shard_map/ppermute | solution.py:390
  33.6 0.0 collective-permute-done.5.other_mid
  33.6 0.8 %final.1 = (f32[128,256]{1,0:T(8,128)}, f32[256,256]{1,0:T(8,128)}, f32[64,256]{1,0:T(8,128)}) custom-call(f32[128,256]{1,0:T(8,128)S(1)} %add.21.own_mid, f32[128,256]{1,0:T(8,128)S(1)} %collective-permute-done.5.other_mid, f32[72,256]{1,0:T(8,128)S(1)} %add.23.factors_ref.own_in, f32[72,256]{1,0:T(8,128)S(1)} %collective-permute-done.8.other_in, ...), custom_call_target="tpu_custom_call" | custom-call | tf_op jit(solution)/shard_map/final/pallas_call | solution.py:416
  (10 shorter events, 0.1 us)
Async XLA Ops:
  5.5 4.6 %collective-permute-start = (f32[4,512]{1,0:T(4,128)S(1)}, f32[4,512]{1,0:T(4,128)S(1)}, u32[]{:S(2)}, u32[]{:S(2)}) collective-permute-start(f32[4,512]{1,0:T(4,128)S(1)} %get-tuple-element.26.own_ref), channel_id=1, source_target_pairs={{0,4},{4,0},{8,12},{12,8},{16,20},{20,16},{24,28},{28,24},{1,5},{5... | collective-permute-start | bytes 24584 | tf_op jit(solution)/shard_map/ppermute | solution.py:344
  10.2 3.7 %collective-permute-start.1 = (f32[4,512]{1,0:T(4,128)S(1)}, f32[4,512]{1,0:T(4,128)S(1)}, u32[]{:S(2)}, u32[]{:S(2)}) collective-permute-start(f32[4,512]{1,0:T(4,128)S(1)} %select_add_fusion.1), channel_id=1, source_target_pairs={{0,8},{4,12},{8,0},{12,4},{16,24},{20,28},{24,16},{28,20},{1,9},{5... | collective-permute-start | bytes 24584 | tf_op jit(solution)/shard_map/ppermute | solution.py:344
  14.1 4.7 %collective-permute-start.2 = (f32[4,512]{1,0:T(4,128)S(1)}, f32[4,512]{1,0:T(4,128)S(1)}, u32[]{:S(2)}, u32[]{:S(2)}) collective-permute-start(f32[4,512]{1,0:T(4,128)S(1)} %select_add_fusion), channel_id=1, source_target_pairs={{0,16},{4,20},{8,24},{12,28},{16,0},{20,4},{24,8},{28,12},{1,17},{... | collective-permute-start | bytes 24584 | tf_op jit(solution)/shard_map/ppermute | solution.py:344
  21.9 2.8 %collective-permute-start.3 = (f32[128,256]{1,0:T(8,128)S(1)}, f32[128,256]{1,0:T(8,128)S(1)}, u32[]{:S(2)}, u32[]{:S(2)}) collective-permute-start(f32[128,256]{1,0:T(8,128)S(1)} %get-tuple-element.35), channel_id=1, source_target_pairs={{0,1},{1,0},{2,3},{3,2},{4,5},{5,4},{6,7},{7,6},{8,9},{9,8},{10,11... | collective-permute-start | bytes 393224 | tf_op jit(solution)/shard_map/ppermute | solution.py:383
  23.3 9.2 %copy-start = (f32[64,3]{0,1:T(4,128)S(1)}, f32[64,3]{0,1:T(4,128)}, u32[]{:S(2)}) copy-start(f32[64,3]{0,1:T(4,128)} %param.20) | copy-start | bytes 2308
  24.7 5.9 %collective-permute-start.4 = (f32[128,256]{1,0:T(8,128)S(1)}, f32[128,256]{1,0:T(8,128)S(1)}, u32[]{:S(2)}, u32[]{:S(2)}) collective-permute-start(f32[128,256]{1,0:T(8,128)S(1)} %add.20), channel_id=1, source_target_pairs={{0,3},{1,2},{2,1},{3,0},{4,7},{5,6},{6,5},{7,4},{8,11},{9,10},{10,... | collective-permute-start | bytes 393224 | tf_op jit(solution)/shard_map/ppermute | solution.py:388
  26.7 1.3 %collective-permute-start.6 = (f32[72,256]{1,0:T(8,128)S(1)}, f32[72,256]{1,0:T(8,128)S(1)}, u32[]{:S(2)}, u32[]{:S(2)}) collective-permute-start(f32[72,256]{1,0:T(8,128)S(1)} %get-tuple-element.44), channel_id=1, source_target_pairs={{0,1},{1,0},{2,3},{3,2},{4,5},{5,4},{6,7},{7,6},{8,9},{9,8},{10,11... | collective-permute-start | bytes 221192 | tf_op jit(solution)/shard_map/ppermute | solution.py:383
  28.0 4.3 %collective-permute-start.7 = (f32[72,256]{1,0:T(8,128)S(1)}, f32[72,256]{1,0:T(8,128)S(1)}, u32[]{:S(2)}, u32[]{:S(2)}) collective-permute-start(f32[72,256]{1,0:T(8,128)S(1)} %add.22), channel_id=1, source_target_pairs={{0,3},{1,2},{2,1},{3,0},{4,7},{5,6},{6,5},{7,4},{8,11},{9,10},{10,... | collective-permute-start | bytes 221192 | tf_op jit(solution)/shard_map/ppermute | solution.py:388
  30.5 3.1 %collective-permute-start.5 = (f32[128,256]{1,0:T(8,128)S(1)}, f32[128,256]{1,0:T(8,128)S(1)}, u32[]{:S(2)}, u32[]{:S(2)}) collective-permute-start(f32[128,256]{1,0:T(8,128)S(1)} %add.21.own_mid), channel_id=1, source_target_pairs={{0,1},{1,0},{2,3},{3,2},{4,5},{5,4},{6,7},{7,6},{8,9},{9,8},{10,11... | collective-permute-start | bytes 393224 | tf_op jit(solution)/shard_map/ppermute | solution.py:390
  32.3 1.3 %collective-permute-start.8 = (f32[72,256]{1,0:T(8,128)S(1)}, f32[72,256]{1,0:T(8,128)S(1)}, u32[]{:S(2)}, u32[]{:S(2)}) collective-permute-start(f32[72,256]{1,0:T(8,128)S(1)} %add.23.factors_ref.own_in), channel_id=1, source_target_pairs={{0,1},{1,0},{2,3},{3,2},{4,5},{5,4},{6,7},{7,6},{8,9},{9,8},{10,11... | collective-permute-start | bytes 221192 | tf_op jit(solution)/shard_map/ppermute | solution.py:390

commit v5 on v4

--- a/solution.py
+++ b/solution.py
@@ -12,9 +12,8 @@
 VMEM = pl.BlockSpec(memory_space=pltpu.VMEM)
 HBM = pl.BlockSpec(memory_space=pltpu.HBM)
 LIMIT = pltpu.CompilerParams(vmem_limit_bytes=32 * 1024 * 1024)
-FORWARD_CHUNKS = 4
+FIRST_LOAD = 4
 BACKWARD_CHUNKS = 8
-INNER_CHUNKS = 8
 FIRST_CHUNKS = 8
 
 
@@ -78,7 +77,7 @@
 ):
     samples, _, rays = out8.shape
     count = x_ref.shape[0]
-    chunk = count // FORWARD_CHUNKS
+    first_rows = min(FIRST_LOAD, samples) * rays
     moves = [
         pltpu.make_async_copy(source, place, sems.at[i])
         for i, (source, place) in enumerate(
@@ -91,7 +90,7 @@
     ]
     loads = [
         pltpu.make_async_copy(x_hbm.at[pl.ds(at, size)], x_ref.at[pl.ds(at, size)], sems.at[len(moves) + i])
-        for i, (at, size) in enumerate(((0, chunk), (chunk, count - chunk)))
+        for i, (at, size) in enumerate(((0, first_rows), (first_rows, count - first_rows)))
     ]
     for move in moves[2:3] + loads[:1] + moves[3:4] + moves[:2] + loads[1:] + moves[4:]:
         move.start()
@@ -99,19 +98,18 @@
         move.wait()
     w16_ref[...] = projection(head_ref[...], w3_ref[...])
 
-    for c in range(FORWARD_CHUNKS):
-        if c == 1:
+    for c in range(samples + 2):
+        if c == first_rows // rays:
             for move in moves[4:] + loads[1:]:
                 move.wait()
-        rows = pl.ds(c * chunk, chunk)
-        h1 = positive(dot_nn(x_ref[rows], w1_ref[...]))
-        h1_ref[rows] = h1
-        h2 = positive(dot_nn(h1, w2_ref[...]))
-        h2_ref[rows] = h2
-        eight = dot_nt(w16_ref[...], h2)[:8]
-        each = chunk // rays
-        for j in range(each):
-            out8[c * each + j] = eight[:, j * rays : (j + 1) * rays]
+        if c < samples:
+            rows = pl.ds(c * rays, rays)
+            h1_ref[rows] = positive(dot_nn(x_ref[rows], w1_ref[...]))
+        if 0 <= c - 1 < samples:
+            rows = pl.ds((c - 1) * rays, rays)
+            h2_ref[rows] = positive(dot_nn(h1_ref[rows], w2_ref[...]))
+        if 0 <= c - 2 < samples:
+            out8[c - 2] = dot_nt(w16_ref[...], h2_ref[pl.ds((c - 2) * rays, rays)])[:8]
 
     slab = lax.axis_index("slab")
     reverse = jnp.minimum(jnp.maximum(direction_ref[...], 0), 1)
@@ -142,11 +140,11 @@
 
 
 def backward_kernel(
-    own_ref, order_ref, h1_ref, h2_ref, save_ref, w16_ref, target_ref, *refs, n_tile,
+    own_ref, order_ref, h1_ref, h2_ref, save_ref, w16_ref, w2_ref, target_ref, *refs, n_tile,
 ):
     n_bits = order_ref.shape[0]
     pieces = refs[:n_bits]
-    front_hbm, keep_ref, send_ref, back_ref, q16, front_ref, q8, mid_ref, sem = refs[n_bits:]
+    front_hbm, keep_ref, send_ref, one_ref, q16, front_ref, q8, mid_ref, sem = refs[n_bits:]
     samples, _, rays = q8.shape
     count = h1_ref.shape[0]
     slab = lax.axis_index("slab")
@@ -193,25 +191,24 @@
         q16[:, j * rays : (j + 1) * rays] = jnp.concatenate([high, rows - high], axis=0).astype(BF16)
 
     chunk = count // BACKWARD_CHUNKS
+    def back_two(c):
+        rows = pl.ds(c * chunk, chunk)
+        return where_positive(h2_ref[rows], dot_tn(q16[:, rows], w16_ref[...]))
+
+    later = back_two(0)
     for c in range(BACKWARD_CHUNKS):
         rows = pl.ds(c * chunk, chunk)
-        back_two = where_positive(h2_ref[rows], dot_tn(q16[:, rows], w16_ref[...]))
-        back_ref[rows] = back_two
-        grad_mid = dot_tn(h1_ref[rows], back_two)
+        now = later
+        if c + 1 < BACKWARD_CHUNKS:
+            later = back_two(c + 1)
+        grad_mid = dot_tn(h1_ref[rows], now)
         mid_ref[...] = grad_mid if c == 0 else mid_ref[...] + grad_mid
+        one_ref[rows] = where_positive(h1_ref[rows], dot_nt(now, w2_ref[...]))
 
     half = mid_ref.shape[0] // 2
     for place, which in ((send_ref, 1 - kept), (keep_ref, kept)):
         place[...] = mid_ref[pl.ds(pl.multiple_of(which * half, half), half)]
     store.wait()
-
-
-def inner_kernel(h1_ref, w2_ref, back_ref, one_ref):
-    count = h1_ref.shape[0]
-    chunk = count // INNER_CHUNKS
-    for c in range(INNER_CHUNKS):
-        rows = pl.ds(c * chunk, chunk)
-        one_ref[rows] = where_positive(h1_ref[rows], dot_nt(back_ref[rows], w2_ref[...]))
 
 
 def first_kernel(x_ref, one_ref, h2_ref, q16, keep_ref, send_ref, in_ref, out_ref, *, n_tile):
@@ -348,7 +345,7 @@
 
         x, h1, h2, save, w16, w2, target_rows = kept
         half_mid, half_in = hidden // 2, width // 2 + 8
-        front, keep_mid, send_mid, back, factors = pl.pallas_call(
+        front, keep_mid, send_mid, back_one, factors = pl.pallas_call(
             functools.partial(backward_kernel, n_tile=n_tile),
             name="backward",
             out_shape=(
@@ -358,7 +355,7 @@
                 pltpu.VMEM((count, hidden), BF16),
                 pltpu.VMEM((16, count), BF16),
             ),
-            in_specs=[VMEM] * (7 + n_bits),
+            in_specs=[VMEM] * (8 + n_bits),
             out_specs=(HBM, VMEM, VMEM, VMEM, VMEM),
             scratch_shapes=[
                 pltpu.VMEM((1, rays), F32),
@@ -368,17 +365,7 @@
             ],
             compiler_params=LIMIT,
             cost_estimate=pl.CostEstimate(flops=4 * count * hidden * hidden, bytes_accessed=0, transcendentals=0),
-        )(seg, order, h1, h2, save, w16, target_rows, *pieces)
-        back_one = pl.pallas_call(
-            inner_kernel,
-            name="inner",
-            out_shape=pltpu.VMEM((count, hidden), BF16),
-            in_specs=[VMEM] * 3,
-            out_specs=VMEM,
-            compiler_params=LIMIT,
-            cost_estimate=pl.CostEstimate(flops=2 * count * hidden * hidden, bytes_accessed=0, transcendentals=0),
-        )(h1, w2, back)
-
+        )(seg, order, h1, h2, save, w16, w2, target_rows, *pieces)
         def chip_sum(keep, send):
             return keep + lax.ppermute(send, "tile", pairs(n_tile, 1))
 

time: 34.6 us -> 33.5 us (0.968)
  Pallas kernels: 11.7 us -> 10.7 us
    pallas_call x1 -> x0, Pallas kernels: 1.29 us -> none  [body(): pl.pallas_call(inner_kernel, name='inner', out_shape=pltpu.VMEM((count, h...]
    pallas_call x1, Pallas kernels: 3.12 us -> 3.71 us  [body(): pl.pallas_call(functools.partial(backward_kernel, n_tile=n_tile), name='b...]
  transfers between devices with their start and end apart: 9 -> 9, of which waited for: 7 -> 7; matrix products, arithmetic and copies ran while one was open for 0% -> 0% of each run, Pallas kernels for 8% -> 5%
where the time goes in v5:
time: 33.5 us; the launch traced here: 33.4 us
  waiting for transfers between devices  11 us (33%)
  Pallas kernels  10.7 us (32%)
  starting transfers between devices  10.7 us (32%)
  between operations  0.72 us (2%)
    ppermute x3, starting transfers between devices, body(): got = lax.ppermute(block, 'slab', pairs(n_slab, 1 << bit))  8.15 us
    ppermute x3, waiting for transfers between devices, body(): got = lax.ppermute(block, 'slab', pairs(n_slab, 1 << bit))  4.86 us
    pallas_call x1, Pallas kernels, body(): pl.pallas_call(forward_kernel, name='forward', out_shape=(pltpu.VMEM((4,...  4.54 us
    ppermute x2, waiting for transfers between devices, tile_sum(): part = part + lax.ppermute(part, 'tile', pairs(n_tile, bit | 1))  4.02 us
    pallas_call x1, Pallas kernels, body(): pl.pallas_call(functools.partial(backward_kernel, n_tile=n_tile), name='b...  3.71 us
    ppermute x2, starting transfers between devices, tile_sum(): part = part + lax.ppermute(part, 'tile', pairs(n_tile, bit | 1))  2.16 us
    pallas_call x1, Pallas kernels, body(): pl.pallas_call(functools.partial(first_kernel, n_tile=n_tile), name='firs...  1.36 us
    ppermute x2, waiting for transfers between devices, chip_sum(): return keep + lax.ppermute(send, 'tile', pairs(n_tile, 1))  1.24 us
  transfers between devices with their start and end apart: 9, of which 7 were waited for; matrix products, arithmetic and copies ran while one was open for 0% of the time, Pallas kernels for 5%

profile of v5, /device:TPU:0, one launch (start us, length us, event | category | flops | bytes accessed | tf_op | source)
XLA Modules:
  0.0 33.4 jit_solution(1885340391677659687)
XLA Ops:
  0.6 4.5 %forward.1 = (f32[4,512]{1,0:T(4,128)S(1)}, s32[3,1,512]{2,1,0:T(1,128)S(1)}, bf16[8192,128]{1,0:T(8,128)(2,1)S(1)}, bf16[8192,256]{1,0:T(8,128)(2,1)S(1)}, bf16...) custom-call(bf16[8192,128]{1,0:T(8,128)(2,1)} %bitcast.21, ...), custom_call_target="tpu_custom_call" | custom-call | tf_op jit(solution)/shard_map/forward/pallas_call | solution.py:299
  5.2 3.0 %collective-permute-start = (f32[4,512]{1,0:T(4,128)S(1)}, f32[4,512]{1,0:T(4,128)S(1)}, u32[]{:S(2)}, u32[]{:S(2)}) collective-permute-start(f32[4,512]{1,0:T(4,128)S(1)} %get-tuple-element.26.own_ref), channel_id=1, source_target_pairs={{0,4},{4,0},{8,12},{12,8},{16,20},{20,16},{24,28},{28,24},{1,5},{5... | collective-permute-start | bytes 24584 | tf_op jit(solution)/shard_map/ppermute | solution.py:341
  8.2 1.6 %collective-permute-done.refs_0_ = f32[4,512]{1,0:T(4,128)S(1)} collective-permute-done((f32[4,512]{1,0:T(4,128)S(1)}, f32[4,512]{1,0:T(4,128)S(1)}, u32[]{:S(2)}, u32[]{:S(2)}) %collective-permute-start) | collective-permute-done | bytes 8224 | tf_op jit(solution)/shard_map/ppermute | solution.py:341
  9.8 0.1 select_add_fusion.1
  9.9 2.1 %collective-permute-start.1 = (f32[4,512]{1,0:T(4,128)S(1)}, f32[4,512]{1,0:T(4,128)S(1)}, u32[]{:S(2)}, u32[]{:S(2)}) collective-permute-start(f32[4,512]{1,0:T(4,128)S(1)} %select_add_fusion.1), channel_id=1, source_target_pairs={{0,8},{4,12},{8,0},{12,4},{16,24},{20,28},{24,16},{28,20},{1,9},{5... | collective-permute-start | bytes 24584 | tf_op jit(solution)/shard_map/ppermute | solution.py:341
  12.0 1.6 %collective-permute-done.1.refs_1_ = f32[4,512]{1,0:T(4,128)S(1)} collective-permute-done((f32[4,512]{1,0:T(4,128)S(1)}, f32[4,512]{1,0:T(4,128)S(1)}, u32[]{:S(2)}, u32[]{:S(2)}) %collective-permute-start.1) | collective-permute-done | bytes 8224 | tf_op jit(solution)/shard_map/ppermute | solution.py:341
  13.7 0.1 select_add_fusion
  13.7 3.0 %collective-permute-start.2 = (f32[4,512]{1,0:T(4,128)S(1)}, f32[4,512]{1,0:T(4,128)S(1)}, u32[]{:S(2)}, u32[]{:S(2)}) collective-permute-start(f32[4,512]{1,0:T(4,128)S(1)} %select_add_fusion), channel_id=1, source_target_pairs={{0,16},{4,20},{8,24},{12,28},{16,0},{20,4},{24,8},{28,12},{1,17},{... | collective-permute-start | bytes 24584 | tf_op jit(solution)/shard_map/ppermute | solution.py:341
  16.8 1.6 %collective-permute-done.2.refs_2_ = f32[4,512]{1,0:T(4,128)S(1)} collective-permute-done((f32[4,512]{1,0:T(4,128)S(1)}, f32[4,512]{1,0:T(4,128)S(1)}, u32[]{:S(2)}, u32[]{:S(2)}) %collective-permute-start.2) | collective-permute-done | bytes 8224 | tf_op jit(solution)/shard_map/ppermute | solution.py:341
  18.4 3.7 %backward.1 = (f32[1,512]{1,0:T(1,128)}, f32[128,256]{1,0:T(8,128)S(1)}, f32[128,256]{1,0:T(8,128)S(1)}, bf16[8192,256]{1,0:T(8,128)(2,1)S(1)}, bf16[16,8192]{1,0:T(8,128)(2,1)S(1)}) custom-call(f32[4,512]{1,0:T(4,128)S(1)} %get-tuple-element.26.own_ref, s32[3,1,512]{2,1,0:T(1,128)S(1)} %get-tuple-element.27.order_ref, ...), custom_call_target="tpu_custom_call" | custom-call | flops 2147483648 | tf_op jit(solution)/shard_map/backward/pallas_call | solution.py:348
  22.1 0.1 collective-permute-start.3
  22.2 0.0 copy-start
  22.2 1.4 %first.1 = (f32[72,256]{1,0:T(8,128)S(1)}, f32[72,256]{1,0:T(8,128)S(1)}) custom-call(bf16[8192,128]{1,0:T(8,128)(2,1)S(1)} %get-tuple-element.37.x_ref, bf16[8192,256]{1,0:T(8,128)(2,1)S(1)} %get-tuple-element.38.one_ref, bf16[8192,256]{1,0:T(8,128)(2,1)S(1)} %get-tuple-element.29.h2_ref, bf16[16,8192]{1,0:T(8,128)(2,1)S(1)} %get-tuple-element.39.q16), custom_call_target="tpu_custom_call" | custom-call | flops 2147483648 | tf_op jit(solution)/shard_map/first/pallas_call | solution.py:380
  23.6 0.0 collective-permute-done.3
  23.6 2.0 %collective-permute-start.4 = (f32[128,256]{1,0:T(8,128)S(1)}, f32[128,256]{1,0:T(8,128)S(1)}, u32[]{:S(2)}, u32[]{:S(2)}) collective-permute-start(f32[128,256]{1,0:T(8,128)S(1)} %add.20), channel_id=1, source_target_pairs={{0,3},{1,2},{2,1},{3,0},{4,7},{5,6},{6,5},{7,4},{8,11},{9,10},{10,... | collective-permute-start | bytes 393224 | tf_op jit(solution)/shard_map/ppermute | solution.py:375
  25.6 0.0 collective-permute-start.6
  25.7 1.2 %collective-permute-done.6 = f32[72,256]{1,0:T(8,128)S(1)} collective-permute-done((f32[72,256]{1,0:T(8,128)S(1)}, f32[72,256]{1,0:T(8,128)S(1)}, u32[]{:S(2)}, u32[]{:S(2)}) %collective-permute-start.6) | collective-permute-done | bytes 73760 | tf_op jit(solution)/shard_map/ppermute | solution.py:370
  26.9 0.1 collective-permute-start.7
  27.1 2.4 %collective-permute-done.4 = f32[128,256]{1,0:T(8,128)S(1)} collective-permute-done((f32[128,256]{1,0:T(8,128)S(1)}, f32[128,256]{1,0:T(8,128)S(1)}, u32[]{:S(2)}, u32[]{:S(2)}) %collective-permute-start.4) | collective-permute-done | bytes 131104 | tf_op jit(solution)/shard_map/ppermute | solution.py:375
  29.5 0.1 collective-permute-start.5
  29.6 1.6 %collective-permute-done.7 = f32[72,256]{1,0:T(8,128)S(1)} collective-permute-done((f32[72,256]{1,0:T(8,128)S(1)}, f32[72,256]{1,0:T(8,128)S(1)}, u32[]{:S(2)}, u32[]{:S(2)}) %collective-permute-start.7) | collective-permute-done | bytes 73760 | tf_op jit(solution)/shard_map/ppermute | solution.py:375
  31.2 0.2 collective-permute-start.8
  31.4 0.0 copy-done
  31.4 0.3 expand.1.out_ref
  31.7 0.8 %collective-permute-done.8.other_in = f32[72,256]{1,0:T(8,128)S(1)} collective-permute-done((f32[72,256]{1,0:T(8,128)S(1)}, f32[72,256]{1,0:T(8,128)S(1)}, u32[]{:S(2)}, u32[]{:S(2)}) %collective-permute-start.8) | collective-permute-done | bytes 73760 | tf_op jit(solution)/shard_map/ppermute | solution.py:377
  32.5 0.0 collective-permute-done.5.other_mid
  32.5 0.8 %final.1 = (f32[128,256]{1,0:T(8,128)}, f32[256,256]{1,0:T(8,128)}, f32[64,256]{1,0:T(8,128)}) custom-call(f32[128,256]{1,0:T(8,128)S(1)} %add.21.own_mid, f32[128,256]{1,0:T(8,128)S(1)} %collective-permute-done.5.other_mid, f32[72,256]{1,0:T(8,128)S(1)} %add.23.factors_ref.own_in, f32[72,256]{1,0:T(8,128)S(1)} %collective-permute-done.8.other_in, ...), custom_call_target="tpu_custom_call" | custom-call | tf_op jit(solution)/shard_map/final/pallas_call | solution.py:403
  (10 shorter events, 0.1 us)
Async XLA Ops:
  5.2 4.6 %collective-permute-start = (f32[4,512]{1,0:T(4,128)S(1)}, f32[4,512]{1,0:T(4,128)S(1)}, u32[]{:S(2)}, u32[]{:S(2)}) collective-permute-start(f32[4,512]{1,0:T(4,128)S(1)} %get-tuple-element.26.own_ref), channel_id=1, source_target_pairs={{0,4},{4,0},{8,12},{12,8},{16,20},{20,16},{24,28},{28,24},{1,5},{5... | collective-permute-start | bytes 24584 | tf_op jit(solution)/shard_map/ppermute | solution.py:341
  9.9 3.7 %collective-permute-start.1 = (f32[4,512]{1,0:T(4,128)S(1)}, f32[4,512]{1,0:T(4,128)S(1)}, u32[]{:S(2)}, u32[]{:S(2)}) collective-permute-start(f32[4,512]{1,0:T(4,128)S(1)} %select_add_fusion.1), channel_id=1, source_target_pairs={{0,8},{4,12},{8,0},{12,4},{16,24},{20,28},{24,16},{28,20},{1,9},{5... | collective-permute-start | bytes 24584 | tf_op jit(solution)/shard_map/ppermute | solution.py:341
  13.7 4.7 %collective-permute-start.2 = (f32[4,512]{1,0:T(4,128)S(1)}, f32[4,512]{1,0:T(4,128)S(1)}, u32[]{:S(2)}, u32[]{:S(2)}) collective-permute-start(f32[4,512]{1,0:T(4,128)S(1)} %select_add_fusion), channel_id=1, source_target_pairs={{0,16},{4,20},{8,24},{12,28},{16,0},{20,4},{24,8},{28,12},{1,17},{... | collective-permute-start | bytes 24584 | tf_op jit(solution)/shard_map/ppermute | solution.py:341
  22.1 1.5 %collective-permute-start.3 = (f32[128,256]{1,0:T(8,128)S(1)}, f32[128,256]{1,0:T(8,128)S(1)}, u32[]{:S(2)}, u32[]{:S(2)}) collective-permute-start(f32[128,256]{1,0:T(8,128)S(1)} %get-tuple-element.36), channel_id=1, source_target_pairs={{0,1},{1,0},{2,3},{3,2},{4,5},{5,4},{6,7},{7,6},{8,9},{9,8},{10,11... | collective-permute-start | bytes 393224 | tf_op jit(solution)/shard_map/ppermute | solution.py:370
  22.2 9.2 %copy-start = (f32[64,3]{0,1:T(4,128)S(1)}, f32[64,3]{0,1:T(4,128)}, u32[]{:S(2)}) copy-start(f32[64,3]{0,1:T(4,128)} %param.20) | copy-start | bytes 2308
  23.6 5.9 %collective-permute-start.4 = (f32[128,256]{1,0:T(8,128)S(1)}, f32[128,256]{1,0:T(8,128)S(1)}, u32[]{:S(2)}, u32[]{:S(2)}) collective-permute-start(f32[128,256]{1,0:T(8,128)S(1)} %add.20), channel_id=1, source_target_pairs={{0,3},{1,2},{2,1},{3,0},{4,7},{5,6},{6,5},{7,4},{8,11},{9,10},{10,... | collective-permute-start | bytes 393224 | tf_op jit(solution)/shard_map/ppermute | solution.py:375
  25.6 1.3 %collective-permute-start.6 = (f32[72,256]{1,0:T(8,128)S(1)}, f32[72,256]{1,0:T(8,128)S(1)}, u32[]{:S(2)}, u32[]{:S(2)}) collective-permute-start(f32[72,256]{1,0:T(8,128)S(1)} %get-tuple-element.44), channel_id=1, source_target_pairs={{0,1},{1,0},{2,3},{3,2},{4,5},{5,4},{6,7},{7,6},{8,9},{9,8},{10,11... | collective-permute-start | bytes 221192 | tf_op jit(solution)/shard_map/ppermute | solution.py:370
  26.9 4.3 %collective-permute-start.7 = (f32[72,256]{1,0:T(8,128)S(1)}, f32[72,256]{1,0:T(8,128)S(1)}, u32[]{:S(2)}, u32[]{:S(2)}) collective-permute-start(f32[72,256]{1,0:T(8,128)S(1)} %add.22), channel_id=1, source_target_pairs={{0,3},{1,2},{2,1},{3,0},{4,7},{5,6},{6,5},{7,4},{8,11},{9,10},{10,... | collective-permute-start | bytes 221192 | tf_op jit(solution)/shard_map/ppermute | solution.py:375
  29.5 3.1 %collective-permute-start.5 = (f32[128,256]{1,0:T(8,128)S(1)}, f32[128,256]{1,0:T(8,128)S(1)}, u32[]{:S(2)}, u32[]{:S(2)}) collective-permute-start(f32[128,256]{1,0:T(8,128)S(1)} %add.21.own_mid), channel_id=1, source_target_pairs={{0,1},{1,0},{2,3},{3,2},{4,5},{5,4},{6,7},{7,6},{8,9},{9,8},{10,11... | collective-permute-start | bytes 393224 | tf_op jit(solution)/shard_map/ppermute | solution.py:377
  31.2 1.3 %collective-permute-start.8 = (f32[72,256]{1,0:T(8,128)S(1)}, f32[72,256]{1,0:T(8,128)S(1)}, u32[]{:S(2)}, u32[]{:S(2)}) collective-permute-start(f32[72,256]{1,0:T(8,128)S(1)} %add.23.factors_ref.own_in), channel_id=1, source_target_pairs={{0,1},{1,0},{2,3},{3,2},{4,5},{5,4},{6,7},{7,6},{8,9},{9,8},{10,11... | collective-permute-start | bytes 221192 | tf_op jit(solution)/shard_map/ppermute | solution.py:377

commit v6 on v5

--- a/solution.py
+++ b/solution.py
@@ -72,8 +72,8 @@
 def forward_kernel(
     x_hbm, spacing_hbm, counts_hbm, first_hbm, last_hbm, direction_hbm, target_hbm,
     w1_hbm, w2_hbm, w3_hbm, head_hbm,
-    seg_ref, order_ref, x_ref, h1_ref, h2_ref, save_ref, w16_ref, w2_ref, target_ref,
-    w1_ref, w3_ref, head_ref, spacing_ref, counts_ref, first_ref, last_ref, direction_ref, out8, sems,
+    seg_ref, x_ref, h1_ref, h2_ref, save_ref, w16_ref, w2_ref, target_ref,
+    w1_ref, w3_ref, head_ref, spacing_ref, counts_ref, first_ref, last_ref, direction_ref, out8, sems, *, n_bits,
 ):
     samples, _, rays = out8.shape
     count = x_ref.shape[0]
@@ -113,9 +113,8 @@
 
     slab = lax.axis_index("slab")
     reverse = jnp.minimum(jnp.maximum(direction_ref[...], 0), 1)
-    for bit in range(order_ref.shape[0]):
-        higher = (slab >> bit) & 1
-        order_ref[bit] = 1 - (reverse ^ higher)
+    ahead = [(1 - (reverse ^ ((slab >> bit) & 1))).astype(F32) for bit in range(n_bits)]
+    ahead += [jnp.zeros_like(ahead[0])] * (seg_ref.shape[0] - 4 - n_bits)
     density = out8[:, 0, :]
     proj = [out8[:, 1 + k, :] + out8[:, 4 + k, :] for k in range(3)]
     ids = lax.broadcasted_iota(jnp.int32, density.shape, 0)
@@ -130,7 +129,7 @@
     passed = jnp.exp(-optical)
     weights = reach * (1.0 - passed)
     seg_ref[...] = jnp.concatenate(
-        [jnp.exp(-column)] + [jnp.sum(weights * p, axis=0, keepdims=True) for p in proj], axis=0
+        [jnp.exp(-column)] + [jnp.sum(weights * p, axis=0, keepdims=True) for p in proj] + ahead, axis=0
     )
     save_ref[0] = weights
     save_ref[1] = reach * passed
@@ -140,9 +139,8 @@
 
 
 def backward_kernel(
-    own_ref, order_ref, h1_ref, h2_ref, save_ref, w16_ref, w2_ref, target_ref, *refs, n_tile,
+    own_ref, h1_ref, h2_ref, save_ref, w16_ref, w2_ref, target_ref, *refs, n_bits, n_tile,
 ):
-    n_bits = order_ref.shape[0]
     pieces = refs[:n_bits]
     front_hbm, keep_ref, send_ref, one_ref, q16, front_ref, q8, mid_ref, sem = refs[n_bits:]
     samples, _, rays = q8.shape
@@ -153,13 +151,13 @@
     front_trans = back_trans = jnp.ones((1, rays), F32)
     front_color = back_color = jnp.zeros((3, rays), F32)
     for bit in range(n_bits):
-        behind = order_ref[bit] > 0
-        trans, color = pieces[bit][0:1], pieces[bit][1:4]
+        behind = own_ref[4 + bit : 5 + bit] > 0
+        trans, color = pieces[bit][1, 0:1], pieces[bit][1, 1:4]
         front_color = jnp.where(behind, front_color, color + trans * front_color)
         front_trans = jnp.where(behind, front_trans, trans * front_trans)
         back_color = jnp.where(behind, back_color + back_trans * color, back_color)
         back_trans = jnp.where(behind, back_trans * trans, back_trans)
-    forward_ray = (order_ref[0] ^ (slab & 1)) > 0
+    forward_ray = own_ref[4:5] + (slab & 1).astype(F32) == 1.0
     front_ref[...] = front_trans
     store = pltpu.make_async_copy(front_ref, front_hbm, sem)
     store.start()
@@ -276,8 +274,8 @@
 def joined(own, got, own_first):
     first = jnp.where(own_first, own, got)
     second = jnp.where(own_first, got, own)
-    row = lax.broadcasted_iota(jnp.int32, own.shape, 0)
-    return first[0:1] * second + jnp.where(row == 0, 0.0, first)
+    row = lax.broadcasted_iota(jnp.int32, own.shape, 1)
+    return first[:, 0:1] * second + jnp.where(row == 0, 0.0, first)
 
 
 def pairs(size, bit):
@@ -296,12 +294,12 @@
         count = samples * rays
         n_bits = (n_slab - 1).bit_length()
         row = lambda a: a.reshape(1, rays)
-        seg, order, *kept = pl.pallas_call(
-            forward_kernel,
+        seg_rows = 8 * ((4 + n_bits + 7) // 8)
+        seg, *kept = pl.pallas_call(
+            functools.partial(forward_kernel, n_bits=n_bits),
             name="forward",
             out_shape=(
-                pltpu.VMEM((4, rays), F32),
-                pltpu.VMEM((n_bits, 1, rays), jnp.int32),
+                pltpu.VMEM((seg_rows, rays), F32),
                 pltpu.VMEM((count, width), BF16),
                 pltpu.VMEM((count, hidden), BF16),
                 pltpu.VMEM((count, hidden), BF16),
@@ -311,7 +309,7 @@
                 pltpu.VMEM((3, rays), F32),
             ),
             in_specs=[HBM] * 11,
-            out_specs=(VMEM,) * 9,
+            out_specs=(VMEM,) * 8,
             scratch_shapes=[
                 pltpu.VMEM((width, hidden), BF16),
                 pltpu.VMEM((features, hidden), BF16),
@@ -335,18 +333,19 @@
             ),
         )
 
-        block = seg
+        both = jnp.stack([seg, lax.ppermute(seg, "tile", pairs(n_tile, 1))])
+        block = both[:, :4]
         pieces = []
         for bit in range(n_bits):
-            got = lax.ppermute(block, "slab", pairs(n_slab, 1 << bit))
+            got = lax.ppermute(block, ("slab", "tile"), pairs(n_slab * n_tile, (n_tile << bit) | 1))
             pieces.append(got)
             if bit + 1 < n_bits:
-                block = joined(block, got, order[bit] > 0)
+                block = joined(block, got[::-1], both[:, 4 + bit : 5 + bit] > 0)
 
         x, h1, h2, save, w16, w2, target_rows = kept
         half_mid, half_in = hidden // 2, width // 2 + 8
         front, keep_mid, send_mid, back_one, factors = pl.pallas_call(
-            functools.partial(backward_kernel, n_tile=n_tile),
+            functools.partial(backward_kernel, n_bits=n_bits, n_tile=n_tile),
             name="backward",
             out_shape=(
                 pltpu.HBM((1, rays), F32),
@@ -355,7 +354,7 @@
                 pltpu.VMEM((count, hidden), BF16),
                 pltpu.VMEM((16, count), BF16),
             ),
-            in_specs=[VMEM] * (8 + n_bits),
+            in_specs=[VMEM] * (7 + n_bits),
             out_specs=(HBM, VMEM, VMEM, VMEM, VMEM),
             scratch_shapes=[
                 pltpu.VMEM((1, rays), F32),
@@ -365,7 +364,7 @@
             ],
             compiler_params=LIMIT,
             cost_estimate=pl.CostEstimate(flops=4 * count * hidden * hidden, bytes_accessed=0, transcendentals=0),
-        )(seg, order, h1, h2, save, w16, w2, target_rows, *pieces)
+        )(seg, h1, h2, save, w16, w2, target_rows, *pieces)
         def chip_sum(keep, send):
             return keep + lax.ppermute(send, "tile", pairs(n_tile, 1))
 

time: 33.5 us -> 33.1 us (0.988)
    ppermute x2, starting transfers between devices: 0.1 us -> 0.56 us  [chip_sum(): return keep + lax.ppermute(send, 'tile', pairs(n_tile, 1))]
    ppermute x3 -> x4, starting transfers between devices: 8.15 us -> 7.69 us  [the longest x3 7.16 us: body(): lax.ppermute(block, ('slab', 'tile'), pairs(n_slab * n_tile, n_tile << bi...]
    ppermute x3 -> x4, waiting for transfers between devices: 4.86 us -> 5.12 us  [the longest x3 4.29 us: body(): lax.ppermute(block, ('slab', 'tile'), pairs(n_slab * n_tile, n_tile << bi...]
  transfers between devices with their start and end apart: 9 -> 10, of which waited for: 7 -> 8; matrix products, arithmetic and copies ran while one was open for 0% -> 0% of each run, Pallas kernels for 5% -> 5%
where the time goes in v6:
time: 33.1 us; the launch traced here: 33 us
  waiting for transfers between devices  10.9 us (33%)
  Pallas kernels  10.5 us (32%)
  starting transfers between devices  10.5 us (32%)
  between operations  0.75 us (2%)
    ppermute x3, starting transfers between devices, body(): lax.ppermute(block, ('slab', 'tile'), pairs(n_slab * n_tile, n_tile << bi...  7.16 us
    pallas_call x1, Pallas kernels, body(): pl.pallas_call(functools.partial(forward_kernel, n_bits=n_bits), name='fo...  4.53 us
    ppermute x3, waiting for transfers between devices, body(): lax.ppermute(block, ('slab', 'tile'), pairs(n_slab * n_tile, n_tile << bi...  4.29 us
    ppermute x2, waiting for transfers between devices, tile_sum(): part = part + lax.ppermute(part, 'tile', pairs(n_tile, bit | 1))  3.84 us
    pallas_call x1, Pallas kernels, body(): pl.pallas_call(functools.partial(backward_kernel, n_bits=n_bits, n_tile=n...  3.64 us
    ppermute x2, starting transfers between devices, tile_sum(): part = part + lax.ppermute(part, 'tile', pairs(n_tile, bit | 1))  1.88 us
    pallas_call x1, Pallas kernels, body(): pl.pallas_call(functools.partial(first_kernel, n_tile=n_tile), name='firs...  1.26 us
    ppermute x2, waiting for transfers between devices, chip_sum(): return keep + lax.ppermute(send, 'tile', pairs(n_tile, 1))  1.1 us
  transfers between devices with their start and end apart: 10, of which 8 were waited for; matrix products, arithmetic and copies ran while one was open for 0% of the time, Pallas kernels for 5%

profile of v6, /device:TPU:0, one launch (start us, length us, event | category | flops | bytes accessed | tf_op | source)
XLA Modules:
  0.0 33.0 jit_solution(6878836058591970168)
XLA Ops:
  0.6 4.5 %forward.1 = (f32[8,512]{1,0:T(8,128)S(1)}, bf16[8192,128]{1,0:T(8,128)(2,1)S(1)}, bf16[8192,256]{1,0:T(8,128)(2,1)S(1)}, bf16[8192,256]{1,0:T(8,128)(2,1)S(1)},...) custom-call(bf16[8192,128]{1,0:T(8,128)(2,1)} %bitcast.37, ...), custom_call_target="tpu_custom_call" | custom-call | tf_op jit(solution)/shard_map/forward/pallas_call | solution.py:298
  5.2 0.5 %collective-permute-start = (f32[8,512]{1,0:T(8,128)S(1)}, f32[8,512]{1,0:T(8,128)S(1)}, u32[]{:S(2)}, u32[]{:S(2)}) collective-permute-start(f32[8,512]{1,0:T(8,128)S(1)} %get-tuple-element.25.own_ref), channel_id=1, source_target_pairs={{0,1},{1,0},{2,3},{3,2},{4,5},{5,4},{6,7},{7,6},{8,9},{9,8},{10,11... | collective-permute-start | bytes 49160 | tf_op jit(solution)/shard_map/ppermute | solution.py:336
  5.7 0.8 %collective-permute-done = f32[8,512]{1,0:T(8,128)S(1)} collective-permute-done((f32[8,512]{1,0:T(8,128)S(1)}, f32[8,512]{1,0:T(8,128)S(1)}, u32[]{:S(2)}, u32[]{:S(2)}) %collective-permute-start) | collective-permute-done | bytes 16416 | tf_op jit(solution)/shard_map/ppermute | solution.py:336
  6.5 2.6 %collective-permute-start.1 = (f32[2,4,512]{2,1,0:T(4,128)S(1)}, f32[2,4,512]{2,1,0:T(4,128)S(1)}, u32[]{:S(2)}, u32[]{:S(2)}) collective-permute-start(f32[2,4,512]{2,1,0:T(4,128)S(1)} %fusion), channel_id=1, source_target_pairs={{0,5},{1,4},{2,7},{3,6},{4,1},{5,0},{6,3},{7,2},{8,13},{9,12},{10,... | collective-permute-start | bytes 49160 | tf_op jit(solution)/shard_map/ppermute | solution.py:340
  9.2 1.4 %collective-permute-done.1.refs_0_ = f32[2,4,512]{2,1,0:T(4,128)S(1)} collective-permute-done((f32[2,4,512]{2,1,0:T(4,128)S(1)}, f32[2,4,512]{2,1,0:T(4,128)S(1)}, u32[]{:S(2)}, u32[]{:S(2)}) %collective-permute-start.1) | collective-permute-done | bytes 16416 | tf_op jit(solution)/shard_map/ppermute | solution.py:340
  10.6 0.1 select_add_fusion.1
  10.7 1.8 %collective-permute-start.2 = (f32[2,4,512]{2,1,0:T(4,128)S(1)}, f32[2,4,512]{2,1,0:T(4,128)S(1)}, u32[]{:S(2)}, u32[]{:S(2)}) collective-permute-start(f32[2,4,512]{2,1,0:T(4,128)S(1)} %select_add_fusion.1), channel_id=1, source_target_pairs={{0,9},{1,8},{2,11},{3,10},{4,13},{5,12},{6,15},{7,14},{8,1},{9,0},... | collective-permute-start | bytes 49160 | tf_op jit(solution)/shard_map/ppermute | solution.py:340
  12.5 1.4 %collective-permute-done.2.refs_1_ = f32[2,4,512]{2,1,0:T(4,128)S(1)} collective-permute-done((f32[2,4,512]{2,1,0:T(4,128)S(1)}, f32[2,4,512]{2,1,0:T(4,128)S(1)}, u32[]{:S(2)}, u32[]{:S(2)}) %collective-permute-start.2) | collective-permute-done | bytes 16416 | tf_op jit(solution)/shard_map/ppermute | solution.py:340
  14.0 0.1 select_add_fusion
  14.1 2.8 %collective-permute-start.3 = (f32[2,4,512]{2,1,0:T(4,128)S(1)}, f32[2,4,512]{2,1,0:T(4,128)S(1)}, u32[]{:S(2)}, u32[]{:S(2)}) collective-permute-start(f32[2,4,512]{2,1,0:T(4,128)S(1)} %select_add_fusion), channel_id=1, source_target_pairs={{0,17},{1,16},{2,19},{3,18},{4,21},{5,20},{6,23},{7,22},{8,25},{9,... | collective-permute-start | bytes 49160 | tf_op jit(solution)/shard_map/ppermute | solution.py:340
  16.8 1.4 %collective-permute-done.3.refs_2_ = f32[2,4,512]{2,1,0:T(4,128)S(1)} collective-permute-done((f32[2,4,512]{2,1,0:T(4,128)S(1)}, f32[2,4,512]{2,1,0:T(4,128)S(1)}, u32[]{:S(2)}, u32[]{:S(2)}) %collective-permute-start.3) | collective-permute-done | bytes 16416 | tf_op jit(solution)/shard_map/ppermute | solution.py:340
  18.3 3.6 %backward.1 = (f32[1,512]{1,0:T(1,128)}, f32[128,256]{1,0:T(8,128)S(1)}, f32[128,256]{1,0:T(8,128)S(1)}, bf16[8192,256]{1,0:T(8,128)(2,1)S(1)}, bf16[16,8192]{1,0:T(8,128)(2,1)S(1)}) custom-call(f32[8,512]{1,0:T(8,128)S(1)} %get-tuple-element.25.own_ref, bf16[8192,256]{1,0:T(8,128)(2,1)S(1)} %get-tuple-element.26.h1_ref, ...), custom_call_target="tpu_custom_call" | custom-call | flops 2147483648 | tf_op jit(solution)/shard_map/backward/pallas_call | solution.py:347
  21.9 0.4 %collective-permute-start.4 = (f32[128,256]{1,0:T(8,128)S(1)}, f32[128,256]{1,0:T(8,128)S(1)}, u32[]{:S(2)}, u32[]{:S(2)}) collective-permute-start(f32[128,256]{1,0:T(8,128)S(1)} %get-tuple-element.34), channel_id=1, source_target_pairs={{0,1},{1,0},{2,3},{3,2},{4,5},{5,4},{6,7},{7,6},{8,9},{9,8},{10,11... | collective-permute-start | bytes 393224 | tf_op jit(solution)/shard_map/ppermute | solution.py:369
  22.3 0.0 copy-start
  22.3 1.3 %first.1 = (f32[72,256]{1,0:T(8,128)S(1)}, f32[72,256]{1,0:T(8,128)S(1)}) custom-call(bf16[8192,128]{1,0:T(8,128)(2,1)S(1)} %get-tuple-element.35.x_ref, bf16[8192,256]{1,0:T(8,128)(2,1)S(1)} %get-tuple-element.36.one_ref, bf16[8192,256]{1,0:T(8,128)(2,1)S(1)} %get-tuple-element.27.h2_ref, bf16[16,8192]{1,0:T(8,128)(2,1)S(1)} %get-tuple-element.37.q16), custom_call_target="tpu_custom_call" | custom-call | flops 2147483648 | tf_op jit(solution)/shard_map/first/pallas_call | solution.py:379
  23.6 0.0 collective-permute-done.4
  23.6 1.6 %collective-permute-start.5 = (f32[128,256]{1,0:T(8,128)S(1)}, f32[128,256]{1,0:T(8,128)S(1)}, u32[]{:S(2)}, u32[]{:S(2)}) collective-permute-start(f32[128,256]{1,0:T(8,128)S(1)} %add.20), channel_id=1, source_target_pairs={{0,3},{1,2},{2,1},{3,0},{4,7},{5,6},{6,5},{7,4},{8,11},{9,10},{10,... | collective-permute-start | bytes 393224 | tf_op jit(solution)/shard_map/ppermute | solution.py:374
  25.2 0.2 collective-permute-start.7
  25.4 1.1 %collective-permute-done.7 = f32[72,256]{1,0:T(8,128)S(1)} collective-permute-done((f32[72,256]{1,0:T(8,128)S(1)}, f32[72,256]{1,0:T(8,128)S(1)}, u32[]{:S(2)}, u32[]{:S(2)}) %collective-permute-start.7) | collective-permute-done | bytes 73760 | tf_op jit(solution)/shard_map/ppermute | solution.py:369
  26.5 0.2 collective-permute-start.8
  26.8 2.4 %collective-permute-done.5 = f32[128,256]{1,0:T(8,128)S(1)} collective-permute-done((f32[128,256]{1,0:T(8,128)S(1)}, f32[128,256]{1,0:T(8,128)S(1)}, u32[]{:S(2)}, u32[]{:S(2)}) %collective-permute-start.5) | collective-permute-done | bytes 131104 | tf_op jit(solution)/shard_map/ppermute | solution.py:374
  29.2 0.2 collective-permute-start.6
  29.4 1.4 %collective-permute-done.8 = f32[72,256]{1,0:T(8,128)S(1)} collective-permute-done((f32[72,256]{1,0:T(8,128)S(1)}, f32[72,256]{1,0:T(8,128)S(1)}, u32[]{:S(2)}, u32[]{:S(2)}) %collective-permute-start.8) | collective-permute-done | bytes 73760 | tf_op jit(solution)/shard_map/ppermute | solution.py:374
  30.8 0.2 collective-permute-start.9
  31.1 0.0 copy-done
  31.1 0.3 expand.1.out_ref
  31.3 0.8 %collective-permute-done.9.other_in = f32[72,256]{1,0:T(8,128)S(1)} collective-permute-done((f32[72,256]{1,0:T(8,128)S(1)}, f32[72,256]{1,0:T(8,128)S(1)}, u32[]{:S(2)}, u32[]{:S(2)}) %collective-permute-start.9) | collective-permute-done | bytes 73760 | tf_op jit(solution)/shard_map/ppermute | solution.py:376
  32.2 0.0 collective-permute-done.6.other_mid
  32.2 0.8 %final.1 = (f32[128,256]{1,0:T(8,128)}, f32[256,256]{1,0:T(8,128)}, f32[64,256]{1,0:T(8,128)}) custom-call(f32[128,256]{1,0:T(8,128)S(1)} %add.21.own_mid, f32[128,256]{1,0:T(8,128)S(1)} %collective-permute-done.6.other_mid, f32[72,256]{1,0:T(8,128)S(1)} %add.23.factors_ref.own_in, f32[72,256]{1,0:T(8,128)S(1)} %collective-permute-done.9.other_in, ...), custom_call_target="tpu_custom_call" | custom-call | tf_op jit(solution)/shard_map/final/pallas_call | solution.py:402
  (15 shorter events, 0.1 us)
Async XLA Ops:
  5.2 1.4 %collective-permute-start = (f32[8,512]{1,0:T(8,128)S(1)}, f32[8,512]{1,0:T(8,128)S(1)}, u32[]{:S(2)}, u32[]{:S(2)}) collective-permute-start(f32[8,512]{1,0:T(8,128)S(1)} %get-tuple-element.25.own_ref), channel_id=1, source_target_pairs={{0,1},{1,0},{2,3},{3,2},{4,5},{5,4},{6,7},{7,6},{8,9},{9,8},{10,11... | collective-permute-start | bytes 49160 | tf_op jit(solution)/shard_map/ppermute | solution.py:336
  6.5 4.0 %collective-permute-start.1 = (f32[2,4,512]{2,1,0:T(4,128)S(1)}, f32[2,4,512]{2,1,0:T(4,128)S(1)}, u32[]{:S(2)}, u32[]{:S(2)}) collective-permute-start(f32[2,4,512]{2,1,0:T(4,128)S(1)} %fusion), channel_id=1, source_target_pairs={{0,5},{1,4},{2,7},{3,6},{4,1},{5,0},{6,3},{7,2},{8,13},{9,12},{10,... | collective-permute-start | bytes 49160 | tf_op jit(solution)/shard_map/ppermute | solution.py:340
  10.7 3.3 %collective-permute-start.2 = (f32[2,4,512]{2,1,0:T(4,128)S(1)}, f32[2,4,512]{2,1,0:T(4,128)S(1)}, u32[]{:S(2)}, u32[]{:S(2)}) collective-permute-start(f32[2,4,512]{2,1,0:T(4,128)S(1)} %select_add_fusion.1), channel_id=1, source_target_pairs={{0,9},{1,8},{2,11},{3,10},{4,13},{5,12},{6,15},{7,14},{8,1},{9,0},... | collective-permute-start | bytes 49160 | tf_op jit(solution)/shard_map/ppermute | solution.py:340
  14.1 4.2 %collective-permute-start.3 = (f32[2,4,512]{2,1,0:T(4,128)S(1)}, f32[2,4,512]{2,1,0:T(4,128)S(1)}, u32[]{:S(2)}, u32[]{:S(2)}) collective-permute-start(f32[2,4,512]{2,1,0:T(4,128)S(1)} %select_add_fusion), channel_id=1, source_target_pairs={{0,17},{1,16},{2,19},{3,18},{4,21},{5,20},{6,23},{7,22},{8,25},{9,... | collective-permute-start | bytes 49160 | tf_op jit(solution)/shard_map/ppermute | solution.py:340
  21.9 1.7 %collective-permute-start.4 = (f32[128,256]{1,0:T(8,128)S(1)}, f32[128,256]{1,0:T(8,128)S(1)}, u32[]{:S(2)}, u32[]{:S(2)}) collective-permute-start(f32[128,256]{1,0:T(8,128)S(1)} %get-tuple-element.34), channel_id=1, source_target_pairs={{0,1},{1,0},{2,3},{3,2},{4,5},{5,4},{6,7},{7,6},{8,9},{9,8},{10,11... | collective-permute-start | bytes 393224 | tf_op jit(solution)/shard_map/ppermute | solution.py:369
  22.3 8.8 %copy-start = (f32[64,3]{0,1:T(4,128)S(1)}, f32[64,3]{0,1:T(4,128)}, u32[]{:S(2)}) copy-start(f32[64,3]{0,1:T(4,128)} %param.20) | copy-start | bytes 2308
  23.6 5.6 %collective-permute-start.5 = (f32[128,256]{1,0:T(8,128)S(1)}, f32[128,256]{1,0:T(8,128)S(1)}, u32[]{:S(2)}, u32[]{:S(2)}) collective-permute-start(f32[128,256]{1,0:T(8,128)S(1)} %add.20), channel_id=1, source_target_pairs={{0,3},{1,2},{2,1},{3,0},{4,7},{5,6},{6,5},{7,4},{8,11},{9,10},{10,... | collective-permute-start | bytes 393224 | tf_op jit(solution)/shard_map/ppermute | solution.py:374
  25.2 1.3 %collective-permute-start.7 = (f32[72,256]{1,0:T(8,128)S(1)}, f32[72,256]{1,0:T(8,128)S(1)}, u32[]{:S(2)}, u32[]{:S(2)}) collective-permute-start(f32[72,256]{1,0:T(8,128)S(1)} %get-tuple-element.42), channel_id=1, source_target_pairs={{0,1},{1,0},{2,3},{3,2},{4,5},{5,4},{6,7},{7,6},{8,9},{9,8},{10,11... | collective-permute-start | bytes 221192 | tf_op jit(solution)/shard_map/ppermute | solution.py:369
  26.5 4.3 %collective-permute-start.8 = (f32[72,256]{1,0:T(8,128)S(1)}, f32[72,256]{1,0:T(8,128)S(1)}, u32[]{:S(2)}, u32[]{:S(2)}) collective-permute-start(f32[72,256]{1,0:T(8,128)S(1)} %add.22), channel_id=1, source_target_pairs={{0,3},{1,2},{2,1},{3,0},{4,7},{5,6},{6,5},{7,4},{8,11},{9,10},{10,... | collective-permute-start | bytes 221192 | tf_op jit(solution)/shard_map/ppermute | solution.py:374
  29.2 2.9 %collective-permute-start.6 = (f32[128,256]{1,0:T(8,128)S(1)}, f32[128,256]{1,0:T(8,128)S(1)}, u32[]{:S(2)}, u32[]{:S(2)}) collective-permute-start(f32[128,256]{1,0:T(8,128)S(1)} %add.21.own_mid), channel_id=1, source_target_pairs={{0,1},{1,0},{2,3},{3,2},{4,5},{5,4},{6,7},{7,6},{8,9},{9,8},{10,11... | collective-permute-start | bytes 393224 | tf_op jit(solution)/shard_map/ppermute | solution.py:376
  30.8 1.3 %collective-permute-start.9 = (f32[72,256]{1,0:T(8,128)S(1)}, f32[72,256]{1,0:T(8,128)S(1)}, u32[]{:S(2)}, u32[]{:S(2)}) collective-permute-start(f32[72,256]{1,0:T(8,128)S(1)} %add.23.factors_ref.own_in), channel_id=1, source_target_pairs={{0,1},{1,0},{2,3},{3,2},{4,5},{5,4},{6,7},{7,6},{8,9},{9,8},{10,11... | collective-permute-start | bytes 221192 | tf_op jit(solution)/shard_map/ppermute | solution.py:376

commit v7 on v6

--- a/solution.py
+++ b/solution.py
@@ -152,7 +152,8 @@
     front_color = back_color = jnp.zeros((3, rays), F32)
     for bit in range(n_bits):
         behind = own_ref[4 + bit : 5 + bit] > 0
-        trans, color = pieces[bit][1, 0:1], pieces[bit][1, 1:4]
+        piece = pieces[bit] if len(pieces[bit].shape) == 2 else pieces[bit].at[1]
+        trans, color = piece[0:1], piece[1:4]
         front_color = jnp.where(behind, front_color, color + trans * front_color)
         front_trans = jnp.where(behind, front_trans, trans * front_trans)
         back_color = jnp.where(behind, back_color + back_trans * color, back_color)
@@ -271,11 +272,19 @@
     return half
 
 
-def joined(own, got, own_first):
-    first = jnp.where(own_first, own, got)
-    second = jnp.where(own_first, got, own)
-    row = lax.broadcasted_iota(jnp.int32, own.shape, 1)
-    return first[:, 0:1] * second + jnp.where(row == 0, 0.0, first)
+def join_kernel(seg_ref, other_ref, block_ref, got_ref, out_ref, *, bit):
+    wanted = (0, 1) if len(out_ref.shape) == 3 else (1,)
+    for i in wanted:
+        own, got = block_ref[i], got_ref[1 - i]
+        own_trans, got_trans = own[0:1], got[0:1]
+        ahead = (other_ref if i else seg_ref)[4 + bit : 5 + bit] > 0
+        color = jnp.where(ahead, own + own_trans * got, got + got_trans * own)
+        row = lax.broadcasted_iota(jnp.int32, own.shape, 0)
+        result = jnp.where(row == 0, own_trans * got_trans, color)
+        if len(wanted) == 2:
+            out_ref[i] = result
+        else:
+            out_ref[...] = result
 
 
 def pairs(size, bit):
@@ -333,14 +342,22 @@
             ),
         )
 
-        both = jnp.stack([seg, lax.ppermute(seg, "tile", pairs(n_tile, 1))])
-        block = both[:, :4]
+        other = lax.ppermute(seg, "tile", pairs(n_tile, 1))
+        block = jnp.stack([seg[:4], other[:4]])
         pieces = []
         for bit in range(n_bits):
             got = lax.ppermute(block, ("slab", "tile"), pairs(n_slab * n_tile, (n_tile << bit) | 1))
             pieces.append(got)
             if bit + 1 < n_bits:
-                block = joined(block, got[::-1], both[:, 4 + bit : 5 + bit] > 0)
+                shape = (2, 4, rays) if bit + 2 < n_bits else (4, rays)
+                block = pl.pallas_call(
+                    functools.partial(join_kernel, bit=bit),
+                    name="join",
+                    out_shape=pltpu.VMEM(shape, F32),
+                    in_specs=[VMEM] * 4,
+                    out_specs=VMEM,
+                    compiler_params=LIMIT,
+                )(seg, other, block, got)
 
         x, h1, h2, save, w16, w2, target_rows = kept
         half_mid, half_in = hidden // 2, width // 2 + 8

time: 33.1 us -> 33.2 us (level)
  no operation moved by 1% of the time
where the time goes in v7:
time: 33.2 us; the launch traced here: 33 us
  waiting for transfers between devices  10.9 us (33%)
  Pallas kernels  10.7 us (32%)
  starting transfers between devices  10.7 us (32%)
  between operations  0.71 us (2%)
    ppermute x3, starting transfers between devices, body(): lax.ppermute(block, ('slab', 'tile'), pairs(n_slab * n_tile, n_tile << bi...  7.32 us
    pallas_call x1, Pallas kernels, body(): pl.pallas_call(functools.partial(forward_kernel, n_bits=n_bits), name='fo...  4.53 us
    ppermute x3, waiting for transfers between devices, body(): lax.ppermute(block, ('slab', 'tile'), pairs(n_slab * n_tile, n_tile << bi...  4.25 us
    ppermute x2, waiting for transfers between devices, tile_sum(): part = part + lax.ppermute(part, 'tile', pairs(n_tile, bit | 1))  3.84 us
    pallas_call x1, Pallas kernels, body(): pl.pallas_call(functools.partial(backward_kernel, n_bits=n_bits, n_tile=n...  3.7 us
    ppermute x2, starting transfers between devices, tile_sum(): part = part + lax.ppermute(part, 'tile', pairs(n_tile, bit | 1))  1.88 us
    pallas_call x1, Pallas kernels, body(): pl.pallas_call(functools.partial(first_kernel, n_tile=n_tile), name='firs...  1.36 us
    ppermute x2, waiting for transfers between devices, chip_sum(): return keep + lax.ppermute(send, 'tile', pairs(n_tile, 1))  1.1 us
  transfers between devices with their start and end apart: 10, of which 8 were waited for; matrix products, arithmetic and copies ran while one was open for 0% of the time, Pallas kernels for 5%

profile of v7, /device:TPU:0, one launch (start us, length us, event | category | flops | bytes accessed | tf_op | source)
XLA Modules:
  0.0 33.0 jit_solution(9236499564947490663)
XLA Ops:
  0.6 4.5 %forward.1 = (f32[8,512]{1,0:T(8,128)S(1)}, bf16[8192,128]{1,0:T(8,128)(2,1)S(1)}, bf16[8192,256]{1,0:T(8,128)(2,1)S(1)}, bf16[8192,256]{1,0:T(8,128)(2,1)S(1)},...) custom-call(bf16[8192,128]{1,0:T(8,128)(2,1)} %bitcast.23, ...), custom_call_target="tpu_custom_call" | custom-call | tf_op jit(solution)/shard_map/forward/pallas_call | solution.py:307
  5.2 0.5 %collective-permute-start = (f32[8,512]{1,0:T(8,128)S(1)}, f32[8,512]{1,0:T(8,128)S(1)}, u32[]{:S(2)}, u32[]{:S(2)}) collective-permute-start(f32[8,512]{1,0:T(8,128)S(1)} %get-tuple-element.25.seg_ref.own_ref), channel_id=1, source_target_pairs={{0,1},{1,0},{2,3},{3,2},{4,5},{5,4},{6,7},{7,6},{8,9},{9,8},{10,11... | collective-permute-start | bytes 49160 | tf_op jit(solution)/shard_map/ppermute | solution.py:345
  5.7 0.8 %collective-permute-done.other_ref = f32[8,512]{1,0:T(8,128)S(1)} collective-permute-done((f32[8,512]{1,0:T(8,128)S(1)}, f32[8,512]{1,0:T(8,128)S(1)}, u32[]{:S(2)}, u32[]{:S(2)}) %collective-permute-start) | collective-permute-done | bytes 16416 | tf_op jit(solution)/shard_map/ppermute | solution.py:345
  6.6 2.7 %collective-permute-start.1 = (f32[2,4,512]{2,1,0:T(4,128)S(1)}, f32[2,4,512]{2,1,0:T(4,128)S(1)}, u32[]{:S(2)}, u32[]{:S(2)}) collective-permute-start(f32[2,4,512]{2,1,0:T(4,128)S(1)} %pad_maximum_fusion.block_ref), channel_id=1, source_target_pairs={{0,5},{1,4},{2,7},{3,6},{4,1},{5,0},{6,3},{7,2},{8,13},{9,12},{10,... | collective-permute-start | bytes 49160 | tf_op jit(solution)/shard_map/ppermute | solution.py:349
  9.2 1.4 %collective-permute-done.1.got_ref.refs_0_ = f32[2,4,512]{2,1,0:T(4,128)S(1)} collective-permute-done((f32[2,4,512]{2,1,0:T(4,128)S(1)}, f32[2,4,512]{2,1,0:T(4,128)S(1)}, u32[]{:S(2)}, u32[]{:S(2)}) %collective-permute-start.1) | collective-permute-done | bytes 16416 | tf_op jit(solution)/shard_map/ppermute | solution.py:349
  10.7 1.9 %collective-permute-start.2 = (f32[2,4,512]{2,1,0:T(4,128)S(1)}, f32[2,4,512]{2,1,0:T(4,128)S(1)}, u32[]{:S(2)}, u32[]{:S(2)}) collective-permute-start(f32[2,4,512]{2,1,0:T(4,128)S(1)} %join.2.block_ref), channel_id=1, source_target_pairs={{0,9},{1,8},{2,11},{3,10},{4,13},{5,12},{6,15},{7,14},{8,1},{9,0},... | collective-permute-start | bytes 49160 | tf_op jit(solution)/shard_map/ppermute | solution.py:349
  12.5 1.4 %collective-permute-done.2.got_ref.refs_1_ = f32[2,4,512]{2,1,0:T(4,128)S(1)} collective-permute-done((f32[2,4,512]{2,1,0:T(4,128)S(1)}, f32[2,4,512]{2,1,0:T(4,128)S(1)}, u32[]{:S(2)}, u32[]{:S(2)}) %collective-permute-start.2) | collective-permute-done | bytes 16416 | tf_op jit(solution)/shard_map/ppermute | solution.py:349
  14.0 2.8 %collective-permute-start.3 = (f32[4,512]{1,0:T(4,128)S(1)}, f32[4,512]{1,0:T(4,128)S(1)}, u32[]{:S(2)}, u32[]{:S(2)}) collective-permute-start(f32[4,512]{1,0:T(4,128)S(1)} %join.3), channel_id=1, source_target_pairs={{0,17},{1,16},{2,19},{3,18},{4,21},{5,20},{6,23},{7,22},{8,25},{9,... | collective-permute-start | bytes 24584 | tf_op jit(solution)/shard_map/ppermute | solution.py:349
  16.8 1.4 %collective-permute-done.3.refs_2_ = f32[4,512]{1,0:T(4,128)S(1)} collective-permute-done((f32[4,512]{1,0:T(4,128)S(1)}, f32[4,512]{1,0:T(4,128)S(1)}, u32[]{:S(2)}, u32[]{:S(2)}) %collective-permute-start.3) | collective-permute-done | bytes 8224 | tf_op jit(solution)/shard_map/ppermute | solution.py:349
  18.2 3.7 %backward.1 = (f32[1,512]{1,0:T(1,128)}, f32[128,256]{1,0:T(8,128)S(1)}, f32[128,256]{1,0:T(8,128)S(1)}, bf16[8192,256]{1,0:T(8,128)(2,1)S(1)}, bf16[16,8192]{1,0:T(8,128)(2,1)S(1)}) custom-call(f32[8,512]{1,0:T(8,128)S(1)} %get-tuple-element.25.seg_ref.own_ref, bf16[8192,256]{1,0:T(8,128)(2,1)S(1)} %get-tuple-element.26.h1_ref, ...), custom_call_target="tpu_custom_call" | custom-call | flops 2147483648 | tf_op jit(solution)/shard_map/backward/pallas_call | solution.py:364
  21.9 0.4 %collective-permute-start.4 = (f32[128,256]{1,0:T(8,128)S(1)}, f32[128,256]{1,0:T(8,128)S(1)}, u32[]{:S(2)}, u32[]{:S(2)}) collective-permute-start(f32[128,256]{1,0:T(8,128)S(1)} %get-tuple-element.34), channel_id=1, source_target_pairs={{0,1},{1,0},{2,3},{3,2},{4,5},{5,4},{6,7},{7,6},{8,9},{9,8},{10,11... | collective-permute-start | bytes 393224 | tf_op jit(solution)/shard_map/ppermute | solution.py:386
  22.3 0.0 copy-start
  22.3 1.4 %first.1 = (f32[72,256]{1,0:T(8,128)S(1)}, f32[72,256]{1,0:T(8,128)S(1)}) custom-call(bf16[8192,128]{1,0:T(8,128)(2,1)S(1)} %get-tuple-element.35.x_ref, bf16[8192,256]{1,0:T(8,128)(2,1)S(1)} %get-tuple-element.36.one_ref, bf16[8192,256]{1,0:T(8,128)(2,1)S(1)} %get-tuple-element.27.h2_ref, bf16[16,8192]{1,0:T(8,128)(2,1)S(1)} %get-tuple-element.37.q16), custom_call_target="tpu_custom_call" | custom-call | flops 2147483648 | tf_op jit(solution)/shard_map/first/pallas_call | solution.py:396
  23.6 0.0 collective-permute-done.4
  23.7 1.6 %collective-permute-start.5 = (f32[128,256]{1,0:T(8,128)S(1)}, f32[128,256]{1,0:T(8,128)S(1)}, u32[]{:S(2)}, u32[]{:S(2)}) collective-permute-start(f32[128,256]{1,0:T(8,128)S(1)} %add.12), channel_id=1, source_target_pairs={{0,3},{1,2},{2,1},{3,0},{4,7},{5,6},{6,5},{7,4},{8,11},{9,10},{10,... | collective-permute-start | bytes 393224 | tf_op jit(solution)/shard_map/ppermute | solution.py:391
  25.3 0.2 collective-permute-start.7
  25.5 1.1 %collective-permute-done.7 = f32[72,256]{1,0:T(8,128)S(1)} collective-permute-done((f32[72,256]{1,0:T(8,128)S(1)}, f32[72,256]{1,0:T(8,128)S(1)}, u32[]{:S(2)}, u32[]{:S(2)}) %collective-permute-start.7) | collective-permute-done | bytes 73760 | tf_op jit(solution)/shard_map/ppermute | solution.py:386
  26.6 0.2 collective-permute-start.8
  26.8 2.4 %collective-permute-done.5 = f32[128,256]{1,0:T(8,128)S(1)} collective-permute-done((f32[128,256]{1,0:T(8,128)S(1)}, f32[128,256]{1,0:T(8,128)S(1)}, u32[]{:S(2)}, u32[]{:S(2)}) %collective-permute-start.5) | collective-permute-done | bytes 131104 | tf_op jit(solution)/shard_map/ppermute | solution.py:391
  29.3 0.2 collective-permute-start.6
  29.4 1.4 %collective-permute-done.8 = f32[72,256]{1,0:T(8,128)S(1)} collective-permute-done((f32[72,256]{1,0:T(8,128)S(1)}, f32[72,256]{1,0:T(8,128)S(1)}, u32[]{:S(2)}, u32[]{:S(2)}) %collective-permute-start.8) | collective-permute-done | bytes 73760 | tf_op jit(solution)/shard_map/ppermute | solution.py:391
  30.9 0.2 collective-permute-start.9
  31.1 0.0 copy-done
  31.1 0.3 expand.1.out_ref
  31.4 0.8 %collective-permute-done.9.other_in = f32[72,256]{1,0:T(8,128)S(1)} collective-permute-done((f32[72,256]{1,0:T(8,128)S(1)}, f32[72,256]{1,0:T(8,128)S(1)}, u32[]{:S(2)}, u32[]{:S(2)}) %collective-permute-start.9) | collective-permute-done | bytes 73760 | tf_op jit(solution)/shard_map/ppermute | solution.py:393
  32.2 0.0 collective-permute-done.6.other_mid
  32.2 0.8 %final.1 = (f32[128,256]{1,0:T(8,128)}, f32[256,256]{1,0:T(8,128)}, f32[64,256]{1,0:T(8,128)}) custom-call(f32[128,256]{1,0:T(8,128)S(1)} %add.13.own_mid, f32[128,256]{1,0:T(8,128)S(1)} %collective-permute-done.6.other_mid, f32[72,256]{1,0:T(8,128)S(1)} %add.15.factors_ref.own_in, f32[72,256]{1,0:T(8,128)S(1)} %collective-permute-done.9.other_in, ...), custom_call_target="tpu_custom_call" | custom-call | tf_op jit(solution)/shard_map/final/pallas_call | solution.py:419
  (9 shorter events, 0.1 us)
Async XLA Ops:
  5.2 1.4 %collective-permute-start = (f32[8,512]{1,0:T(8,128)S(1)}, f32[8,512]{1,0:T(8,128)S(1)}, u32[]{:S(2)}, u32[]{:S(2)}) collective-permute-start(f32[8,512]{1,0:T(8,128)S(1)} %get-tuple-element.25.seg_ref.own_ref), channel_id=1, source_target_pairs={{0,1},{1,0},{2,3},{3,2},{4,5},{5,4},{6,7},{7,6},{8,9},{9,8},{10,11... | collective-permute-start | bytes 49160 | tf_op jit(solution)/shard_map/ppermute | solution.py:345
  6.6 4.1 %collective-permute-start.1 = (f32[2,4,512]{2,1,0:T(4,128)S(1)}, f32[2,4,512]{2,1,0:T(4,128)S(1)}, u32[]{:S(2)}, u32[]{:S(2)}) collective-permute-start(f32[2,4,512]{2,1,0:T(4,128)S(1)} %pad_maximum_fusion.block_ref), channel_id=1, source_target_pairs={{0,5},{1,4},{2,7},{3,6},{4,1},{5,0},{6,3},{7,2},{8,13},{9,12},{10,... | collective-permute-start | bytes 49160 | tf_op jit(solution)/shard_map/ppermute | solution.py:349
  10.7 3.3 %collective-permute-start.2 = (f32[2,4,512]{2,1,0:T(4,128)S(1)}, f32[2,4,512]{2,1,0:T(4,128)S(1)}, u32[]{:S(2)}, u32[]{:S(2)}) collective-permute-start(f32[2,4,512]{2,1,0:T(4,128)S(1)} %join.2.block_ref), channel_id=1, source_target_pairs={{0,9},{1,8},{2,11},{3,10},{4,13},{5,12},{6,15},{7,14},{8,1},{9,0},... | collective-permute-start | bytes 49160 | tf_op jit(solution)/shard_map/ppermute | solution.py:349
  14.0 4.2 %collective-permute-start.3 = (f32[4,512]{1,0:T(4,128)S(1)}, f32[4,512]{1,0:T(4,128)S(1)}, u32[]{:S(2)}, u32[]{:S(2)}) collective-permute-start(f32[4,512]{1,0:T(4,128)S(1)} %join.3), channel_id=1, source_target_pairs={{0,17},{1,16},{2,19},{3,18},{4,21},{5,20},{6,23},{7,22},{8,25},{9,... | collective-permute-start | bytes 24584 | tf_op jit(solution)/shard_map/ppermute | solution.py:349
  21.9 1.7 %collective-permute-start.4 = (f32[128,256]{1,0:T(8,128)S(1)}, f32[128,256]{1,0:T(8,128)S(1)}, u32[]{:S(2)}, u32[]{:S(2)}) collective-permute-start(f32[128,256]{1,0:T(8,128)S(1)} %get-tuple-element.34), channel_id=1, source_target_pairs={{0,1},{1,0},{2,3},{3,2},{4,5},{5,4},{6,7},{7,6},{8,9},{9,8},{10,11... | collective-permute-start | bytes 393224 | tf_op jit(solution)/shard_map/ppermute | solution.py:386
  22.3 8.9 %copy-start = (f32[64,3]{0,1:T(4,128)S(1)}, f32[64,3]{0,1:T(4,128)}, u32[]{:S(2)}) copy-start(f32[64,3]{0,1:T(4,128)} %param.20) | copy-start | bytes 2308
  23.7 5.6 %collective-permute-start.5 = (f32[128,256]{1,0:T(8,128)S(1)}, f32[128,256]{1,0:T(8,128)S(1)}, u32[]{:S(2)}, u32[]{:S(2)}) collective-permute-start(f32[128,256]{1,0:T(8,128)S(1)} %add.12), channel_id=1, source_target_pairs={{0,3},{1,2},{2,1},{3,0},{4,7},{5,6},{6,5},{7,4},{8,11},{9,10},{10,... | collective-permute-start | bytes 393224 | tf_op jit(solution)/shard_map/ppermute | solution.py:391
  25.3 1.3 %collective-permute-start.7 = (f32[72,256]{1,0:T(8,128)S(1)}, f32[72,256]{1,0:T(8,128)S(1)}, u32[]{:S(2)}, u32[]{:S(2)}) collective-permute-start(f32[72,256]{1,0:T(8,128)S(1)} %get-tuple-element.42), channel_id=1, source_target_pairs={{0,1},{1,0},{2,3},{3,2},{4,5},{5,4},{6,7},{7,6},{8,9},{9,8},{10,11... | collective-permute-start | bytes 221192 | tf_op jit(solution)/shard_map/ppermute | solution.py:386
  26.6 4.3 %collective-permute-start.8 = (f32[72,256]{1,0:T(8,128)S(1)}, f32[72,256]{1,0:T(8,128)S(1)}, u32[]{:S(2)}, u32[]{:S(2)}) collective-permute-start(f32[72,256]{1,0:T(8,128)S(1)} %add.14), channel_id=1, source_target_pairs={{0,3},{1,2},{2,1},{3,0},{4,7},{5,6},{6,5},{7,4},{8,11},{9,10},{10,... | collective-permute-start | bytes 221192 | tf_op jit(solution)/shard_map/ppermute | solution.py:391
  29.3 3.0 %collective-permute-start.6 = (f32[128,256]{1,0:T(8,128)S(1)}, f32[128,256]{1,0:T(8,128)S(1)}, u32[]{:S(2)}, u32[]{:S(2)}) collective-permute-start(f32[128,256]{1,0:T(8,128)S(1)} %add.13.own_mid), channel_id=1, source_target_pairs={{0,1},{1,0},{2,3},{3,2},{4,5},{5,4},{6,7},{7,6},{8,9},{9,8},{10,11... | collective-permute-start | bytes 393224 | tf_op jit(solution)/shard_map/ppermute | solution.py:393
  30.9 1.3 %collective-permute-start.9 = (f32[72,256]{1,0:T(8,128)S(1)}, f32[72,256]{1,0:T(8,128)S(1)}, u32[]{:S(2)}, u32[]{:S(2)}) collective-permute-start(f32[72,256]{1,0:T(8,128)S(1)} %add.15.factors_ref.own_in), channel_id=1, source_target_pairs={{0,1},{1,0},{2,3},{3,2},{4,5},{5,4},{6,7},{7,6},{8,9},{9,8},{10,11... | collective-permute-start | bytes 221192 | tf_op jit(solution)/shard_map/ppermute | solution.py:393

commit v8 on v7

--- a/solution.py
+++ b/solution.py
@@ -96,7 +96,6 @@
         move.start()
     for move in moves[:4] + loads[:1]:
         move.wait()
-    w16_ref[...] = projection(head_ref[...], w3_ref[...])
 
     for c in range(samples + 2):
         if c == first_rows // rays:
@@ -108,6 +107,8 @@
         if 0 <= c - 1 < samples:
             rows = pl.ds((c - 1) * rays, rays)
             h2_ref[rows] = positive(dot_nn(h1_ref[rows], w2_ref[...]))
+        if c == 2:
+            w16_ref[...] = projection(head_ref[...], w3_ref[...])
         if 0 <= c - 2 < samples:
             out8[c - 2] = dot_nt(w16_ref[...], h2_ref[pl.ds((c - 2) * rays, rays)])[:8]
 
@@ -349,7 +350,7 @@
             got = lax.ppermute(block, ("slab", "tile"), pairs(n_slab * n_tile, (n_tile << bit) | 1))
             pieces.append(got)
             if bit + 1 < n_bits:
-                shape = (2, 4, rays) if bit + 2 < n_bits else (4, rays)
+                shape = (2, 4, rays)
                 block = pl.pallas_call(
                     functools.partial(join_kernel, bit=bit),
                     name="join",

time: 33.2 us -> 33.1 us (level)
  no operation moved by 1% of the time
where the time goes in v8:
time: 33.1 us; the launch traced here: 33 us
  waiting for transfers between devices  10.9 us (33%)
  starting transfers between devices  10.7 us (32%)
  Pallas kernels  10.5 us (32%)
  between operations  0.7 us (2%)
    ppermute x3, starting transfers between devices, body(): lax.ppermute(block, ('slab', 'tile'), pairs(n_slab * n_tile, n_tile << bi...  7.34 us
    pallas_call x1, Pallas kernels, body(): pl.pallas_call(functools.partial(forward_kernel, n_bits=n_bits), name='fo...  4.54 us
    ppermute x3, waiting for transfers between devices, body(): lax.ppermute(block, ('slab', 'tile'), pairs(n_slab * n_tile, n_tile << bi...  4.33 us
    ppermute x2, waiting for transfers between devices, tile_sum(): part = part + lax.ppermute(part, 'tile', pairs(n_tile, bit | 1))  3.84 us
    pallas_call x1, Pallas kernels, body(): pl.pallas_call(functools.partial(backward_kernel, n_bits=n_bits, n_tile=n...  3.64 us
    ppermute x2, starting transfers between devices, tile_sum(): part = part + lax.ppermute(part, 'tile', pairs(n_tile, bit | 1))  1.88 us
    pallas_call x1, Pallas kernels, body(): pl.pallas_call(functools.partial(first_kernel, n_tile=n_tile), name='firs...  1.26 us
    ppermute x2, waiting for transfers between devices, chip_sum(): return keep + lax.ppermute(send, 'tile', pairs(n_tile, 1))  1.1 us
  transfers between devices with their start and end apart: 10, of which 8 were waited for; matrix products, arithmetic and copies ran while one was open for 0% of the time, Pallas kernels for 5%

profile of v8, /device:TPU:0, one launch (start us, length us, event | category | flops | bytes accessed | tf_op | source)
XLA Modules:
  0.0 33.0 jit_solution(18207588961509368038)
XLA Ops:
  0.6 4.5 %forward.1 = (f32[8,512]{1,0:T(8,128)S(1)}, bf16[8192,128]{1,0:T(8,128)(2,1)S(1)}, bf16[8192,256]{1,0:T(8,128)(2,1)S(1)}, bf16[8192,256]{1,0:T(8,128)(2,1)S(1)},...) custom-call(bf16[8192,128]{1,0:T(8,128)(2,1)} %bitcast.23, ...), custom_call_target="tpu_custom_call" | custom-call | tf_op jit(solution)/shard_map/forward/pallas_call | solution.py:308
  5.2 0.5 %collective-permute-start = (f32[8,512]{1,0:T(8,128)S(1)}, f32[8,512]{1,0:T(8,128)S(1)}, u32[]{:S(2)}, u32[]{:S(2)}) collective-permute-start(f32[8,512]{1,0:T(8,128)S(1)} %get-tuple-element.25.seg_ref.own_ref), channel_id=1, source_target_pairs={{0,1},{1,0},{2,3},{3,2},{4,5},{5,4},{6,7},{7,6},{8,9},{9,8},{10,11... | collective-permute-start | bytes 49160 | tf_op jit(solution)/shard_map/ppermute | solution.py:346
  5.7 0.8 %collective-permute-done.other_ref = f32[8,512]{1,0:T(8,128)S(1)} collective-permute-done((f32[8,512]{1,0:T(8,128)S(1)}, f32[8,512]{1,0:T(8,128)S(1)}, u32[]{:S(2)}, u32[]{:S(2)}) %collective-permute-start) | collective-permute-done | bytes 16416 | tf_op jit(solution)/shard_map/ppermute | solution.py:346
  6.6 2.7 %collective-permute-start.1 = (f32[2,4,512]{2,1,0:T(4,128)S(1)}, f32[2,4,512]{2,1,0:T(4,128)S(1)}, u32[]{:S(2)}, u32[]{:S(2)}) collective-permute-start(f32[2,4,512]{2,1,0:T(4,128)S(1)} %pad_maximum_fusion.block_ref), channel_id=1, source_target_pairs={{0,5},{1,4},{2,7},{3,6},{4,1},{5,0},{6,3},{7,2},{8,13},{9,12},{10,... | collective-permute-start | bytes 49160 | tf_op jit(solution)/shard_map/ppermute | solution.py:350
  9.2 1.4 %collective-permute-done.1.got_ref.refs_0_ = f32[2,4,512]{2,1,0:T(4,128)S(1)} collective-permute-done((f32[2,4,512]{2,1,0:T(4,128)S(1)}, f32[2,4,512]{2,1,0:T(4,128)S(1)}, u32[]{:S(2)}, u32[]{:S(2)}) %collective-permute-start.1) | collective-permute-done | bytes 16416 | tf_op jit(solution)/shard_map/ppermute | solution.py:350
  10.7 1.9 %collective-permute-start.2 = (f32[2,4,512]{2,1,0:T(4,128)S(1)}, f32[2,4,512]{2,1,0:T(4,128)S(1)}, u32[]{:S(2)}, u32[]{:S(2)}) collective-permute-start(f32[2,4,512]{2,1,0:T(4,128)S(1)} %join.2.block_ref), channel_id=1, source_target_pairs={{0,9},{1,8},{2,11},{3,10},{4,13},{5,12},{6,15},{7,14},{8,1},{9,0},... | collective-permute-start | bytes 49160 | tf_op jit(solution)/shard_map/ppermute | solution.py:350
  12.6 1.4 %collective-permute-done.2.got_ref.refs_1_ = f32[2,4,512]{2,1,0:T(4,128)S(1)} collective-permute-done((f32[2,4,512]{2,1,0:T(4,128)S(1)}, f32[2,4,512]{2,1,0:T(4,128)S(1)}, u32[]{:S(2)}, u32[]{:S(2)}) %collective-permute-start.2) | collective-permute-done | bytes 16416 | tf_op jit(solution)/shard_map/ppermute | solution.py:350
  14.0 2.8 %collective-permute-start.3 = (f32[2,4,512]{2,1,0:T(4,128)S(1)}, f32[2,4,512]{2,1,0:T(4,128)S(1)}, u32[]{:S(2)}, u32[]{:S(2)}) collective-permute-start(f32[2,4,512]{2,1,0:T(4,128)S(1)} %join.3), channel_id=1, source_target_pairs={{0,17},{1,16},{2,19},{3,18},{4,21},{5,20},{6,23},{7,22},{8,25},{9,... | collective-permute-start | bytes 49160 | tf_op jit(solution)/shard_map/ppermute | solution.py:350
  16.8 1.4 %collective-permute-done.3.refs_2_ = f32[2,4,512]{2,1,0:T(4,128)S(1)} collective-permute-done((f32[2,4,512]{2,1,0:T(4,128)S(1)}, f32[2,4,512]{2,1,0:T(4,128)S(1)}, u32[]{:S(2)}, u32[]{:S(2)}) %collective-permute-start.3) | collective-permute-done | bytes 16416 | tf_op jit(solution)/shard_map/ppermute | solution.py:350
  18.3 3.6 %backward.1 = (f32[1,512]{1,0:T(1,128)}, f32[128,256]{1,0:T(8,128)S(1)}, f32[128,256]{1,0:T(8,128)S(1)}, bf16[8192,256]{1,0:T(8,128)(2,1)S(1)}, bf16[16,8192]{1,0:T(8,128)(2,1)S(1)}) custom-call(f32[8,512]{1,0:T(8,128)S(1)} %get-tuple-element.25.seg_ref.own_ref, bf16[8192,256]{1,0:T(8,128)(2,1)S(1)} %get-tuple-element.26.h1_ref, ...), custom_call_target="tpu_custom_call" | custom-call | flops 2147483648 | tf_op jit(solution)/shard_map/backward/pallas_call | solution.py:365
  21.9 0.4 %collective-permute-start.4 = (f32[128,256]{1,0:T(8,128)S(1)}, f32[128,256]{1,0:T(8,128)S(1)}, u32[]{:S(2)}, u32[]{:S(2)}) collective-permute-start(f32[128,256]{1,0:T(8,128)S(1)} %get-tuple-element.34), channel_id=1, source_target_pairs={{0,1},{1,0},{2,3},{3,2},{4,5},{5,4},{6,7},{7,6},{8,9},{9,8},{10,11... | collective-permute-start | bytes 393224 | tf_op jit(solution)/shard_map/ppermute | solution.py:387
  22.3 0.0 copy-start
  22.3 1.3 %first.1 = (f32[72,256]{1,0:T(8,128)S(1)}, f32[72,256]{1,0:T(8,128)S(1)}) custom-call(bf16[8192,128]{1,0:T(8,128)(2,1)S(1)} %get-tuple-element.35.x_ref, bf16[8192,256]{1,0:T(8,128)(2,1)S(1)} %get-tuple-element.36.one_ref, bf16[8192,256]{1,0:T(8,128)(2,1)S(1)} %get-tuple-element.27.h2_ref, bf16[16,8192]{1,0:T(8,128)(2,1)S(1)} %get-tuple-element.37.q16), custom_call_target="tpu_custom_call" | custom-call | flops 2147483648 | tf_op jit(solution)/shard_map/first/pallas_call | solution.py:397
  23.6 0.0 collective-permute-done.4
  23.6 1.6 %collective-permute-start.5 = (f32[128,256]{1,0:T(8,128)S(1)}, f32[128,256]{1,0:T(8,128)S(1)}, u32[]{:S(2)}, u32[]{:S(2)}) collective-permute-start(f32[128,256]{1,0:T(8,128)S(1)} %add.12), channel_id=1, source_target_pairs={{0,3},{1,2},{2,1},{3,0},{4,7},{5,6},{6,5},{7,4},{8,11},{9,10},{10,... | collective-permute-start | bytes 393224 | tf_op jit(solution)/shard_map/ppermute | solution.py:392
  25.2 0.2 collective-permute-start.7
  25.4 1.1 %collective-permute-done.7 = f32[72,256]{1,0:T(8,128)S(1)} collective-permute-done((f32[72,256]{1,0:T(8,128)S(1)}, f32[72,256]{1,0:T(8,128)S(1)}, u32[]{:S(2)}, u32[]{:S(2)}) %collective-permute-start.7) | collective-permute-done | bytes 73760 | tf_op jit(solution)/shard_map/ppermute | solution.py:387
  26.5 0.2 collective-permute-start.8
  26.8 2.4 %collective-permute-done.5 = f32[128,256]{1,0:T(8,128)S(1)} collective-permute-done((f32[128,256]{1,0:T(8,128)S(1)}, f32[128,256]{1,0:T(8,128)S(1)}, u32[]{:S(2)}, u32[]{:S(2)}) %collective-permute-start.5) | collective-permute-done | bytes 131104 | tf_op jit(solution)/shard_map/ppermute | solution.py:392
  29.2 0.2 collective-permute-start.6
  29.4 1.4 %collective-permute-done.8 = f32[72,256]{1,0:T(8,128)S(1)} collective-permute-done((f32[72,256]{1,0:T(8,128)S(1)}, f32[72,256]{1,0:T(8,128)S(1)}, u32[]{:S(2)}, u32[]{:S(2)}) %collective-permute-start.8) | collective-permute-done | bytes 73760 | tf_op jit(solution)/shard_map/ppermute | solution.py:392
  30.8 0.2 collective-permute-start.9
  31.1 0.0 copy-done
  31.1 0.3 expand.1.out_ref
  31.3 0.8 %collective-permute-done.9.other_in = f32[72,256]{1,0:T(8,128)S(1)} collective-permute-done((f32[72,256]{1,0:T(8,128)S(1)}, f32[72,256]{1,0:T(8,128)S(1)}, u32[]{:S(2)}, u32[]{:S(2)}) %collective-permute-start.9) | collective-permute-done | bytes 73760 | tf_op jit(solution)/shard_map/ppermute | solution.py:394
  32.2 0.0 collective-permute-done.6.other_mid
  32.2 0.8 %final.1 = (f32[128,256]{1,0:T(8,128)}, f32[256,256]{1,0:T(8,128)}, f32[64,256]{1,0:T(8,128)}) custom-call(f32[128,256]{1,0:T(8,128)S(1)} %add.13.own_mid, f32[128,256]{1,0:T(8,128)S(1)} %collective-permute-done.6.other_mid, f32[72,256]{1,0:T(8,128)S(1)} %add.15.factors_ref.own_in, f32[72,256]{1,0:T(8,128)S(1)} %collective-permute-done.9.other_in, ...), custom_call_target="tpu_custom_call" | custom-call | tf_op jit(solution)/shard_map/final/pallas_call | solution.py:420
  (9 shorter events, 0.1 us)
Async XLA Ops:
  5.2 1.4 %collective-permute-start = (f32[8,512]{1,0:T(8,128)S(1)}, f32[8,512]{1,0:T(8,128)S(1)}, u32[]{:S(2)}, u32[]{:S(2)}) collective-permute-start(f32[8,512]{1,0:T(8,128)S(1)} %get-tuple-element.25.seg_ref.own_ref), channel_id=1, source_target_pairs={{0,1},{1,0},{2,3},{3,2},{4,5},{5,4},{6,7},{7,6},{8,9},{9,8},{10,11... | collective-permute-start | bytes 49160 | tf_op jit(solution)/shard_map/ppermute | solution.py:346
  6.6 4.1 %collective-permute-start.1 = (f32[2,4,512]{2,1,0:T(4,128)S(1)}, f32[2,4,512]{2,1,0:T(4,128)S(1)}, u32[]{:S(2)}, u32[]{:S(2)}) collective-permute-start(f32[2,4,512]{2,1,0:T(4,128)S(1)} %pad_maximum_fusion.block_ref), channel_id=1, source_target_pairs={{0,5},{1,4},{2,7},{3,6},{4,1},{5,0},{6,3},{7,2},{8,13},{9,12},{10,... | collective-permute-start | bytes 49160 | tf_op jit(solution)/shard_map/ppermute | solution.py:350
  10.7 3.3 %collective-permute-start.2 = (f32[2,4,512]{2,1,0:T(4,128)S(1)}, f32[2,4,512]{2,1,0:T(4,128)S(1)}, u32[]{:S(2)}, u32[]{:S(2)}) collective-permute-start(f32[2,4,512]{2,1,0:T(4,128)S(1)} %join.2.block_ref), channel_id=1, source_target_pairs={{0,9},{1,8},{2,11},{3,10},{4,13},{5,12},{6,15},{7,14},{8,1},{9,0},... | collective-permute-start | bytes 49160 | tf_op jit(solution)/shard_map/ppermute | solution.py:350
  14.0 4.2 %collective-permute-start.3 = (f32[2,4,512]{2,1,0:T(4,128)S(1)}, f32[2,4,512]{2,1,0:T(4,128)S(1)}, u32[]{:S(2)}, u32[]{:S(2)}) collective-permute-start(f32[2,4,512]{2,1,0:T(4,128)S(1)} %join.3), channel_id=1, source_target_pairs={{0,17},{1,16},{2,19},{3,18},{4,21},{5,20},{6,23},{7,22},{8,25},{9,... | collective-permute-start | bytes 49160 | tf_op jit(solution)/shard_map/ppermute | solution.py:350
  21.9 1.7 %collective-permute-start.4 = (f32[128,256]{1,0:T(8,128)S(1)}, f32[128,256]{1,0:T(8,128)S(1)}, u32[]{:S(2)}, u32[]{:S(2)}) collective-permute-start(f32[128,256]{1,0:T(8,128)S(1)} %get-tuple-element.34), channel_id=1, source_target_pairs={{0,1},{1,0},{2,3},{3,2},{4,5},{5,4},{6,7},{7,6},{8,9},{9,8},{10,11... | collective-permute-start | bytes 393224 | tf_op jit(solution)/shard_map/ppermute | solution.py:387
  22.3 8.7 %copy-start = (f32[64,3]{0,1:T(4,128)S(1)}, f32[64,3]{0,1:T(4,128)}, u32[]{:S(2)}) copy-start(f32[64,3]{0,1:T(4,128)} %param.20) | copy-start | bytes 2308
  23.6 5.6 %collective-permute-start.5 = (f32[128,256]{1,0:T(8,128)S(1)}, f32[128,256]{1,0:T(8,128)S(1)}, u32[]{:S(2)}, u32[]{:S(2)}) collective-permute-start(f32[128,256]{1,0:T(8,128)S(1)} %add.12), channel_id=1, source_target_pairs={{0,3},{1,2},{2,1},{3,0},{4,7},{5,6},{6,5},{7,4},{8,11},{9,10},{10,... | collective-permute-start | bytes 393224 | tf_op jit(solution)/shard_map/ppermute | solution.py:392
  25.2 1.3 %collective-permute-start.7 = (f32[72,256]{1,0:T(8,128)S(1)}, f32[72,256]{1,0:T(8,128)S(1)}, u32[]{:S(2)}, u32[]{:S(2)}) collective-permute-start(f32[72,256]{1,0:T(8,128)S(1)} %get-tuple-element.42), channel_id=1, source_target_pairs={{0,1},{1,0},{2,3},{3,2},{4,5},{5,4},{6,7},{7,6},{8,9},{9,8},{10,11... | collective-permute-start | bytes 221192 | tf_op jit(solution)/shard_map/ppermute | solution.py:387
  26.5 4.3 %collective-permute-start.8 = (f32[72,256]{1,0:T(8,128)S(1)}, f32[72,256]{1,0:T(8,128)S(1)}, u32[]{:S(2)}, u32[]{:S(2)}) collective-permute-start(f32[72,256]{1,0:T(8,128)S(1)} %add.14), channel_id=1, source_target_pairs={{0,3},{1,2},{2,1},{3,0},{4,7},{5,6},{6,5},{7,4},{8,11},{9,10},{10,... | collective-permute-start | bytes 221192 | tf_op jit(solution)/shard_map/ppermute | solution.py:392
  29.2 2.9 %collective-permute-start.6 = (f32[128,256]{1,0:T(8,128)S(1)}, f32[128,256]{1,0:T(8,128)S(1)}, u32[]{:S(2)}, u32[]{:S(2)}) collective-permute-start(f32[128,256]{1,0:T(8,128)S(1)} %add.13.own_mid), channel_id=1, source_target_pairs={{0,1},{1,0},{2,3},{3,2},{4,5},{5,4},{6,7},{7,6},{8,9},{9,8},{10,11... | collective-permute-start | bytes 393224 | tf_op jit(solution)/shard_map/ppermute | solution.py:394
  30.8 1.3 %collective-permute-start.9 = (f32[72,256]{1,0:T(8,128)S(1)}, f32[72,256]{1,0:T(8,128)S(1)}, u32[]{:S(2)}, u32[]{:S(2)}) collective-permute-start(f32[72,256]{1,0:T(8,128)S(1)} %add.15.factors_ref.own_in), channel_id=1, source_target_pairs={{0,1},{1,0},{2,3},{3,2},{4,5},{5,4},{6,7},{7,6},{8,9},{9,8},{10,11... | collective-permute-start | bytes 221192 | tf_op jit(solution)/shard_map/ppermute | solution.py:394

commit v9 on v6

--- a/solution.py
+++ b/solution.py
@@ -222,12 +222,18 @@
 
     half = in_ref.shape[0] // 2
     for place, which in ((send_ref, 1 - kept), (keep_ref, kept)):
-        place[:half] = in_ref[pl.ds(pl.multiple_of(which * half, half), half)]
-        place[half:] = out_ref[:8] + out_ref[8:]
+        rows = pl.ds(pl.multiple_of(which * half, half), half)
+        lanes = place.shape[1]
+        place[:half] = in_ref[rows, :lanes]
+        place[half : 2 * half] = in_ref[rows, lanes:]
+        four = out_ref[:4] + out_ref[8:12]
+        place[2 * half :] = jnp.concatenate([four[:, :lanes], four[:, lanes:]], axis=0)
 
 
 def expand_kernel(factors_ref, head_ref, out_ref):
-    factors = factors_ref[factors_ref.shape[0] - 8 :]
+    packed = factors_ref[factors_ref.shape[0] - 8 :]
+    factors = jnp.concatenate([packed[:4], packed[4:]], axis=1)
+    factors = jnp.concatenate([factors, jnp.zeros_like(factors)], axis=0)
     head = head_ref[...]
     width = head.shape[1]
     first = jnp.where(lax.broadcasted_iota(jnp.int32, (1, width), 1) == 0, 1.0, 0.0)
@@ -241,17 +247,20 @@
     kept = kept_half(lax.axis_index("tile"), n_tile)
     half_mid = mid_hbm.shape[0] // 2
     half_in = in_hbm.shape[0] // 2
+    lanes = own_in.shape[1]
     moves = []
-    for source, place, size, half in (
-        (own_mid, mid_hbm, half_mid, kept),
-        (other_mid, mid_hbm, half_mid, 1 - kept),
-        (own_in, in_hbm, half_in, kept),
-        (other_in, in_hbm, half_in, 1 - kept),
+    for source, place, start, size, half, columns in (
+        (own_mid, mid_hbm, 0, half_mid, kept, pl.ds(0, 2 * lanes)),
+        (other_mid, mid_hbm, 0, half_mid, 1 - kept, pl.ds(0, 2 * lanes)),
+        (own_in, in_hbm, 0, half_in, kept, pl.ds(0, lanes)),
+        (own_in, in_hbm, half_in, half_in, kept, pl.ds(lanes, lanes)),
+        (other_in, in_hbm, 0, half_in, 1 - kept, pl.ds(0, lanes)),
+        (other_in, in_hbm, half_in, half_in, 1 - kept, pl.ds(lanes, lanes)),
     ):
         moves.append(
             pltpu.make_async_copy(
-                source.at[pl.ds(0, size)],
-                place.at[pl.ds(pl.multiple_of(half * size, size), size)],
+                source.at[pl.ds(start, size)],
+                place.at[pl.ds(pl.multiple_of(half * size, size), size), columns],
                 sems.at[len(moves)],
             )
         )
@@ -343,7 +352,7 @@
                 block = joined(block, got[::-1], both[:, 4 + bit : 5 + bit] > 0)
 
         x, h1, h2, save, w16, w2, target_rows = kept
-        half_mid, half_in = hidden // 2, width // 2 + 8
+        half_mid, half_in = hidden // 2, width + 8
         front, keep_mid, send_mid, back_one, factors = pl.pallas_call(
             functools.partial(backward_kernel, n_bits=n_bits, n_tile=n_tile),
             name="backward",
@@ -379,7 +388,7 @@
         keep_in, send_in = pl.pallas_call(
             functools.partial(first_kernel, n_tile=n_tile),
             name="first",
-            out_shape=(pltpu.VMEM((half_in, hidden), F32), pltpu.VMEM((half_in, hidden), F32)),
+            out_shape=(pltpu.VMEM((half_in, hidden // 2), F32), pltpu.VMEM((half_in, hidden // 2), F32)),
             in_specs=[VMEM] * 4,
             out_specs=(VMEM, VMEM),
             scratch_shapes=[pltpu.VMEM((width, hidden), F32), pltpu.VMEM((16, hidden), F32)],
@@ -409,7 +418,7 @@
             ),
             in_specs=[VMEM] * 5,
             out_specs=(HBM,) * 3,
-            scratch_shapes=[pltpu.SemaphoreType.DMA((5,))],
+            scratch_shapes=[pltpu.SemaphoreType.DMA((7,))],
             compiler_params=LIMIT,
         )(own_mid, other_mid, own_in, other_in, expanded)
         return front, grad_in[None], grad_mid[None], grad_out.T[None]

time: 33.1 us -> 33 us (level)
  no operation moved by 1% of the time
where the time goes in v9:
time: 33 us; the launch traced here: 32.9 us
  waiting for transfers between devices  10.8 us (33%)
  Pallas kernels  10.5 us (32%)
  starting transfers between devices  10.5 us (32%)
  between operations  0.75 us (2%)
    ppermute x3, starting transfers between devices, body(): lax.ppermute(block, ('slab', 'tile'), pairs(n_slab * n_tile, n_tile << bi...  7.16 us
    pallas_call x1, Pallas kernels, body(): pl.pallas_call(functools.partial(forward_kernel, n_bits=n_bits), name='fo...  4.53 us
    ppermute x3, waiting for transfers between devices, body(): lax.ppermute(block, ('slab', 'tile'), pairs(n_slab * n_tile, n_tile << bi...  4.29 us
    ppermute x2, waiting for transfers between devices, tile_sum(): part = part + lax.ppermute(part, 'tile', pairs(n_tile, bit | 1))  3.75 us
    pallas_call x1, Pallas kernels, body(): pl.pallas_call(functools.partial(backward_kernel, n_bits=n_bits, n_tile=n...  3.64 us
    ppermute x2, starting transfers between devices, tile_sum(): part = part + lax.ppermute(part, 'tile', pairs(n_tile, bit | 1))  1.88 us
    pallas_call x1, Pallas kernels, body(): pl.pallas_call(functools.partial(first_kernel, n_tile=n_tile), name='firs...  1.26 us
    ppermute x2, waiting for transfers between devices, chip_sum(): return keep + lax.ppermute(send, 'tile', pairs(n_tile, 1))  1.1 us
  transfers between devices with their start and end apart: 10, of which 8 were waited for; matrix products, arithmetic and copies ran while one was open for 0% of the time, Pallas kernels for 5%

profile of v9, /device:TPU:0, one launch (start us, length us, event | category | flops | bytes accessed | tf_op | source)
XLA Modules:
  0.0 32.9 jit_solution(8064798049207923408)
XLA Ops:
  0.6 4.5 %forward.1 = (f32[8,512]{1,0:T(8,128)S(1)}, bf16[8192,128]{1,0:T(8,128)(2,1)S(1)}, bf16[8192,256]{1,0:T(8,128)(2,1)S(1)}, bf16[8192,256]{1,0:T(8,128)(2,1)S(1)},...) custom-call(bf16[8192,128]{1,0:T(8,128)(2,1)} %bitcast.37, ...), custom_call_target="tpu_custom_call" | custom-call | tf_op jit(solution)/shard_map/forward/pallas_call | solution.py:307
  5.2 0.5 %collective-permute-start = (f32[8,512]{1,0:T(8,128)S(1)}, f32[8,512]{1,0:T(8,128)S(1)}, u32[]{:S(2)}, u32[]{:S(2)}) collective-permute-start(f32[8,512]{1,0:T(8,128)S(1)} %get-tuple-element.25.own_ref), channel_id=1, source_target_pairs={{0,1},{1,0},{2,3},{3,2},{4,5},{5,4},{6,7},{7,6},{8,9},{9,8},{10,11... | collective-permute-start | bytes 49160 | tf_op jit(solution)/shard_map/ppermute | solution.py:345
  5.7 0.8 %collective-permute-done = f32[8,512]{1,0:T(8,128)S(1)} collective-permute-done((f32[8,512]{1,0:T(8,128)S(1)}, f32[8,512]{1,0:T(8,128)S(1)}, u32[]{:S(2)}, u32[]{:S(2)}) %collective-permute-start) | collective-permute-done | bytes 16416 | tf_op jit(solution)/shard_map/ppermute | solution.py:345
  6.5 2.6 %collective-permute-start.1 = (f32[2,4,512]{2,1,0:T(4,128)S(1)}, f32[2,4,512]{2,1,0:T(4,128)S(1)}, u32[]{:S(2)}, u32[]{:S(2)}) collective-permute-start(f32[2,4,512]{2,1,0:T(4,128)S(1)} %fusion), channel_id=1, source_target_pairs={{0,5},{1,4},{2,7},{3,6},{4,1},{5,0},{6,3},{7,2},{8,13},{9,12},{10,... | collective-permute-start | bytes 49160 | tf_op jit(solution)/shard_map/ppermute | solution.py:349
  9.2 1.4 %collective-permute-done.1.refs_0_ = f32[2,4,512]{2,1,0:T(4,128)S(1)} collective-permute-done((f32[2,4,512]{2,1,0:T(4,128)S(1)}, f32[2,4,512]{2,1,0:T(4,128)S(1)}, u32[]{:S(2)}, u32[]{:S(2)}) %collective-permute-start.1) | collective-permute-done | bytes 16416 | tf_op jit(solution)/shard_map/ppermute | solution.py:349
  10.6 0.1 select_add_fusion.1
  10.7 1.8 %collective-permute-start.2 = (f32[2,4,512]{2,1,0:T(4,128)S(1)}, f32[2,4,512]{2,1,0:T(4,128)S(1)}, u32[]{:S(2)}, u32[]{:S(2)}) collective-permute-start(f32[2,4,512]{2,1,0:T(4,128)S(1)} %select_add_fusion.1), channel_id=1, source_target_pairs={{0,9},{1,8},{2,11},{3,10},{4,13},{5,12},{6,15},{7,14},{8,1},{9,0},... | collective-permute-start | bytes 49160 | tf_op jit(solution)/shard_map/ppermute | solution.py:349
  12.5 1.4 %collective-permute-done.2.refs_1_ = f32[2,4,512]{2,1,0:T(4,128)S(1)} collective-permute-done((f32[2,4,512]{2,1,0:T(4,128)S(1)}, f32[2,4,512]{2,1,0:T(4,128)S(1)}, u32[]{:S(2)}, u32[]{:S(2)}) %collective-permute-start.2) | collective-permute-done | bytes 16416 | tf_op jit(solution)/shard_map/ppermute | solution.py:349
  14.0 0.1 select_add_fusion
  14.1 2.8 %collective-permute-start.3 = (f32[2,4,512]{2,1,0:T(4,128)S(1)}, f32[2,4,512]{2,1,0:T(4,128)S(1)}, u32[]{:S(2)}, u32[]{:S(2)}) collective-permute-start(f32[2,4,512]{2,1,0:T(4,128)S(1)} %select_add_fusion), channel_id=1, source_target_pairs={{0,17},{1,16},{2,19},{3,18},{4,21},{5,20},{6,23},{7,22},{8,25},{9,... | collective-permute-start | bytes 49160 | tf_op jit(solution)/shard_map/ppermute | solution.py:349
  16.8 1.4 %collective-permute-done.3.refs_2_ = f32[2,4,512]{2,1,0:T(4,128)S(1)} collective-permute-done((f32[2,4,512]{2,1,0:T(4,128)S(1)}, f32[2,4,512]{2,1,0:T(4,128)S(1)}, u32[]{:S(2)}, u32[]{:S(2)}) %collective-permute-start.3) | collective-permute-done | bytes 16416 | tf_op jit(solution)/shard_map/ppermute | solution.py:349
  18.3 3.6 %backward.1 = (f32[1,512]{1,0:T(1,128)}, f32[128,256]{1,0:T(8,128)S(1)}, f32[128,256]{1,0:T(8,128)S(1)}, bf16[8192,256]{1,0:T(8,128)(2,1)S(1)}, bf16[16,8192]{1,0:T(8,128)(2,1)S(1)}) custom-call(f32[8,512]{1,0:T(8,128)S(1)} %get-tuple-element.25.own_ref, bf16[8192,256]{1,0:T(8,128)(2,1)S(1)} %get-tuple-element.26.h1_ref, ...), custom_call_target="tpu_custom_call" | custom-call | flops 2147483648 | tf_op jit(solution)/shard_map/backward/pallas_call | solution.py:356
  21.9 0.4 %collective-permute-start.4 = (f32[128,256]{1,0:T(8,128)S(1)}, f32[128,256]{1,0:T(8,128)S(1)}, u32[]{:S(2)}, u32[]{:S(2)}) collective-permute-start(f32[128,256]{1,0:T(8,128)S(1)} %get-tuple-element.34), channel_id=1, source_target_pairs={{0,1},{1,0},{2,3},{3,2},{4,5},{5,4},{6,7},{7,6},{8,9},{9,8},{10,11... | collective-permute-start | bytes 393224 | tf_op jit(solution)/shard_map/ppermute | solution.py:378
  22.3 0.0 copy-start
  22.3 1.3 %first.1 = (f32[136,128]{1,0:T(8,128)S(1)}, f32[136,128]{1,0:T(8,128)S(1)}) custom-call(bf16[8192,128]{1,0:T(8,128)(2,1)S(1)} %get-tuple-element.35.x_ref, bf16[8192,256]{1,0:T(8,128)(2,1)S(1)} %get-tuple-element.36.one_ref, bf16[8192,256]{1,0:T(8,128)(2,1)S(1)} %get-tuple-element.27.h2_ref, bf16[16,8192]{1,0:T(8,128)(2,1)S(1)} %get-tuple-element.37.q16), custom_call_target="tpu_custom_call" | custom-call | flops 2147483648 | tf_op jit(solution)/shard_map/first/pallas_call | solution.py:388
  23.6 0.0 collective-permute-done.4
  23.6 1.6 %collective-permute-start.5 = (f32[128,256]{1,0:T(8,128)S(1)}, f32[128,256]{1,0:T(8,128)S(1)}, u32[]{:S(2)}, u32[]{:S(2)}) collective-permute-start(f32[128,256]{1,0:T(8,128)S(1)} %add.20), channel_id=1, source_target_pairs={{0,3},{1,2},{2,1},{3,0},{4,7},{5,6},{6,5},{7,4},{8,11},{9,10},{10,... | collective-permute-start | bytes 393224 | tf_op jit(solution)/shard_map/ppermute | solution.py:383
  25.2 0.2 collective-permute-start.7
  25.4 1.1 %collective-permute-done.7 = f32[136,128]{1,0:T(8,128)S(1)} collective-permute-done((f32[136,128]{1,0:T(8,128)S(1)}, f32[136,128]{1,0:T(8,128)S(1)}, u32[]{:S(2)}, u32[]{:S(2)}) %collective-permute-start.7) | collective-permute-done | bytes 69664 | tf_op jit(solution)/shard_map/ppermute | solution.py:378
  26.5 0.2 collective-permute-start.8
  26.8 2.4 %collective-permute-done.5 = f32[128,256]{1,0:T(8,128)S(1)} collective-permute-done((f32[128,256]{1,0:T(8,128)S(1)}, f32[128,256]{1,0:T(8,128)S(1)}, u32[]{:S(2)}, u32[]{:S(2)}) %collective-permute-start.5) | collective-permute-done | bytes 131104 | tf_op jit(solution)/shard_map/ppermute | solution.py:383
  29.2 0.2 collective-permute-start.6
  29.4 1.3 %collective-permute-done.8 = f32[136,128]{1,0:T(8,128)S(1)} collective-permute-done((f32[136,128]{1,0:T(8,128)S(1)}, f32[136,128]{1,0:T(8,128)S(1)}, u32[]{:S(2)}, u32[]{:S(2)}) %collective-permute-start.8) | collective-permute-done | bytes 69664 | tf_op jit(solution)/shard_map/ppermute | solution.py:383
  30.7 0.2 collective-permute-start.9
  31.0 0.0 copy-done
  31.0 0.3 expand.1.out_ref
  31.2 0.8 %collective-permute-done.9.other_in = f32[136,128]{1,0:T(8,128)S(1)} collective-permute-done((f32[136,128]{1,0:T(8,128)S(1)}, f32[136,128]{1,0:T(8,128)S(1)}, u32[]{:S(2)}, u32[]{:S(2)}) %collective-permute-start.9) | collective-permute-done | bytes 69664 | tf_op jit(solution)/shard_map/ppermute | solution.py:385
  32.0 0.0 collective-permute-done.6.other_mid
  32.1 0.8 %final.1 = (f32[128,256]{1,0:T(8,128)}, f32[256,256]{1,0:T(8,128)}, f32[64,256]{1,0:T(8,128)}) custom-call(f32[128,256]{1,0:T(8,128)S(1)} %add.21.own_mid, f32[128,256]{1,0:T(8,128)S(1)} %collective-permute-done.6.other_mid, f32[136,128]{1,0:T(8,128)S(1)} %add.23.factors_ref.own_in, f32[136,128]{1,0:T(8,128)S(1)} %collective-permute-done.9.other_in, ...), custom_call_target="tpu_custom_call" | custom-call | tf_op jit(solution)/shard_map/final/pallas_call | solution.py:411
  (15 shorter events, 0.1 us)
Async XLA Ops:
  5.2 1.4 %collective-permute-start = (f32[8,512]{1,0:T(8,128)S(1)}, f32[8,512]{1,0:T(8,128)S(1)}, u32[]{:S(2)}, u32[]{:S(2)}) collective-permute-start(f32[8,512]{1,0:T(8,128)S(1)} %get-tuple-element.25.own_ref), channel_id=1, source_target_pairs={{0,1},{1,0},{2,3},{3,2},{4,5},{5,4},{6,7},{7,6},{8,9},{9,8},{10,11... | collective-permute-start | bytes 49160 | tf_op jit(solution)/shard_map/ppermute | solution.py:345
  6.5 4.0 %collective-permute-start.1 = (f32[2,4,512]{2,1,0:T(4,128)S(1)}, f32[2,4,512]{2,1,0:T(4,128)S(1)}, u32[]{:S(2)}, u32[]{:S(2)}) collective-permute-start(f32[2,4,512]{2,1,0:T(4,128)S(1)} %fusion), channel_id=1, source_target_pairs={{0,5},{1,4},{2,7},{3,6},{4,1},{5,0},{6,3},{7,2},{8,13},{9,12},{10,... | collective-permute-start | bytes 49160 | tf_op jit(solution)/shard_map/ppermute | solution.py:349
  10.7 3.3 %collective-permute-start.2 = (f32[2,4,512]{2,1,0:T(4,128)S(1)}, f32[2,4,512]{2,1,0:T(4,128)S(1)}, u32[]{:S(2)}, u32[]{:S(2)}) collective-permute-start(f32[2,4,512]{2,1,0:T(4,128)S(1)} %select_add_fusion.1), channel_id=1, source_target_pairs={{0,9},{1,8},{2,11},{3,10},{4,13},{5,12},{6,15},{7,14},{8,1},{9,0},... | collective-permute-start | bytes 49160 | tf_op jit(solution)/shard_map/ppermute | solution.py:349
  14.1 4.2 %collective-permute-start.3 = (f32[2,4,512]{2,1,0:T(4,128)S(1)}, f32[2,4,512]{2,1,0:T(4,128)S(1)}, u32[]{:S(2)}, u32[]{:S(2)}) collective-permute-start(f32[2,4,512]{2,1,0:T(4,128)S(1)} %select_add_fusion), channel_id=1, source_target_pairs={{0,17},{1,16},{2,19},{3,18},{4,21},{5,20},{6,23},{7,22},{8,25},{9,... | collective-permute-start | bytes 49160 | tf_op jit(solution)/shard_map/ppermute | solution.py:349
  21.9 1.7 %collective-permute-start.4 = (f32[128,256]{1,0:T(8,128)S(1)}, f32[128,256]{1,0:T(8,128)S(1)}, u32[]{:S(2)}, u32[]{:S(2)}) collective-permute-start(f32[128,256]{1,0:T(8,128)S(1)} %get-tuple-element.34), channel_id=1, source_target_pairs={{0,1},{1,0},{2,3},{3,2},{4,5},{5,4},{6,7},{7,6},{8,9},{9,8},{10,11... | collective-permute-start | bytes 393224 | tf_op jit(solution)/shard_map/ppermute | solution.py:378
  22.3 8.7 %copy-start = (f32[64,3]{0,1:T(4,128)S(1)}, f32[64,3]{0,1:T(4,128)}, u32[]{:S(2)}) copy-start(f32[64,3]{0,1:T(4,128)} %param.20) | copy-start | bytes 2308
  23.6 5.6 %collective-permute-start.5 = (f32[128,256]{1,0:T(8,128)S(1)}, f32[128,256]{1,0:T(8,128)S(1)}, u32[]{:S(2)}, u32[]{:S(2)}) collective-permute-start(f32[128,256]{1,0:T(8,128)S(1)} %add.20), channel_id=1, source_target_pairs={{0,3},{1,2},{2,1},{3,0},{4,7},{5,6},{6,5},{7,4},{8,11},{9,10},{10,... | collective-permute-start | bytes 393224 | tf_op jit(solution)/shard_map/ppermute | solution.py:383
  25.2 1.3 %collective-permute-start.7 = (f32[136,128]{1,0:T(8,128)S(1)}, f32[136,128]{1,0:T(8,128)S(1)}, u32[]{:S(2)}, u32[]{:S(2)}) collective-permute-start(f32[136,128]{1,0:T(8,128)S(1)} %get-tuple-element.42), channel_id=1, source_target_pairs={{0,1},{1,0},{2,3},{3,2},{4,5},{5,4},{6,7},{7,6},{8,9},{9,8},{10,11... | collective-permute-start | bytes 208904 | tf_op jit(solution)/shard_map/ppermute | solution.py:378
  26.5 4.2 %collective-permute-start.8 = (f32[136,128]{1,0:T(8,128)S(1)}, f32[136,128]{1,0:T(8,128)S(1)}, u32[]{:S(2)}, u32[]{:S(2)}) collective-permute-start(f32[136,128]{1,0:T(8,128)S(1)} %add.22), channel_id=1, source_target_pairs={{0,3},{1,2},{2,1},{3,0},{4,7},{5,6},{6,5},{7,4},{8,11},{9,10},{10,... | collective-permute-start | bytes 208904 | tf_op jit(solution)/shard_map/ppermute | solution.py:383
  29.2 2.8 %collective-permute-start.6 = (f32[128,256]{1,0:T(8,128)S(1)}, f32[128,256]{1,0:T(8,128)S(1)}, u32[]{:S(2)}, u32[]{:S(2)}) collective-permute-start(f32[128,256]{1,0:T(8,128)S(1)} %add.21.own_mid), channel_id=1, source_target_pairs={{0,1},{1,0},{2,3},{3,2},{4,5},{5,4},{6,7},{7,6},{8,9},{9,8},{10,11... | collective-permute-start | bytes 393224 | tf_op jit(solution)/shard_map/ppermute | solution.py:385
  30.7 1.3 %collective-permute-start.9 = (f32[136,128]{1,0:T(8,128)S(1)}, f32[136,128]{1,0:T(8,128)S(1)}, u32[]{:S(2)}, u32[]{:S(2)}) collective-permute-start(f32[136,128]{1,0:T(8,128)S(1)} %add.23.factors_ref.own_in), channel_id=1, source_target_pairs={{0,1},{1,0},{2,3},{3,2},{4,5},{5,4},{6,7},{7,6},{8,9},{9,8},{10,11... | collective-permute-start | bytes 208904 | tf_op jit(solution)/shard_map/ppermute | solution.py:385
